TPU v7x, 128 devices: a whole 4x4x4 slice. The times are simulated.
128 devices in a mesh: pipe: 8 (over x, y_lo), dp: 16 (over y_hi, z, core).
Axes of the slice: x: 4, y: 4 (y_hi: 2, y_lo: 2; y = y_hi * 2 + y_lo), z: 4, core: 2. Of those that a mesh axis runs over, the one named last changes fastest.
Arguments:
- section_output: bfloat16 [2048, 4608], P('dp', 'pipe'), may hold values from -0.29882812 to 0.29882812
- norm_gain: bfloat16 [4608], P('pipe'), may hold values from 0.5 to 1.5
- head_weight: bfloat16 [65536, 4608], P(('pipe', 'dp')), may hold values from -0.25 to 0.25
- targets: int32 [2048], replicated, may hold values from 0 to 65535
Outputs:
- token_loss: float32 [2048], P('dp')
- grad_input: bfloat16 [2048, 4608], P('dp', 'pipe')
- head_grad: bfloat16 [65536, 4608], P(('pipe', 'dp'))
- gain_grad: float32 [4608], P('pipe')
All inputs are finite; a program needn't handle non-finite values.
Results may differ from a plain program's by a relative error of at most 0.017.
Values may be sent and summed in bfloat16 or wider, within the bound.
No kernel may reach another device: no remote copies, remote signals or barrier semaphores. Data moves between devices by JAX's collectives and lax.ppermute only.
A program may use at most 128 MiB of HBM per device.

v0:
```python
import functools

import jax
import jax.numpy as jnp
import numpy as np
from jax import lax
from jax.experimental import pallas as pl
from jax.experimental.pallas import tpu as pltpu
from jax.sharding import Mesh, PartitionSpec as P

AX = ("x", "ylo", "yhi", "z", "core")
D = 4608
FB = 576
PT = 192
SQ = 16
TB = 128
VB = 512
CAP = 30.0
EPS = 1e-06
VMEM = 60 * 1024 * 1024
BF = jnp.bfloat16
F32 = jnp.float32

ORDER = ((0, 1, 2), (1, 2, 0), (2, 0, 1))


def coords(i):
    core, z, yhi, ylo, x = i % 2, i // 2 % 4, i // 8 % 2, i // 16 % 2, i // 32
    return [x, yhi * 2 + ylo, z], core


def number(c, core):
    return (((c[0] * 2 + c[1] % 2) * 2 + c[1] // 2) * 4 + c[2]) * 2 + core


@functools.cache
def across(dim, step):
    pairs = []
    for i in range(128):
        c, core = coords(i)
        bit = step if core == 0 else 1 - step
        gray = (c[dim] ^ (c[dim] >> 1)) ^ (1 << bit)
        c[dim] = gray ^ (gray >> 1)
        pairs.append((i, number(c, core)))
    return pairs


TWIN = [(i, i ^ 1) for i in range(128)]


def send(a, pairs):
    return lax.ppermute(a, AX, pairs)


def gather(blocks):
    held = [b[None] for b in blocks]
    for phase in range(3):
        for step in range(2):
            got = [send(held[p], across(ORDER[p][phase], step)) for p in range(3)]
            if phase == 2 and step == 1:
                return [a for p in range(3) for a in (held[p], got[p])]
            held = [jnp.concatenate([held[p], got[p]]) for p in range(3)]


def reduce_scatter(away, kept):
    for phase in (2, 1, 0):
        for step in (1, 0):
            got = [send(away[p], across(ORDER[p][phase], step)) for p in range(3)]
            if phase == 0 and step == 0:
                return [kept[p][0].astype(F32) + got[p][0].astype(F32) for p in range(3)]
            half = kept[0].shape[0] // 2
            away = [add(kept[p][half:], got[p][half:]) for p in range(3)]
            kept = [add(kept[p][:half], got[p][:half]) for p in range(3)]


def split3(v):
    hi = lax.reduce_precision(v, 8, 7)
    mid = lax.reduce_precision(v - hi, 8, 7)
    lo = v - hi - mid
    return [hi.astype(BF), mid.astype(BF), lo.astype(BF)]


def add(a, b):
    return (a.astype(F32) + b.astype(F32)).astype(a.dtype)


def table(x, y, z, core, shard):
    out = []
    place = jnp.arange(4, dtype=jnp.int32)
    turned = jnp.where(core == 0, place, (place & 1) * 2 + (place >> 1))
    for c in (x, y, z):
        gray = (c ^ (c >> 1)) ^ turned
        out.append(gray ^ (gray >> 1))
    for c in (x, y, z):
        gray = (place ^ (place >> 1)) ^ (c ^ (c >> 1))
        out.append(jnp.where(core == 0, gray, (gray & 1) * 2 + (gray >> 1)))
    out.append(jnp.stack([shard * VB, (shard ^ 1) * VB]))
    return jnp.concatenate(out).astype(jnp.int32)


def at_of(tab, dim, place):
    return tab[4 * dim + place]


def place_of(tab, dim, at):
    return tab[12 + 4 * dim + at]


def flip_kernel(own_ref, other_ref, a_ref, b_ref, c_ref):
    for h, ref in enumerate((own_ref, other_ref)):
        turned = ref[...].T
        cols = pl.ds(h * VB, VB)
        for ylo in range(2):
            at = ylo * FB
            a_ref[0, ylo, :, cols] = turned[at : at + PT]
            b_ref[0, ylo, :, cols] = turned[at + PT : at + 2 * PT]
            c_ref[ylo, 0, :, cols] = turned[at + 2 * PT : at + 3 * PT]


def flip(own, other):
    block = pl.BlockSpec((VB, 2 * FB), lambda x: (0, x))
    return pl.pallas_call(
        flip_kernel,
        grid=(4,),
        in_specs=[block, block],
        out_specs=[
            pl.BlockSpec((1, 2, PT, 2 * VB), lambda x: (x, 0, 0, 0)),
            pl.BlockSpec((1, 2, PT, 2 * VB), lambda x: (x, 0, 0, 0)),
            pl.BlockSpec((2, 1, PT, 2 * VB), lambda x: (0, x, 0, 0)),
        ],
        out_shape=[
            jax.ShapeDtypeStruct((4, 2, PT, 2 * VB), BF),
            jax.ShapeDtypeStruct((4, 2, PT, 2 * VB), BF),
            jax.ShapeDtypeStruct((2, 4, PT, 2 * VB), BF),
        ],
        compiler_params=pltpu.CompilerParams(vmem_limit_bytes=VMEM),
        cost_estimate=pl.CostEstimate(
            flops=0, bytes_accessed=4 * VB * D * 2, transcendentals=0
        ),
        name="flip",
    )(own, other)


def act_kernel(tab, *refs):
    halves = [refs[2 * p : 2 * p + 2] for p in range(3)]
    own_ref, other_ref = refs[6:8]
    act_ref, total_ref, rinv_ref, xt_out = refs[8:12]
    xt, squares, weights, acc, sems, out_sems, w_sems = refs[12:]
    step = pl.program_id(0)

    def fetch(src, tile, x, y, part):
        row = (x * 2 + (y & 1)) * FB + part * PT
        lanes = pl.ds(pl.multiple_of((y >> 1) * TB, TB), TB)
        pltpu.make_async_copy(
            src.at[pl.ds(0, PT)],
            xt.at[tile, pl.ds(pl.multiple_of(row, 16), PT), lanes],
            sems.at[tile],
        ).start()
        if part == 0:
            row = (x * 2 + (y & 1)) * SQ
            pltpu.make_async_copy(
                src.at[pl.ds(PT, SQ)],
                squares.at[tile, pl.ds(pl.multiple_of(row, 16), SQ), lanes],
                sems.at[tile],
            ).start()

    def issue(tile, carry):
        for half in range(2):
            @pl.when((tile >> 1) == half)
            def _():
                for ky in range(4):
                    for kx in range(4):
                        src = halves[0][half].at[((tile & 1) * 4 + ky) * 4 + kx]
                        fetch(src, tile, at_of(tab, 0, kx), at_of(tab, 1, ky), 0)
        for half in range(2):
            for low in range(2):
                for k in range(4):
                    src = halves[1][half].at[(low * 4 + tile) * 4 + k]
                    fetch(src, tile, at_of(tab, 0, half * 2 + low), at_of(tab, 1, k), 1)
                    src = halves[2][half].at[(low * 4 + k) * 4 + tile]
                    fetch(src, tile, at_of(tab, 0, k), at_of(tab, 1, half * 2 + low), 2)
        return carry

    def load(h, ref):
        return pltpu.make_async_copy(ref, weights.at[pl.ds(h * VB, VB)], w_sems.at[h])

    @pl.when(step == 0)
    def _():
        issue(step, 0)
        for h, ref in enumerate((own_ref, other_ref)):
            load(h, ref).start()

    @pl.when(step < 3)
    def _():
        issue(step + 1, 0)

    @pl.when(step == 0)
    def _():
        for h, ref in enumerate((own_ref, other_ref)):
            load(h, ref).wait()

    pltpu.make_async_copy(xt.at[step], xt.at[step], sems.at[step]).wait()
    pltpu.make_async_copy(squares.at[step], squares.at[step], sems.at[step]).wait()
    pltpu.make_async_copy(xt.at[step], xt_out.at[step], out_sems.at[step]).start()
    acc[...] = jnp.dot(weights[...], xt[step], preferred_element_type=F32)
    mean = jnp.sum(squares[step].astype(F32), axis=0, keepdims=True) / D
    rinv = lax.rsqrt(mean + EPS)
    z = at_of(tab, 2, step)
    rinv_ref[z] = rinv
    rows = 64

    def chunk(i, total):
        here = pl.ds(pl.multiple_of(i * rows, rows), rows)
        act = acc[here, :] * rinv
        act_ref[0, here, :] = act
        return total + jnp.exp(jnp.tanh(act * (1.0 / CAP)) * CAP)

    total = lax.fori_loop(0, 2 * VB // rows, chunk, jnp.zeros((rows, 2 * TB), F32))
    total = jnp.sum(total, axis=0, keepdims=True)
    for yhi in range(2):
        total_ref[pl.ds(z * 2 + yhi, 1), :] = total[:, yhi * TB : (yhi + 1) * TB]

    @pl.when(step == 3)
    def _():
        for tile in range(4):
            pltpu.make_async_copy(xt.at[tile], xt_out.at[tile], out_sems.at[tile]).wait()


ANYWHERE = pl.BlockSpec(memory_space=pl.ANY)
SMEM_SPEC = pl.BlockSpec(memory_space=pltpu.SMEM)
VMEM_SPEC = pl.BlockSpec(memory_space=pltpu.VMEM)


def act_call(tab, halves, own, other):
    return pl.pallas_call(
        act_kernel,
        grid_spec=pltpu.PrefetchScalarGridSpec(
            num_scalar_prefetch=1,
            grid=(4,),
            in_specs=[ANYWHERE] * 8,
            out_specs=[
                pl.BlockSpec((1, 2 * VB, 2 * TB), lambda z, w: (z, 0, 0)),
                pl.BlockSpec((8, TB), lambda z, w: (0, 0)),
                pl.BlockSpec((4, 1, 2 * TB), lambda z, w: (0, 0, 0)),
                ANYWHERE,
            ],
            scratch_shapes=[
                pltpu.VMEM((4, D, 2 * TB), BF),
                pltpu.VMEM((4, 8 * SQ, 2 * TB), BF),
                pltpu.VMEM((2 * VB, D), BF),
                pltpu.VMEM((2 * VB, 2 * TB), F32),
                pltpu.SemaphoreType.DMA((4,)),
                pltpu.SemaphoreType.DMA((4,)),
                pltpu.SemaphoreType.DMA((2,)),
            ],
        ),
        out_shape=[
            jax.ShapeDtypeStruct((4, 2 * VB, 2 * TB), F32),
            jax.ShapeDtypeStruct((8, TB), F32),
            jax.ShapeDtypeStruct((4, 1, 2 * TB), F32),
            jax.ShapeDtypeStruct((4, D, 2 * TB), BF),
        ],
        compiler_params=pltpu.CompilerParams(vmem_limit_bytes=VMEM),
        cost_estimate=pl.CostEstimate(
            flops=2 * 1024 * 1024 * D, bytes_accessed=30_000_000, transcendentals=2 << 20
        ),
        name="act",
    )(tab, *halves, own, other)


def prep_kernel(tab, act_ref, tgt_ref, expo_ref, stat_ref, bend_ref):
    step = pl.program_id(0)
    z = at_of(tab, 2, step)
    tgt = tgt_ref[z]
    rows = 32
    zeros = jnp.zeros((rows, 2 * TB), F32)
    sums = (zeros, zeros, zeros, zeros)
    for h in range(2):
        row0 = lax.broadcasted_iota(jnp.int32, (rows, 2 * TB), 0) + tab[24 + h]

        def chunk(i, sums, h=h, row0=row0):
            picked, slope, slope_at, bend = sums
            at = pl.multiple_of(i * rows, rows)
            here = pl.ds(h * VB + at, rows)
            act = act_ref[0, here, :]
            t = jnp.tanh(act * (1.0 / CAP))
            capped = t * CAP
            bent = 1.0 - t * t
            expo = jnp.exp(capped) * bent
            expo_ref[0, here, :] = expo
            hit = row0 + at == tgt
            return (
                picked + jnp.where(hit, capped, 0.0),
                slope + expo * act,
                slope_at + jnp.where(hit, bent * act, 0.0),
                bend + jnp.where(hit, bent, 0.0),
            )

        sums = lax.fori_loop(0, VB // rows, chunk, sums)
    sums = [jnp.sum(s, axis=0, keepdims=True) for s in sums]
    for i in range(3):
        for yhi in range(2):
            stat_ref[i, pl.ds(z * 2 + yhi, 1), :] = sums[i][:, yhi * TB : (yhi + 1) * TB]
    bend_ref[0] = sums[3]


def prep_call(tab, act, tgt):
    tile = pl.BlockSpec((1, 2 * VB, 2 * TB), lambda z, w: (z, 0, 0))
    return pl.pallas_call(
        prep_kernel,
        grid_spec=pltpu.PrefetchScalarGridSpec(
            num_scalar_prefetch=1,
            grid=(4,),
            in_specs=[tile, pl.BlockSpec((4, 1, 2 * TB), lambda z, w: (0, 0, 0))],
            out_specs=[
                tile,
                pl.BlockSpec((3, 8, TB), lambda z, w: (0, 0, 0)),
                pl.BlockSpec((1, 1, 2 * TB), lambda z, w: (z, 0, 0)),
            ],
        ),
        out_shape=[
            jax.ShapeDtypeStruct((4, 2 * VB, 2 * TB), F32),
            jax.ShapeDtypeStruct((3, 8, TB), F32),
            jax.ShapeDtypeStruct((4, 1, 2 * TB), F32),
        ],
        compiler_params=pltpu.CompilerParams(vmem_limit_bytes=VMEM),
        cost_estimate=pl.CostEstimate(
            flops=16 << 20, bytes_accessed=8 << 20, transcendentals=2 << 20
        ),
        name="prep",
    )(tab, act, tgt)


def pieces(tab, lead, gz, gy, w0, w1, w2, outs):
    out0, out1, out2 = outs
    for low in range(2):
        place = lead * 2 + low
        got = jnp.dot(
            w0[...].reshape(8 * PT, 2 * VB), gz[place], preferred_element_type=F32
        ).astype(BF)
        for x in range(4):
            for ylo in range(2):
                for yhi in range(2):
                    at = (low * 4 + place_of(tab, 1, yhi * 2 + ylo)) * 4 + place_of(tab, 0, x)
                    row = (x * 2 + ylo) * PT
                    out0[at] = got[row : row + PT, yhi * TB : (yhi + 1) * TB]
    for low in range(2):
        x = at_of(tab, 0, lead * 2 + low)
        w = w1[x].reshape(2 * PT, 2 * VB)
        for z in range(4):
            got = jnp.dot(w, gz[z], preferred_element_type=F32).astype(BF)
            for ylo in range(2):
                for yhi in range(2):
                    at = (low * 4 + z) * 4 + place_of(tab, 1, yhi * 2 + ylo)
                    out1[at] = got[ylo * PT : (ylo + 1) * PT, yhi * TB : (yhi + 1) * TB]
    for low in range(2):
        y = at_of(tab, 1, lead * 2 + low)
        w = w2[y & 1].reshape(4 * PT, 2 * VB)
        for pair in range(2):
            got = jnp.dot(w, gy[y >> 1, pair], preferred_element_type=F32).astype(BF)
            for x in range(4):
                for z in range(2):
                    at = (low * 4 + place_of(tab, 0, x)) * 4 + 2 * pair + z
                    out2[at] = got[x * PT : (x + 1) * PT, z * TB : (z + 1) * TB]


def grad_kernel(tab, expo_ref, bend_ref, totals_ref, rinv_ref, tgt_ref, w0, w1, w2, *outs):
    gz, gr, gy = outs[:3]
    rows = 32
    inv = 1.0 / jnp.sum(totals_ref[...], axis=0)
    line = lax.broadcasted_iota(jnp.int32, (8, TB), 0)

    def chunk(i, carry, place, h, inv_z, rinv, bend, tgt, row0):
        at = pl.multiple_of(i * rows, rows)
        here = pl.ds(h * VB + at, rows)
        g = expo_ref[place, here, :] * inv_z - jnp.where(row0 + at == tgt, bend, 0.0)
        gr[place, here, :] = (g * rinv).astype(BF)
        g = g.astype(BF)
        gz[place, here, :] = g
        for yhi in range(2):
            gy[yhi, place // 2, here, pl.ds(place % 2 * TB, TB)] = g[:, yhi * TB : (yhi + 1) * TB]
        return carry

    for place in range(4):
        z = at_of(tab, 2, place)
        inv_z = jnp.concatenate(
            [
                jnp.sum(jnp.where(line == z * 2 + yhi, inv, 0.0), axis=0, keepdims=True)
                for yhi in range(2)
            ],
            axis=1,
        )
        for h in range(2):
            row0 = lax.broadcasted_iota(jnp.int32, (rows, 2 * TB), 0) + tab[24 + h]
            lax.fori_loop(
                0,
                VB // rows,
                functools.partial(
                    chunk, place=place, h=h, inv_z=inv_z, rinv=rinv_ref[z],
                    bend=bend_ref[place], tgt=tgt_ref[z], row0=row0,
                ),
                0,
            )
    pieces(tab, 1, gz, gy, w0, w1, w2, outs[3:])


def keep_kernel(tab, gz, gy, w0, w1, w2, *outs):
    pieces(tab, 0, gz, gy, w0, w1, w2, outs)


HALF = jax.ShapeDtypeStruct((32, PT, TB), BF)


def grad_call(tab, expo, bend, totals, rinv, tgt, turned):
    shapes = [
        jax.ShapeDtypeStruct((4, 2 * VB, 2 * TB), BF),
        jax.ShapeDtypeStruct((4, 2 * VB, 2 * TB), BF),
        jax.ShapeDtypeStruct((2, 2, 2 * VB, 2 * TB), BF),
    ] + [HALF] * 3
    return pl.pallas_call(
        grad_kernel,
        in_specs=[SMEM_SPEC] + [VMEM_SPEC] * 8,
        out_specs=[VMEM_SPEC] * 6,
        out_shape=shapes,
        compiler_params=pltpu.CompilerParams(vmem_limit_bytes=VMEM),
        cost_estimate=pl.CostEstimate(
            flops=1024 * 1024 * D, bytes_accessed=24_000_000, transcendentals=0
        ),
        name="grad",
    )(tab, expo, bend, totals, rinv, tgt, *turned)


def keep_call(tab, gz, gy, turned):
    return pl.pallas_call(
        keep_kernel,
        in_specs=[SMEM_SPEC] + [VMEM_SPEC] * 5,
        out_specs=[VMEM_SPEC] * 3,
        out_shape=[HALF] * 3,
        compiler_params=pltpu.CompilerParams(vmem_limit_bytes=VMEM),
        cost_estimate=pl.CostEstimate(
            flops=1024 * 1024 * D, bytes_accessed=18_000_000, transcendentals=0
        ),
        name="keep",
    )(tab, gz, gy, *turned)


def head_kernel(gr, xt, own_w, other_w, own_ref, other_ref, gain_ref):
    gain = None
    for h, (w, ref) in enumerate(((own_w, own_ref), (other_w, other_ref))):
        total = None
        for z in range(4):
            part = lax.dot_general(
                gr[z, h * VB : (h + 1) * VB, :], xt[z],
                (((1,), (1,)), ((), ())), preferred_element_type=F32,
            )
            total = part if total is None else total + part
        ref[...] = total.astype(BF)
        here = jnp.sum(total * w[...].astype(F32), axis=0, keepdims=True)
        gain = here if gain is None else gain + here
    gain_ref[...] = gain


def head_call(gr, xt, own, other, half):
    tile = 768
    tiles = D // 2 // tile
    cols = pl.BlockSpec((VB, tile), lambda f: (0, f + half * tiles))
    return pl.pallas_call(
        head_kernel,
        grid=(tiles,),
        in_specs=[
            pl.BlockSpec((4, 2 * VB, 2 * TB), lambda f: (0, 0, 0), pipeline_mode=pl.Buffered(1)),
            pl.BlockSpec((4, tile, 2 * TB), lambda f: (0, f + half * tiles, 0)),
            cols,
            cols,
        ],
        out_specs=[pl.BlockSpec((VB, tile), lambda f: (0, f))] * 2
        + [pl.BlockSpec((1, tile), lambda f: (0, f))],
        out_shape=[jax.ShapeDtypeStruct((VB, D // 2), BF)] * 2
        + [jax.ShapeDtypeStruct((1, D // 2), F32)],
        compiler_params=pltpu.CompilerParams(vmem_limit_bytes=VMEM),
        cost_estimate=pl.CostEstimate(
            flops=1024 * 1024 * D, bytes_accessed=16_000_000, transcendentals=0
        ),
        name="head",
    )(gr, xt, own, other)


def shards(section_output, norm_gain, head_weight, targets):
    x, ylo, yhi, z, core = (lax.axis_index(a) for a in AX)
    y = yhi * 2 + ylo
    shard = (((x * 2 + ylo) * 2 + yhi) * 4 + z) * 2 + core
    tab = table(x, y, z, core, shard)

    xt = section_output.T.astype(F32)
    gain = norm_gain.astype(F32)[:, None]
    scaled_x = (xt * gain).astype(BF)
    squares = jnp.sum(xt * xt, axis=0, keepdims=True)
    extra = jnp.concatenate(
        split3(squares) + [jnp.zeros((SQ - 3, TB), BF)], axis=0
    )
    blocks = [
        jnp.concatenate([scaled_x[:PT], extra], axis=0),
        scaled_x[PT : 2 * PT],
        scaled_x[2 * PT :],
    ]
    other = send(head_weight, TWIN)
    turned = flip(head_weight, other)

    tgt = lax.dynamic_index_in_dim(
        targets.reshape(2, 4, 2, TB), core, axis=2, keepdims=False
    ).transpose(1, 0, 2).reshape(4, 1, 2 * TB)
    halves = gather(blocks)
    halves, turned, tgt, tab = lax.optimization_barrier((halves, turned, tgt, tab))

    act, total, rinv, xt_all = act_call(tab, halves, head_weight, other)
    totals = lax.all_to_all(
        jnp.broadcast_to(total[None], (64, 8, TB)), AX[:4], 0, 0
    )
    expo, stats, bend = prep_call(tab, act, tgt)

    out = grad_call(tab, expo, bend, totals, rinv, tgt, turned)
    gz, gr, gy = out[:3]
    kept = keep_call(tab, gz, gy, turned)
    own0, other0, gain0 = head_call(gr, xt_all, head_weight, other, 0)
    own1, other1, gain1 = head_call(gr, xt_all, head_weight, other, 1)
    sums = reduce_scatter(list(out[3:]), kept)
    head_grad = jnp.concatenate(
        [add(own0, send(other0, TWIN)), add(own1, send(other1, TWIN))], axis=1
    )

    by_owner = jnp.broadcast_to(
        stats.reshape(1, 1, 3, 4, 2, TB).transpose(0, 1, 4, 3, 2, 5).reshape(1, 2, 4, 3 * TB),
        (8, 2, 4, 3 * TB),
    )
    gains = jnp.concatenate([gain0, gain1], axis=1).reshape(8, 1, 1, FB)
    gains = jnp.concatenate([gains, jnp.zeros((8, 1, 1, TB // 2), F32)], axis=3)
    mixed = jnp.concatenate(
        [by_owner, jnp.broadcast_to(gains, (8, 2, 4, 5 * TB))], axis=3
    ).reshape(64, 8, TB)
    mixed = jnp.sum(lax.all_to_all(mixed, AX[:4], 0, 0), axis=0)
    picked, slope, slope_at = mixed[0:1], mixed[1:2], mixed[2:3]
    gain_part = mixed[3:].reshape(5 * TB)[:FB]
    gain_grad = (gain_part + send(gain_part, TWIN)) / norm_gain.astype(F32)

    row = jnp.sum(totals, axis=0)
    total = lax.dynamic_slice(row, (z * 2 + yhi, 0), (1, TB))
    rinv = lax.dynamic_slice(rinv, (z, 0, yhi * TB), (1, 1, TB)).reshape(1, TB)
    token_loss = (jnp.log(total) - picked).reshape(TB)
    inner = slope / total - slope_at
    grad_hidden = jnp.concatenate(sums, axis=0)
    grad_input = (rinv * (grad_hidden * gain) - xt * (rinv * rinv * inner / D)).astype(BF).T
    return (token_loss, grad_input, head_grad, gain_grad)


def solution(mesh):
    fine = Mesh(mesh.devices.reshape(4, 2, 2, 4, 2), AX)
    pipe, dp = ("x", "ylo"), ("yhi", "z", "core")
    return jax.shard_map(
        shards,
        mesh=fine,
        in_specs=(P(dp, pipe), P(pipe), P(pipe + dp, None), P()),
        out_specs=(P(dp), P(dp, pipe), P(pipe + dp, None), P(pipe)),
        check_vma=False,
    )
```

profile of v0, /device:TPU:0, one launch (start us, length us, event | category | flops | bytes accessed | tf_op | source)
XLA Modules:
  0.0 247.5 jit_solution(5912963273230947121)
XLA Ops:
  1.3 1.1 fusion.1
  2.4 2.1 collective-permute-start.12
  4.5 1.6 collective-permute-start.6
  6.2 1.6 collective-permute-start
  7.8 3.8 %collective-permute-start.18 = (bf16[512,4608]{1,0:T(8,128)(2,1)}, bf16[512,4608]{1,0:T(8,128)(2,1)}, u32[]{:S(2)}, u32[]{:S(2)}) collective-permute-start(bf16[512,4608]{1,0:T(8,128)(2,1)} %own_w.3), channel_id=1, source_target_pairs={{0,1},{1,0},{2,3},{3,2},{4,5},{5,4},{6,7},{7,6},{8,9},{9,8},{10,11... | collective-permute-start | bytes 14155784 | tf_op jit(solution)/shard_map/ppermute | solution.py:52
  15.3 2.7 %collective-permute-start.1 = (bf16[2,208,128]{2,1,0:T(8,128)(2,1)S(1)}, bf16[2,208,128]{2,1,0:T(8,128)(2,1)S(1)}, u32[]{:S(2)}, u32[]{:S(2)}) collective-permute-start(bf16[2,208,128]{2,1,0:T(8,128)(2,1)S(1)} %pad_maximum_fusion.8), channel_id=1, source_target_pairs={{0,96},{1,33},{2,98},{3,35},{4,100},{5,37},{6,102},{7,39},{8,104},... | collective-permute-start | bytes 319496 | tf_op jit(solution)/shard_map/ppermute | solution.py:52
  21.3 0.9 collective-permute-done.1
  22.2 1.0 collective-permute-start.2
  24.7 1.4 collective-permute-start.15
  26.0 2.1 collective-permute-done.2
  28.1 1.9 collective-permute-start.3
  30.1 3.8 %collective-permute-start.9 = (bf16[8,192,128]{2,1,0:T(8,128)(2,1)S(1)}, bf16[8,192,128]{2,1,0:T(8,128)(2,1)S(1)}, u32[]{:S(2)}, u32[]{:S(2)}) collective-permute-start(bf16[8,192,128]{2,1,0:T(8,128)(2,1)S(1)} %pad_maximum_fusion.2), channel_id=1, source_target_pairs={{0,6},{1,3},{2,4},{3,1},{4,2},{5,7},{6,0},{7,5},{8,14},{9,11},{10,... | collective-permute-start | bytes 1179656 | tf_op jit(solution)/shard_map/ppermute | solution.py:52
  35.4 0.9 constant_dynamic-update-slice_fusion.22
  36.3 3.6 %collective-permute-done.3 = bf16[8,208,128]{2,1,0:T(8,128)(2,1)S(1)} collective-permute-done((bf16[8,208,128]{2,1,0:T(8,128)(2,1)S(1)}, bf16[8,208,128]{2,1,0:T(8,128)(2,1)S(1)}, u32[]{:S(2)}, u32[]{:S(2)}) %collective-permute-start.3) | collective-permute-done | bytes 426016 | tf_op jit(solution)/shard_map/ppermute | solution.py:52
  39.9 0.9 constant_dynamic-update-slice_fusion
  40.8 2.9 %collective-permute-start.4 = (bf16[16,208,128]{2,1,0:T(8,128)(2,1)S(1)}, bf16[16,208,128]{2,1,0:T(8,128)(2,1)S(1)}, u32[]{:S(2)}, u32[]{:S(2)}) collective-permute-start(bf16[16,208,128]{2,1,0:T(8,128)(2,1)S(1)} %get-tuple-element.94), channel_id=1, source_target_pairs={{0,2},{1,7},{2,0},{3,5},{4,6},{5,3},{6,4},{7,1},{8,10},{9,15},{10,... | collective-permute-start | bytes 2555912 | tf_op jit(solution)/shard_map/ppermute | solution.py:52
  44.4 0.9 constant_dynamic-update-slice_fusion.11
  45.3 2.6 %collective-permute-start.10 = (bf16[16,192,128]{2,1,0:T(8,128)(2,1)S(1)}, bf16[16,192,128]{2,1,0:T(8,128)(2,1)S(1)}, u32[]{:S(2)}, u32[]{:S(2)}) collective-permute-start(bf16[16,192,128]{2,1,0:T(8,128)(2,1)S(1)} %get-tuple-element.104), channel_id=1, source_target_pairs={{0,32},{1,97},{2,34},{3,99},{4,36},{5,101},{6,38},{7,103},{8,40},{... | collective-permute-start | bytes 2359304 | tf_op jit(solution)/shard_map/ppermute | solution.py:52
  48.3 1.0 constant_dynamic-update-slice_fusion.27.refs_4_
  49.3 8.1 %collective-permute-done.4 = bf16[16,208,128]{2,1,0:T(8,128)(2,1)S(1)} collective-permute-done((bf16[16,208,128]{2,1,0:T(8,128)(2,1)S(1)}, bf16[16,208,128]{2,1,0:T(8,128)(2,1)S(1)}, u32[]{:S(2)}, u32[]{:S(2)}) %collective-permute-start.4) | collective-permute-done | bytes 852000 | tf_op jit(solution)/shard_map/ppermute | solution.py:52
  57.4 1.0 constant_dynamic-update-slice_fusion.5.refs_0_
  58.4 3.1 %collective-permute-start.5 = (bf16[32,208,128]{2,1,0:T(8,128)(2,1)}, bf16[32,208,128]{2,1,0:T(8,128)(2,1)S(1)}, u32[]{:S(2)}, u32[]{:S(2)}) collective-permute-start(bf16[32,208,128]{2,1,0:T(8,128)(2,1)} %constant_dynamic-update-slice_fusion.5.refs_0_), channel_id=1, source_target_pairs={{0,6},{1,3},{2,4},{3,1},{4,2},{5,7},{6,0},{7,5},{8,14},{9,11},{10,... | collective-permute-start | bytes 5111816 | tf_op jit(solution)/shard_map/ppermute | solution.py:52
  61.5 1.4 collective-permute-done.10
  63.0 0.9 constant_dynamic-update-slice_fusion.16.refs_2_
  63.9 2.1 collective-permute-start.11
  67.3 8.6 %flip.1 = (bf16[4,2,192,1024]{3,2,1,0:T(8,128)(2,1)}, bf16[4,2,192,1024]{3,2,1,0:T(8,128)(2,1)}, bf16[2,4,192,1024]{3,2,1,0:T(8,128)(2,1)}) custom-call(bf16[512,4608]{1,0:T(8,128)(2,1)} %own_w.3, bf16[512,4608]{1,0:T(8,128)(2,1)} %collective-permute-done.18.other_ref.refs_7_.other_w), custom_call_target="tpu_custom_call" | custom-call | bytes 18874368 | tf_op jit(solution)/shard_map/flip/pallas_call | solution.py:122
  75.9 10.0 %collective-permute-done.11.refs_3_ = bf16[32,192,128]{2,1,0:T(8,128)(2,1)} collective-permute-done((bf16[32,192,128]{2,1,0:T(8,128)(2,1)}, bf16[32,192,128]{2,1,0:T(8,128)(2,1)}, u32[]{:S(2)}, u32[]{:S(2)}) %collective-permute-start.11) | collective-permute-done | bytes 1572896 | tf_op jit(solution)/shard_map/ppermute | solution.py:52
  85.9 1.2 copy-done.11
  87.1 19.7 %act.1 = (f32[4,1024,256]{2,1,0:T(8,128)}, f32[8,128]{1,0:T(8,128)}, f32[4,1,256]{2,1,0:T(1,128)}, bf16[4,4608,256]{2,1,0:T(8,128)(2,1)}) custom-call(s32[26]{0:T(128)} %concatenate.94.tab, bf16[32,208,128]{2,1,0:T(8,128)(2,1)} %constant_dynamic-update-slice_fusion.5.refs_0_, bf16[32,208,128]{2,1,0:T(8,128)(2,1)} %copy-done.11, ...), custom_call_target="tpu_custom_call" | custom-call | flops 9663676416 | bytes 30000000 | tf_op jit(solution)/shard_map/act/pallas_call | solution.py:235
  106.8 1.4 broadcast_in_dim.39
  108.2 10.7 %all-to-all-start = ((f32[64,8,128]{2,1,0:T(8,128)}), f32[64,8,128]{2,1,0:T(8,128)S(1)}, u32[]{:S(2)}, u32[]{:S(2)}) async-start(f32[64,8,128]{2,1,0:T(8,128)} %broadcast_in_dim.39), calls=%async_computation | async-start | bytes 524288 | tf_op jit(solution)/shard_map/all_to_all | solution.py:516
  118.9 8.6 %prep.1 = (f32[4,1024,256]{2,1,0:T(8,128)}, f32[3,8,128]{2,1,0:T(8,128)}, f32[4,1,256]{2,1,0:T(1,128)}) custom-call(s32[26]{0:T(128)} %concatenate.94.tab, f32[4,1024,256]{2,1,0:T(8,128)} %get-tuple-element.51.act_ref, s32[4,1,256]{2,1,0:T(1,128)} %bitcast.76), custom_call_target="tpu_custom_call" | custom-call | flops 16777216 | bytes 8388608 | tf_op jit(solution)/shard_map/prep/pallas_call | solution.py:309
  129.8 15.5 %grad.1 = (bf16[4,1024,256]{2,1,0:T(8,128)(2,1)}, bf16[4,1024,256]{2,1,0:T(8,128)(2,1)}, bf16[2,2,1024,256]{3,2,1,0:T(8,128)(2,1)}, bf16[32,192,128]{2,1,0:T(8,1...) custom-call(s32[26]{0:T(128)} %concatenate.94.tab, f32[4,1024,256]{2,1,0:T(8,128)} %get-tuple-element.54.expo_ref, ...), custom_call_target="tpu_custom_call" | custom-call | flops 4831838208 | bytes 24000000 | tf_op jit(solution)/shard_map/grad/pallas_call | solution.py:420
  145.3 2.4 collective-permute-start.19
  147.7 2.9 %collective-permute-start.25 = (bf16[32,192,128]{2,1,0:T(8,128)(2,1)}, bf16[32,192,128]{2,1,0:T(8,128)(2,1)}, u32[]{:S(2)}, u32[]{:S(2)}) collective-permute-start(bf16[32,192,128]{2,1,0:T(8,128)(2,1)} %get-tuple-element.69), channel_id=1, source_target_pairs={{0,96},{1,33},{2,98},{3,35},{4,100},{5,37},{6,102},{7,39},{8,104},... | collective-permute-start | bytes 4718600 | tf_op jit(solution)/shard_map/ppermute | solution.py:52
  150.6 2.7 %collective-permute-start.31 = (bf16[32,192,128]{2,1,0:T(8,128)(2,1)}, bf16[32,192,128]{2,1,0:T(8,128)(2,1)}, u32[]{:S(2)}, u32[]{:S(2)}) collective-permute-start(bf16[32,192,128]{2,1,0:T(8,128)(2,1)} %get-tuple-element.71), channel_id=1, source_target_pairs={{0,24},{1,17},{2,26},{3,19},{4,28},{5,21},{6,30},{7,23},{8,16},{9,... | collective-permute-start | bytes 4718600 | tf_op jit(solution)/shard_map/ppermute | solution.py:52
  153.3 10.0 %head.3 = (bf16[512,2304]{1,0:T(8,128)(2,1)}, bf16[512,2304]{1,0:T(8,128)(2,1)}, f32[1,2304]{1,0:T(1,128)}) custom-call(bf16[4,1024,256]{2,1,0:T(8,128)(2,1)} %get-tuple-element.60.gr, bf16[4,4608,256]{2,1,0:T(8,128)(2,1)} %get-tuple-element.61.xt, bf16[512,4608]{1,0:T(8,128)(2,1)} %own_w.3, bf16[512,4608]{1,0:T(8,128)(2,1)} %collective-permute-done.18.other_ref.refs_7_.other_w), custom_call_target="tpu_custom_call" | custom-call | flops 4831838208 | bytes 16000000 | tf_op jit(solution)/shard_map/head/pallas_call | solution.py:467
  163.3 10.1 %head.2 = (bf16[512,2304]{1,0:T(8,128)(2,1)}, bf16[512,2304]{1,0:T(8,128)(2,1)}, f32[1,2304]{1,0:T(1,128)}) custom-call(bf16[4,1024,256]{2,1,0:T(8,128)(2,1)} %get-tuple-element.60.gr, bf16[4,4608,256]{2,1,0:T(8,128)(2,1)} %get-tuple-element.61.xt, bf16[512,4608]{1,0:T(8,128)(2,1)} %own_w.3, bf16[512,4608]{1,0:T(8,128)(2,1)} %collective-permute-done.18.other_ref.refs_7_.other_w), custom_call_target="tpu_custom_call" | custom-call | flops 4831838208 | bytes 16000000 | tf_op jit(solution)/shard_map/head/pallas_call | solution.py:467
  175.2 4.6 %all-to-all-start.1 = ((f32[64,8,128]{2,1,0:T(8,128)}), f32[64,8,128]{2,1,0:T(8,128)S(1)}, u32[]{:S(2)}, u32[]{:S(2)}) async-start(f32[64,8,128]{2,1,0:T(8,128)} %reshape.101), calls=%async_computation.1 | async-start | bytes 524288 | tf_op jit(solution)/shard_map/all_to_all | solution.py:540
  180.5 11.6 %keep.1 = (bf16[32,192,128]{2,1,0:T(8,128)(2,1)}, bf16[32,192,128]{2,1,0:T(8,128)(2,1)}, bf16[32,192,128]{2,1,0:T(8,128)(2,1)}) custom-call(s32[26]{0:T(128)} %concatenate.94.tab, bf16[4,1024,256]{2,1,0:T(8,128)(2,1)} %get-tuple-element.64.gz, bf16[2,2,1024,256]{3,2,1,0:T(8,128)(2,1)} %get-tuple-element.65.gy, ...), custom_call_target="tpu_custom_call" | custom-call | flops 4831838208 | bytes 18000000 | tf_op jit(solution)/shard_map/keep/pallas_call | solution.py:434
  192.5 2.5 %add_convert_fusion.7 = (bf16[16,192,128]{2,1,0:T(8,128)(2,1)S(1)}, bf16[16,192,128]{2,1,0:T(8,128)(2,1)S(1)}) fusion(bf16[32,192,128]{2,1,0:T(8,128)(2,1)} %collective-permute-done.19, bf16[32,192,128]{2,1,0:T(8,128)(2,1)} %get-tuple-element.66), kind=kLoop, calls=%fused_computation.8 | loop fusion | flops 3145728 | bytes 4718592 | tf_op jit(solution)/shard_map/convert_element_type | solution.py:84
  195.1 1.5 collective-permute-start.20
  196.6 2.1 add_convert_fusion.5
  198.7 1.7 collective-permute-start.26
  200.4 2.0 add_convert_fusion.3
  202.4 1.6 collective-permute-start.32
  203.9 1.2 fusion.13
  205.8 1.4 collective-permute-done.20
  207.4 2.8 %collective-permute-start.21 = (bf16[8,192,128]{2,1,0:T(8,128)(2,1)S(1)}, bf16[8,192,128]{2,1,0:T(8,128)(2,1)S(1)}, u32[]{:S(2)}, u32[]{:S(2)}) collective-permute-start(bf16[8,192,128]{2,1,0:T(8,128)(2,1)S(1)} %get-tuple-element.83), channel_id=1, source_target_pairs={{0,24},{1,17},{2,26},{3,19},{4,28},{5,21},{6,30},{7,23},{8,16},{9,... | collective-permute-start | bytes 1179656 | tf_op jit(solution)/shard_map/ppermute | solution.py:52
  211.0 2.2 collective-permute-start.27
  213.2 4.0 %collective-permute-done.32 = bf16[16,192,128]{2,1,0:T(8,128)(2,1)S(1)} collective-permute-done((bf16[16,192,128]{2,1,0:T(8,128)(2,1)S(1)}, bf16[16,192,128]{2,1,0:T(8,128)(2,1)S(1)}, u32[]{:S(2)}, u32[]{:S(2)}) %collective-permute-start.32) | collective-permute-done | bytes 786464 | tf_op jit(solution)/shard_map/ppermute | solution.py:52
  217.4 2.8 %collective-permute-start.33 = (bf16[8,192,128]{2,1,0:T(8,128)(2,1)S(1)}, bf16[8,192,128]{2,1,0:T(8,128)(2,1)S(1)}, u32[]{:S(2)}, u32[]{:S(2)}) collective-permute-start(bf16[8,192,128]{2,1,0:T(8,128)(2,1)S(1)} %get-tuple-element.87), channel_id=1, source_target_pairs={{0,96},{1,33},{2,98},{3,35},{4,100},{5,37},{6,102},{7,39},{8,104},... | collective-permute-start | bytes 1179656 | tf_op jit(solution)/shard_map/ppermute | solution.py:52
  220.1 2.4 add_convert_fusion
  223.2 2.5 %pad_maximum_fusion = bf16[512,4608]{1,0:T(8,128)(2,1)} fusion(bf16[512,2304]{1,0:T(8,128)(2,1)S(1)} %add_convert_fusion, bf16[512,2304]{1,0:T(8,128)(2,1)S(1)} %add_convert_fusion.1), kind=kLoop, calls=%fused_computation | loop fusion | flops 9437184 | bytes 9437184 | tf_op jit(solution)/shard_map/concatenate | solution.py:527
  225.8 1.6 collective-permute-start.22
  228.3 1.3 collective-permute-start.34
  229.6 2.0 collective-permute-done.22
  231.7 1.1 collective-permute-start.23
  233.4 3.2 %collective-permute-start.29 = (bf16[2,192,128]{2,1,0:T(8,128)(2,1)S(1)}, bf16[2,192,128]{2,1,0:T(8,128)(2,1)S(1)}, u32[]{:S(2)}, u32[]{:S(2)}) collective-permute-start(bf16[2,192,128]{2,1,0:T(8,128)(2,1)S(1)} %get-tuple-element.99), channel_id=1, source_target_pairs={{0,24},{1,17},{2,26},{3,19},{4,28},{5,21},{6,30},{7,23},{8,16},{9,... | collective-permute-start | bytes 294920 | tf_op jit(solution)/shard_map/ppermute | solution.py:52
  236.6 2.0 collective-permute-start.35
  238.6 1.0 collective-permute-start.24
  240.2 2.3 collective-permute-done.35
  242.8 1.0 collective-permute-done.30
  243.8 2.8 %collective-permute-done.36 = bf16[1,192,128]{2,1,0:T(8,128)(2,1)S(1)} collective-permute-done((bf16[1,192,128]{2,1,0:T(8,128)(2,1)S(1)}, bf16[1,192,128]{2,1,0:T(8,128)(2,1)S(1)}, u32[]{:S(2)}, u32[]{:S(2)}) %collective-permute-start.36) | collective-permute-done | bytes 49184 | tf_op jit(solution)/shard_map/ppermute | solution.py:52
  (128 shorter events, 24.4 us)
Async XLA Ops:
  0.6 65.4 %copy-start = (s32[2048]{0:T(1024)S(1)}, s32[2048]{0:T(1024)}, u32[]{:S(2)}) copy-start(s32[2048]{0:T(1024)} %param.7) | copy-start | bytes 24580
  2.4 10.5 %collective-permute-start.12 = (bf16[1,192,128]{2,1,0:T(8,128)(2,1)S(1)}, bf16[1,192,128]{2,1,0:T(8,128)(2,1)S(1)}, u32[]{:S(2)}, u32[]{:S(2)}) collective-permute-start(bf16[1,192,128]{2,1,0:T(8,128)(2,1)S(1)} %get-tuple-element.116), channel_id=1, source_target_pairs={{0,2},{1,7},{2,0},{3,5},{4,6},{5,3},{6,4},{7,1},{8,10},{9,15},{10,... | collective-permute-start | bytes 147464 | tf_op jit(solution)/shard_map/ppermute | solution.py:52
  4.5 8.9 %collective-permute-start.6 = (bf16[1,192,128]{2,1,0:T(8,128)(2,1)S(1)}, bf16[1,192,128]{2,1,0:T(8,128)(2,1)S(1)}, u32[]{:S(2)}, u32[]{:S(2)}) collective-permute-start(bf16[1,192,128]{2,1,0:T(8,128)(2,1)S(1)} %get-tuple-element.117), channel_id=1, source_target_pairs={{0,16},{1,25},{2,18},{3,27},{4,20},{5,29},{6,22},{7,31},{8,24},{9,... | collective-permute-start | bytes 147464 | tf_op jit(solution)/shard_map/ppermute | solution.py:52
  6.2 9.0 %collective-permute-start = (bf16[1,208,128]{2,1,0:T(8,128)(2,1)S(1)}, bf16[1,208,128]{2,1,0:T(8,128)(2,1)S(1)}, u32[]{:S(2)}, u32[]{:S(2)}) collective-permute-start(bf16[1,208,128]{2,1,0:T(8,128)(2,1)S(1)} %bitcast.71), channel_id=1, source_target_pairs={{0,32},{1,97},{2,34},{3,99},{4,36},{5,101},{6,38},{7,103},{8,40},{... | collective-permute-start | bytes 159752 | tf_op jit(solution)/shard_map/ppermute | solution.py:52
  7.8 59.4 %collective-permute-start.18 = (bf16[512,4608]{1,0:T(8,128)(2,1)}, bf16[512,4608]{1,0:T(8,128)(2,1)}, u32[]{:S(2)}, u32[]{:S(2)}) collective-permute-start(bf16[512,4608]{1,0:T(8,128)(2,1)} %own_w.3), channel_id=1, source_target_pairs={{0,1},{1,0},{2,3},{3,2},{4,5},{5,4},{6,7},{7,6},{8,9},{9,8},{10,11... | collective-permute-start | bytes 14155784 | tf_op jit(solution)/shard_map/ppermute | solution.py:52
  12.9 5.9 %collective-permute-start.13 = (bf16[2,192,128]{2,1,0:T(8,128)(2,1)S(1)}, bf16[2,192,128]{2,1,0:T(8,128)(2,1)S(1)}, u32[]{:S(2)}, u32[]{:S(2)}) collective-permute-start(bf16[2,192,128]{2,1,0:T(8,128)(2,1)S(1)} %pad_maximum_fusion.10), channel_id=1, source_target_pairs={{0,6},{1,3},{2,4},{3,1},{4,2},{5,7},{6,0},{7,5},{8,14},{9,11},{10,... | collective-permute-start | bytes 294920 | tf_op jit(solution)/shard_map/ppermute | solution.py:52
  13.4 5.9 %collective-permute-start.7 = (bf16[2,192,128]{2,1,0:T(8,128)(2,1)S(1)}, bf16[2,192,128]{2,1,0:T(8,128)(2,1)S(1)}, u32[]{:S(2)}, u32[]{:S(2)}) collective-permute-start(bf16[2,192,128]{2,1,0:T(8,128)(2,1)S(1)} %pad_maximum_fusion.9), channel_id=1, source_target_pairs={{0,24},{1,17},{2,26},{3,19},{4,28},{5,21},{6,30},{7,23},{8,16},{9,... | collective-permute-start | bytes 294920 | tf_op jit(solution)/shard_map/ppermute | solution.py:52
  15.3 6.9 %collective-permute-start.1 = (bf16[2,208,128]{2,1,0:T(8,128)(2,1)S(1)}, bf16[2,208,128]{2,1,0:T(8,128)(2,1)S(1)}, u32[]{:S(2)}, u32[]{:S(2)}) collective-permute-start(bf16[2,208,128]{2,1,0:T(8,128)(2,1)S(1)} %pad_maximum_fusion.8), channel_id=1, source_target_pairs={{0,96},{1,33},{2,98},{3,35},{4,100},{5,37},{6,102},{7,39},{8,104},... | collective-permute-start | bytes 319496 | tf_op jit(solution)/shard_map/ppermute | solution.py:52
  18.9 5.7 %collective-permute-start.14 = (bf16[4,192,128]{2,1,0:T(8,128)(2,1)S(1)}, bf16[4,192,128]{2,1,0:T(8,128)(2,1)S(1)}, u32[]{:S(2)}, u32[]{:S(2)}) collective-permute-start(bf16[4,192,128]{2,1,0:T(8,128)(2,1)S(1)} %pad_maximum_fusion.7), channel_id=1, source_target_pairs={{0,32},{1,97},{2,34},{3,99},{4,36},{5,101},{6,38},{7,103},{8,40},{... | collective-permute-start | bytes 589832 | tf_op jit(solution)/shard_map/ppermute | solution.py:52
  19.3 10.7 %collective-permute-start.8 = (bf16[4,192,128]{2,1,0:T(8,128)(2,1)S(1)}, bf16[4,192,128]{2,1,0:T(8,128)(2,1)S(1)}, u32[]{:S(2)}, u32[]{:S(2)}) collective-permute-start(bf16[4,192,128]{2,1,0:T(8,128)(2,1)S(1)} %pad_maximum_fusion.6), channel_id=1, source_target_pairs={{0,2},{1,7},{2,0},{3,5},{4,6},{5,3},{6,4},{7,1},{8,10},{9,15},{10,... | collective-permute-start | bytes 589832 | tf_op jit(solution)/shard_map/ppermute | solution.py:52
  22.2 5.9 %collective-permute-start.2 = (bf16[4,208,128]{2,1,0:T(8,128)(2,1)S(1)}, bf16[4,208,128]{2,1,0:T(8,128)(2,1)S(1)}, u32[]{:S(2)}, u32[]{:S(2)}) collective-permute-start(bf16[4,208,128]{2,1,0:T(8,128)(2,1)S(1)} %pad_maximum_fusion.5), channel_id=1, source_target_pairs={{0,16},{1,25},{2,18},{3,27},{4,20},{5,29},{6,22},{7,31},{8,24},{9,... | collective-permute-start | bytes 638984 | tf_op jit(solution)/shard_map/ppermute | solution.py:52
  24.7 10.7 %collective-permute-start.15 = (bf16[8,192,128]{2,1,0:T(8,128)(2,1)S(1)}, bf16[8,192,128]{2,1,0:T(8,128)(2,1)S(1)}, u32[]{:S(2)}, u32[]{:S(2)}) collective-permute-start(bf16[8,192,128]{2,1,0:T(8,128)(2,1)S(1)} %pad_maximum_fusion.3), channel_id=1, source_target_pairs={{0,96},{1,33},{2,98},{3,35},{4,100},{5,37},{6,102},{7,39},{8,104},... | collective-permute-start | bytes 1179656 | tf_op jit(solution)/shard_map/ppermute | solution.py:52
  28.1 11.8 %collective-permute-start.3 = (bf16[8,208,128]{2,1,0:T(8,128)(2,1)S(1)}, bf16[8,208,128]{2,1,0:T(8,128)(2,1)S(1)}, u32[]{:S(2)}, u32[]{:S(2)}) collective-permute-start(bf16[8,208,128]{2,1,0:T(8,128)(2,1)S(1)} %pad_maximum_fusion.1), channel_id=1, source_target_pairs={{0,24},{1,17},{2,26},{3,19},{4,28},{5,21},{6,30},{7,23},{8,16},{9,... | collective-permute-start | bytes 1277960 | tf_op jit(solution)/shard_map/ppermute | solution.py:52
  30.1 14.3 %collective-permute-start.9 = (bf16[8,192,128]{2,1,0:T(8,128)(2,1)S(1)}, bf16[8,192,128]{2,1,0:T(8,128)(2,1)S(1)}, u32[]{:S(2)}, u32[]{:S(2)}) collective-permute-start(bf16[8,192,128]{2,1,0:T(8,128)(2,1)S(1)} %pad_maximum_fusion.2), channel_id=1, source_target_pairs={{0,6},{1,3},{2,4},{3,1},{4,2},{5,7},{6,0},{7,5},{8,14},{9,11},{10,... | collective-permute-start | bytes 1179656 | tf_op jit(solution)/shard_map/ppermute | solution.py:52
  36.3 12.0 %collective-permute-start.16 = (bf16[16,192,128]{2,1,0:T(8,128)(2,1)S(1)}, bf16[16,192,128]{2,1,0:T(8,128)(2,1)S(1)}, u32[]{:S(2)}, u32[]{:S(2)}) collective-permute-start(bf16[16,192,128]{2,1,0:T(8,128)(2,1)S(1)} %get-tuple-element.102), channel_id=1, source_target_pairs={{0,16},{1,25},{2,18},{3,27},{4,20},{5,29},{6,22},{7,31},{8,24},{9,... | collective-permute-start | bytes 2359304 | tf_op jit(solution)/shard_map/ppermute | solution.py:52
  40.8 16.6 %collective-permute-start.4 = (bf16[16,208,128]{2,1,0:T(8,128)(2,1)S(1)}, bf16[16,208,128]{2,1,0:T(8,128)(2,1)S(1)}, u32[]{:S(2)}, u32[]{:S(2)}) collective-permute-start(bf16[16,208,128]{2,1,0:T(8,128)(2,1)S(1)} %get-tuple-element.94), channel_id=1, source_target_pairs={{0,2},{1,7},{2,0},{3,5},{4,6},{5,3},{6,4},{7,1},{8,10},{9,15},{10,... | collective-permute-start | bytes 2555912 | tf_op jit(solution)/shard_map/ppermute | solution.py:52
  45.3 17.7 %collective-permute-start.10 = (bf16[16,192,128]{2,1,0:T(8,128)(2,1)S(1)}, bf16[16,192,128]{2,1,0:T(8,128)(2,1)S(1)}, u32[]{:S(2)}, u32[]{:S(2)}) collective-permute-start(bf16[16,192,128]{2,1,0:T(8,128)(2,1)S(1)} %get-tuple-element.104), channel_id=1, source_target_pairs={{0,32},{1,97},{2,34},{3,99},{4,36},{5,101},{6,38},{7,103},{8,40},{... | collective-permute-start | bytes 2359304 | tf_op jit(solution)/shard_map/ppermute | solution.py:52
  49.3 26.6 %collective-permute-start.17 = (bf16[32,192,128]{2,1,0:T(8,128)(2,1)}, bf16[32,192,128]{2,1,0:T(8,128)(2,1)S(1)}, u32[]{:S(2)}, u32[]{:S(2)}) collective-permute-start(bf16[32,192,128]{2,1,0:T(8,128)(2,1)} %constant_dynamic-update-slice_fusion.27.refs_4_), channel_id=1, source_target_pairs={{0,24},{1,17},{2,26},{3,19},{4,28},{5,21},{6,30},{7,23},{8,16},{9,... | collective-permute-start | bytes 4718600 | tf_op jit(solution)/shard_map/ppermute | solution.py:52
  58.4 27.4 %collective-permute-start.5 = (bf16[32,208,128]{2,1,0:T(8,128)(2,1)}, bf16[32,208,128]{2,1,0:T(8,128)(2,1)S(1)}, u32[]{:S(2)}, u32[]{:S(2)}) collective-permute-start(bf16[32,208,128]{2,1,0:T(8,128)(2,1)} %constant_dynamic-update-slice_fusion.5.refs_0_), channel_id=1, source_target_pairs={{0,6},{1,3},{2,4},{3,1},{4,2},{5,7},{6,0},{7,5},{8,14},{9,11},{10,... | collective-permute-start | bytes 5111816 | tf_op jit(solution)/shard_map/ppermute | solution.py:52
  63.9 21.9 %collective-permute-start.11 = (bf16[32,192,128]{2,1,0:T(8,128)(2,1)}, bf16[32,192,128]{2,1,0:T(8,128)(2,1)}, u32[]{:S(2)}, u32[]{:S(2)}) collective-permute-start(bf16[32,192,128]{2,1,0:T(8,128)(2,1)} %constant_dynamic-update-slice_fusion.16.refs_2_), channel_id=1, source_target_pairs={{0,96},{1,33},{2,98},{3,35},{4,100},{5,37},{6,102},{7,39},{8,104},... | collective-permute-start | bytes 4718600 | tf_op jit(solution)/shard_map/ppermute | solution.py:52
  75.9 10.0 %copy-start.12 = (bf16[32,192,128]{2,1,0:T(8,128)(2,1)}, bf16[32,192,128]{2,1,0:T(8,128)(2,1)S(1)}, u32[]{:S(2)}) copy-start(bf16[32,192,128]{2,1,0:T(8,128)(2,1)S(1)} %collective-permute-done.17.refs_5_) | copy-start | bytes 4718596
  85.9 1.3 copy-start.11
  108.2 20.9 %all-to-all-start = ((f32[64,8,128]{2,1,0:T(8,128)}), f32[64,8,128]{2,1,0:T(8,128)S(1)}, u32[]{:S(2)}, u32[]{:S(2)}) async-start(f32[64,8,128]{2,1,0:T(8,128)} %broadcast_in_dim.39), calls=%async_computation | async-start | bytes 524288 | tf_op jit(solution)/shard_map/all_to_all | solution.py:516
  129.2 0.7 copy-start.6
  145.3 46.8 %collective-permute-start.19 = (bf16[32,192,128]{2,1,0:T(8,128)(2,1)}, bf16[32,192,128]{2,1,0:T(8,128)(2,1)}, u32[]{:S(2)}, u32[]{:S(2)}) collective-permute-start(bf16[32,192,128]{2,1,0:T(8,128)(2,1)} %get-tuple-element.67), channel_id=1, source_target_pairs={{0,6},{1,3},{2,4},{3,1},{4,2},{5,7},{6,0},{7,5},{8,14},{9,11},{10,... | collective-permute-start | bytes 4718600 | tf_op jit(solution)/shard_map/ppermute | solution.py:52
  147.7 47.4 %collective-permute-start.25 = (bf16[32,192,128]{2,1,0:T(8,128)(2,1)}, bf16[32,192,128]{2,1,0:T(8,128)(2,1)}, u32[]{:S(2)}, u32[]{:S(2)}) collective-permute-start(bf16[32,192,128]{2,1,0:T(8,128)(2,1)} %get-tuple-element.69), channel_id=1, source_target_pairs={{0,96},{1,33},{2,98},{3,35},{4,100},{5,37},{6,102},{7,39},{8,104},... | collective-permute-start | bytes 4718600 | tf_op jit(solution)/shard_map/ppermute | solution.py:52
  150.6 48.1 %collective-permute-start.31 = (bf16[32,192,128]{2,1,0:T(8,128)(2,1)}, bf16[32,192,128]{2,1,0:T(8,128)(2,1)}, u32[]{:S(2)}, u32[]{:S(2)}) collective-permute-start(bf16[32,192,128]{2,1,0:T(8,128)(2,1)} %get-tuple-element.71), channel_id=1, source_target_pairs={{0,24},{1,17},{2,26},{3,19},{4,28},{5,21},{6,30},{7,23},{8,16},{9,... | collective-permute-start | bytes 4718600 | tf_op jit(solution)/shard_map/ppermute | solution.py:52
  163.3 10.1 %copy-start.9 = (f32[1,2304]{1,0:T(1,128)S(1)}, f32[1,2304]{1,0:T(1,128)}, u32[]{:S(2)}) copy-start(f32[1,2304]{1,0:T(1,128)} %get-tuple-element.63) | copy-start | bytes 27652
  173.4 7.0 %copy-start.7 = (f32[64,8,128]{2,1,0:T(8,128)S(1)}, f32[64,8,128]{2,1,0:T(8,128)}, u32[]{:S(2)}) copy-start(f32[64,8,128]{2,1,0:T(8,128)} %copy-done.6) | copy-start | bytes 786436
  175.2 16.9 %all-to-all-start.1 = ((f32[64,8,128]{2,1,0:T(8,128)}), f32[64,8,128]{2,1,0:T(8,128)S(1)}, u32[]{:S(2)}, u32[]{:S(2)}) async-start(f32[64,8,128]{2,1,0:T(8,128)} %reshape.101), calls=%async_computation.1 | async-start | bytes 524288 | tf_op jit(solution)/shard_map/all_to_all | solution.py:540
  179.8 40.3 %collective-permute-start.38 = (bf16[512,2304]{1,0:T(8,128)(2,1)}, bf16[512,2304]{1,0:T(8,128)(2,1)}, u32[]{:S(2)}, u32[]{:S(2)}) collective-permute-start(bf16[512,2304]{1,0:T(8,128)(2,1)} %get-tuple-element.75), channel_id=1, source_target_pairs={{0,1},{1,0},{2,3},{3,2},{4,5},{5,4},{6,7},{7,6},{8,9},{9,8},{10,11... | collective-permute-start | bytes 7077896 | tf_op jit(solution)/shard_map/ppermute | solution.py:52
  179.9 42.6 %collective-permute-start.37 = (bf16[512,2304]{1,0:T(8,128)(2,1)}, bf16[512,2304]{1,0:T(8,128)(2,1)S(1)}, u32[]{:S(2)}, u32[]{:S(2)}) collective-permute-start(bf16[512,2304]{1,0:T(8,128)(2,1)} %get-tuple-element.73), channel_id=1, source_target_pairs={{0,1},{1,0},{2,3},{3,2},{4,5},{5,4},{6,7},{7,6},{8,9},{9,8},{10,11... | collective-permute-start | bytes 7077896 | tf_op jit(solution)/shard_map/ppermute | solution.py:52
  192.2 10.2 %collective-permute-start.39 = (f32[576]{0:T(1024)S(1)}, f32[576]{0:T(1024)S(1)}, u32[]{:S(2)}, u32[]{:S(2)}) collective-permute-start(f32[576]{0:T(1024)S(1)} %bitcast.78), channel_id=1, source_target_pairs={{0,1},{1,0},{2,3},{3,2},{4,5},{5,4},{6,7},{7,6},{8,9},{9,8},{10,11... | collective-permute-start | bytes 6920 | tf_op jit(solution)/shard_map/ppermute | solution.py:52
  192.5 4.1 %copy-start.5 = (bf16[32,192,128]{2,1,0:T(8,128)(2,1)S(1)}, bf16[32,192,128]{2,1,0:T(8,128)(2,1)}, u32[]{:S(2)}) copy-start(bf16[32,192,128]{2,1,0:T(8,128)(2,1)} %get-tuple-element.68) | copy-start | bytes 4718596
  195.1 12.1 %collective-permute-start.20 = (bf16[16,192,128]{2,1,0:T(8,128)(2,1)S(1)}, bf16[16,192,128]{2,1,0:T(8,128)(2,1)S(1)}, u32[]{:S(2)}, u32[]{:S(2)}) collective-permute-start(bf16[16,192,128]{2,1,0:T(8,128)(2,1)S(1)} %get-tuple-element.77), channel_id=1, source_target_pairs={{0,2},{1,7},{2,0},{3,5},{4,6},{5,3},{6,4},{7,1},{8,10},{9,15},{10,... | collective-permute-start | bytes 2359304 | tf_op jit(solution)/shard_map/ppermute | solution.py:52
  196.6 3.7 %copy-start.4 = (bf16[32,192,128]{2,1,0:T(8,128)(2,1)S(1)}, bf16[32,192,128]{2,1,0:T(8,128)(2,1)}, u32[]{:S(2)}) copy-start(bf16[32,192,128]{2,1,0:T(8,128)(2,1)} %get-tuple-element.70) | copy-start | bytes 4718596
  198.7 12.1 %collective-permute-start.26 = (bf16[16,192,128]{2,1,0:T(8,128)(2,1)S(1)}, bf16[16,192,128]{2,1,0:T(8,128)(2,1)S(1)}, u32[]{:S(2)}, u32[]{:S(2)}) collective-permute-start(bf16[16,192,128]{2,1,0:T(8,128)(2,1)S(1)} %get-tuple-element.79), channel_id=1, source_target_pairs={{0,32},{1,97},{2,34},{3,99},{4,36},{5,101},{6,38},{7,103},{8,40},{... | collective-permute-start | bytes 2359304 | tf_op jit(solution)/shard_map/ppermute | solution.py:52
  200.4 4.8 %copy-start.10 = (bf16[576]{0:T(1024)(128)(2,1)S(1)}, bf16[576]{0:T(1024)(128)(2,1)}, u32[]{:S(2)}) copy-start(bf16[576]{0:T(1024)(128)(2,1)} %param.5) | copy-start | bytes 3460
  202.4 14.8 %collective-permute-start.32 = (bf16[16,192,128]{2,1,0:T(8,128)(2,1)S(1)}, bf16[16,192,128]{2,1,0:T(8,128)(2,1)S(1)}, u32[]{:S(2)}, u32[]{:S(2)}) collective-permute-start(bf16[16,192,128]{2,1,0:T(8,128)(2,1)S(1)} %get-tuple-element.81), channel_id=1, source_target_pairs={{0,16},{1,25},{2,18},{3,27},{4,20},{5,29},{6,22},{7,31},{8,24},{9,... | collective-permute-start | bytes 2359304 | tf_op jit(solution)/shard_map/ppermute | solution.py:52
  207.4 18.4 %collective-permute-start.21 = (bf16[8,192,128]{2,1,0:T(8,128)(2,1)S(1)}, bf16[8,192,128]{2,1,0:T(8,128)(2,1)S(1)}, u32[]{:S(2)}, u32[]{:S(2)}) collective-permute-start(bf16[8,192,128]{2,1,0:T(8,128)(2,1)S(1)} %get-tuple-element.83), channel_id=1, source_target_pairs={{0,24},{1,17},{2,26},{3,19},{4,28},{5,21},{6,30},{7,23},{8,16},{9,... | collective-permute-start | bytes 1179656 | tf_op jit(solution)/shard_map/ppermute | solution.py:52
  211.0 9.1 %copy-start.3 = (bf16[512,2304]{1,0:T(8,128)(2,1)S(1)}, bf16[512,2304]{1,0:T(8,128)(2,1)}, u32[]{:S(2)}) copy-start(bf16[512,2304]{1,0:T(8,128)(2,1)} %get-tuple-element.74) | copy-start | bytes 7077892
  211.0 16.4 %collective-permute-start.27 = (bf16[8,192,128]{2,1,0:T(8,128)(2,1)S(1)}, bf16[8,192,128]{2,1,0:T(8,128)(2,1)S(1)}, u32[]{:S(2)}, u32[]{:S(2)}) collective-permute-start(bf16[8,192,128]{2,1,0:T(8,128)(2,1)S(1)} %get-tuple-element.85), channel_id=1, source_target_pairs={{0,6},{1,3},{2,4},{3,1},{4,2},{5,7},{6,0},{7,5},{8,14},{9,11},{10,... | collective-permute-start | bytes 1179656 | tf_op jit(solution)/shard_map/ppermute | solution.py:52
  217.4 10.8 %collective-permute-start.33 = (bf16[8,192,128]{2,1,0:T(8,128)(2,1)S(1)}, bf16[8,192,128]{2,1,0:T(8,128)(2,1)S(1)}, u32[]{:S(2)}, u32[]{:S(2)}) collective-permute-start(bf16[8,192,128]{2,1,0:T(8,128)(2,1)S(1)} %get-tuple-element.87), channel_id=1, source_target_pairs={{0,96},{1,33},{2,98},{3,35},{4,100},{5,37},{6,102},{7,39},{8,104},... | collective-permute-start | bytes 1179656 | tf_op jit(solution)/shard_map/ppermute | solution.py:52
  220.1 2.4 copy-start.2
  225.8 5.7 %collective-permute-start.22 = (bf16[4,192,128]{2,1,0:T(8,128)(2,1)S(1)}, bf16[4,192,128]{2,1,0:T(8,128)(2,1)S(1)}, u32[]{:S(2)}, u32[]{:S(2)}) collective-permute-start(bf16[4,192,128]{2,1,0:T(8,128)(2,1)S(1)} %get-tuple-element.89), channel_id=1, source_target_pairs={{0,16},{1,25},{2,18},{3,27},{4,20},{5,29},{6,22},{7,31},{8,24},{9,... | collective-permute-start | bytes 589832 | tf_op jit(solution)/shard_map/ppermute | solution.py:52
  227.5 5.8 %collective-permute-start.28 = (bf16[4,192,128]{2,1,0:T(8,128)(2,1)S(1)}, bf16[4,192,128]{2,1,0:T(8,128)(2,1)S(1)}, u32[]{:S(2)}, u32[]{:S(2)}) collective-permute-start(bf16[4,192,128]{2,1,0:T(8,128)(2,1)S(1)} %get-tuple-element.91), channel_id=1, source_target_pairs={{0,2},{1,7},{2,0},{3,5},{4,6},{5,3},{6,4},{7,1},{8,10},{9,15},{10,... | collective-permute-start | bytes 589832 | tf_op jit(solution)/shard_map/ppermute | solution.py:52
  228.3 18.4 %copy-start.8 = (bf16[128,576]{0,1:T(8,128)(2,1)S(1)}, bf16[128,576]{0,1:T(8,128)(2,1)}, u32[]{:S(2)}) copy-start(bf16[128,576]{0,1:T(8,128)(2,1)} %param.4) | copy-start | bytes 442372
  228.3 8.2 %collective-permute-start.34 = (bf16[4,192,128]{2,1,0:T(8,128)(2,1)S(1)}, bf16[4,192,128]{2,1,0:T(8,128)(2,1)S(1)}, u32[]{:S(2)}, u32[]{:S(2)}) collective-permute-start(bf16[4,192,128]{2,1,0:T(8,128)(2,1)S(1)} %get-tuple-element.93), channel_id=1, source_target_pairs={{0,32},{1,97},{2,34},{3,99},{4,36},{5,101},{6,38},{7,103},{8,40},{... | collective-permute-start | bytes 589832 | tf_op jit(solution)/shard_map/ppermute | solution.py:52
  231.6 15.9 %copy-start.1 = (s32[2048]{0:T(1024)S(1)}, s32[2048]{0:T(1024)}, u32[]{:S(2)}) copy-start(s32[2048]{0:T(1024)} %param.7) | copy-start | bytes 24580
  231.7 6.9 %collective-permute-start.23 = (bf16[2,192,128]{2,1,0:T(8,128)(2,1)S(1)}, bf16[2,192,128]{2,1,0:T(8,128)(2,1)S(1)}, u32[]{:S(2)}, u32[]{:S(2)}) collective-permute-start(bf16[2,192,128]{2,1,0:T(8,128)(2,1)S(1)} %get-tuple-element.97), channel_id=1, source_target_pairs={{0,96},{1,33},{2,98},{3,35},{4,100},{5,37},{6,102},{7,39},{8,104},... | collective-permute-start | bytes 294920 | tf_op jit(solution)/shard_map/ppermute | solution.py:52
  233.4 6.3 %collective-permute-start.29 = (bf16[2,192,128]{2,1,0:T(8,128)(2,1)S(1)}, bf16[2,192,128]{2,1,0:T(8,128)(2,1)S(1)}, u32[]{:S(2)}, u32[]{:S(2)}) collective-permute-start(bf16[2,192,128]{2,1,0:T(8,128)(2,1)S(1)} %get-tuple-element.99), channel_id=1, source_target_pairs={{0,24},{1,17},{2,26},{3,19},{4,28},{5,21},{6,30},{7,23},{8,16},{9,... | collective-permute-start | bytes 294920 | tf_op jit(solution)/shard_map/ppermute | solution.py:52
  236.6 5.9 %collective-permute-start.35 = (bf16[2,192,128]{2,1,0:T(8,128)(2,1)S(1)}, bf16[2,192,128]{2,1,0:T(8,128)(2,1)S(1)}, u32[]{:S(2)}, u32[]{:S(2)}) collective-permute-start(bf16[2,192,128]{2,1,0:T(8,128)(2,1)S(1)} %get-tuple-element.101), channel_id=1, source_target_pairs={{0,6},{1,3},{2,4},{3,1},{4,2},{5,7},{6,0},{7,5},{8,14},{9,11},{10,... | collective-permute-start | bytes 294920 | tf_op jit(solution)/shard_map/ppermute | solution.py:52
  238.6 4.2 %collective-permute-start.24 = (bf16[1,192,128]{2,1,0:T(8,128)(2,1)S(1)}, bf16[1,192,128]{2,1,0:T(8,128)(2,1)S(1)}, u32[]{:S(2)}, u32[]{:S(2)}) collective-permute-start(bf16[1,192,128]{2,1,0:T(8,128)(2,1)S(1)} %add_convert_fusion.30), channel_id=1, source_target_pairs={{0,32},{1,97},{2,34},{3,99},{4,36},{5,101},{6,38},{7,103},{8,40},{... | collective-permute-start | bytes 147464 | tf_op jit(solution)/shard_map/ppermute | solution.py:52
  239.6 4.2 %collective-permute-start.30 = (bf16[1,192,128]{2,1,0:T(8,128)(2,1)S(1)}, bf16[1,192,128]{2,1,0:T(8,128)(2,1)S(1)}, u32[]{:S(2)}, u32[]{:S(2)}) collective-permute-start(bf16[1,192,128]{2,1,0:T(8,128)(2,1)S(1)} %add_convert_fusion.28), channel_id=1, source_target_pairs={{0,16},{1,25},{2,18},{3,27},{4,20},{5,29},{6,22},{7,31},{8,24},{9,... | collective-permute-start | bytes 147464 | tf_op jit(solution)/shard_map/ppermute | solution.py:52
  242.5 4.2 %collective-permute-start.36 = (bf16[1,192,128]{2,1,0:T(8,128)(2,1)S(1)}, bf16[1,192,128]{2,1,0:T(8,128)(2,1)S(1)}, u32[]{:S(2)}, u32[]{:S(2)}) collective-permute-start(bf16[1,192,128]{2,1,0:T(8,128)(2,1)S(1)} %add_convert_fusion.26), channel_id=1, source_target_pairs={{0,2},{1,7},{2,0},{3,5},{4,6},{5,3},{6,4},{7,1},{8,10},{9,15},{10,... | collective-permute-start | bytes 147464 | tf_op jit(solution)/shard_map/ppermute | solution.py:52
where the time goes:
time: 248 us
  Pallas kernels  84.1 us (34%)
  starting transfers between devices  80.8 us (33%)
  waiting for transfers between devices  42.6 us (17%)
  local copies, waits for them, and re-layouts  20.1 us (8%)
  other arithmetic  18.9 us (8%)
    ppermute x40, starting transfers between devices, send(): return lax.ppermute(a, AX, pairs)  65.5 us
    ppermute x40, waiting for transfers between devices, send(): return lax.ppermute(a, AX, pairs)  42.3 us
    pallas_call x2, Pallas kernels, head_call(): pl.pallas_call(head_kernel, grid=(tiles,), in_specs=[pl.BlockSpec((4, 2 *...  20.1 us
    pallas_call x1, Pallas kernels, act_call(): pl.pallas_call(act_kernel, grid_spec=pltpu.PrefetchScalarGridSpec(num_sca...  19.7 us
    pallas_call x1, Pallas kernels, grad_call(): pl.pallas_call(grad_kernel, in_specs=[SMEM_SPEC] + [VMEM_SPEC] * 8, out_s...  15.5 us
    pallas_call x1, Pallas kernels, keep_call(): pl.pallas_call(keep_kernel, in_specs=[SMEM_SPEC] + [VMEM_SPEC] * 5, out_s...  11.6 us
    convert_element_type x17, other arithmetic, add(): return (a.astype(F32) + b.astype(F32)).astype(a.dtype)  10.7 us
    all_to_all x1, starting transfers between devices, shards(): lax.all_to_all(jnp.broadcast_to(total[None], (64, 8, TB)), AX[:4], 0, 0)  10.7 us
  transfers between devices with their start and end apart: 42, of which 20 were waited for; matrix products, arithmetic and copies ran while one was open for 13% of the time, Pallas kernels for 20%

commit v1 on v0

v1 whole, which is shorter than its diff:
```python
import functools
import itertools

import jax
import jax.numpy as jnp
import numpy as np
from jax import lax
from jax.experimental import pallas as pl
from jax.experimental.pallas import tpu as pltpu
from jax.sharding import Mesh, PartitionSpec as P

AX = ("x", "ylo", "yhi", "z", "core")
D = 4608
FB = 576
PT = 192
SQ = 16
TB = 128
VB = 512
CAP = 30.0
EPS = 1e-06
VMEM = 60 * 1024 * 1024
BF = jnp.bfloat16
F32 = jnp.float32

ORDER = ((0, 1, 2), (1, 2, 0), (2, 0, 1))


def coords(i):
    core, z, yhi, ylo, x = i % 2, i // 2 % 4, i // 8 % 2, i // 16 % 2, i // 32
    return [x, yhi * 2 + ylo, z], core


def number(c, core):
    return (((c[0] * 2 + c[1] % 2) * 2 + c[1] // 2) * 4 + c[2]) * 2 + core


def from_bits(core, late, early):
    gray = late * 2 + early if core == 0 else early * 2 + late
    return gray ^ (gray >> 1)


BITS = list(itertools.product((0, 1), repeat=3))
CUBES = [
    [number([from_bits(core, b, e) for b, e in zip(late, early)], core) for early in BITS]
    for core in (0, 1)
    for late in BITS
]
TWIN = [(i, i ^ 1) for i in range(128)]


@functools.cache
def across(dim):
    pairs = []
    for i in range(128):
        c, core = coords(i)
        gray = (c[dim] ^ (c[dim] >> 1)) ^ (2 if core == 0 else 1)
        c[dim] = gray ^ (gray >> 1)
        pairs.append((i, number(c, core)))
    return pairs


def send(a, pairs):
    return lax.ppermute(a, AX, pairs)


def in_cube(a):
    return lax.all_to_all(a, AX, 0, 0, axis_index_groups=CUBES)


def gather(block):
    cube = in_cube(jnp.broadcast_to(block[None], (8,) + block.shape))
    cuts = (0, PT + SQ, 2 * PT + SQ, 3 * PT + SQ)
    held = [cube[:, cuts[p] : cuts[p + 1]] for p in range(3)]
    for phase in range(2):
        got = [send(held[p], across(ORDER[p][phase])) for p in range(3)]
        held = [jnp.concatenate([held[p], got[p]]) for p in range(3)]
    got = [send(held[p], across(ORDER[p][2])) for p in range(3)]
    return [a for p in range(3) for a in (held[p], got[p])]


def block_at(part, places):
    late = [place >> 1 for place in places]
    early = [place & 1 for place in places]
    first, second, _ = ORDER[part]
    return (late[second] * 2 + late[first]) * 8 + early[0] * 4 + early[1] * 2 + early[2]


def total(arrays):
    return functools.reduce(lambda a, b: a + b, [a.astype(F32) for a in arrays])


def split3(v):
    hi = lax.reduce_precision(v, 8, 7)
    mid = lax.reduce_precision(v - hi, 8, 7)
    lo = v - hi - mid
    return [hi.astype(BF), mid.astype(BF), lo.astype(BF)]


def add(a, b):
    return (a.astype(F32) + b.astype(F32)).astype(a.dtype)


def table(x, y, z, core, shard):
    out = []
    place = jnp.arange(4, dtype=jnp.int32)

    def swap(bits):
        return jnp.where(core == 0, bits, (bits & 1) * 2 + (bits >> 1))

    mine = [swap(c ^ (c >> 1)) & 2 for c in (x, y, z)]
    for late in mine:
        gray = swap(place ^ late)
        out.append(gray ^ (gray >> 1))
    for late in mine:
        out.append(swap(place ^ (place >> 1)) ^ late)
    out.append(jnp.stack([shard * VB, (shard ^ 1) * VB]))
    return jnp.concatenate(out).astype(jnp.int32)


def at_of(tab, dim, place):
    return tab[4 * dim + place]


def place_of(tab, dim, at):
    return tab[12 + 4 * dim + at]


def flip_kernel(own_ref, other_ref, a_ref, b_ref, c_ref):
    for h, ref in enumerate((own_ref, other_ref)):
        turned = ref[...].T
        cols = pl.ds(h * VB, VB)
        for ylo in range(2):
            at = ylo * FB
            a_ref[0, ylo, :, cols] = turned[at : at + PT]
            b_ref[0, ylo, :, cols] = turned[at + PT : at + 2 * PT]
            c_ref[ylo, 0, :, cols] = turned[at + 2 * PT : at + 3 * PT]


def flip(own, other):
    block = pl.BlockSpec((VB, 2 * FB), lambda x: (0, x))
    return pl.pallas_call(
        flip_kernel,
        grid=(4,),
        in_specs=[block, block],
        out_specs=[
            pl.BlockSpec((1, 2, PT, 2 * VB), lambda x: (x, 0, 0, 0)),
            pl.BlockSpec((1, 2, PT, 2 * VB), lambda x: (x, 0, 0, 0)),
            pl.BlockSpec((2, 1, PT, 2 * VB), lambda x: (0, x, 0, 0)),
        ],
        out_shape=[
            jax.ShapeDtypeStruct((4, 2, PT, 2 * VB), BF),
            jax.ShapeDtypeStruct((4, 2, PT, 2 * VB), BF),
            jax.ShapeDtypeStruct((2, 4, PT, 2 * VB), BF),
        ],
        compiler_params=pltpu.CompilerParams(vmem_limit_bytes=VMEM),
        cost_estimate=pl.CostEstimate(
            flops=0, bytes_accessed=4 * VB * D * 2, transcendentals=0
        ),
        name="flip",
    )(own, other)


def act_kernel(tab, *refs):
    halves = [refs[2 * p : 2 * p + 2] for p in range(3)]
    own_ref, other_ref, tgt_ref = refs[6:9]
    expo_ref, bend_ref, rinv_ref, stat_ref, xt_out = refs[9:14]
    xt, squares, weights, acc, totals, stats, sems, out_sems, w_sems = refs[14:]
    step = pl.program_id(0)

    def fetch(src, tile, x, y, part):
        row = (x * 2 + (y & 1)) * FB + part * PT
        lanes = pl.ds(pl.multiple_of((y >> 1) * TB, TB), TB)
        pltpu.make_async_copy(
            src.at[pl.ds(0, PT)],
            xt.at[tile, pl.ds(pl.multiple_of(row, 16), PT), lanes],
            sems.at[tile],
        ).start()
        if part == 0:
            row = (x * 2 + (y & 1)) * SQ
            pltpu.make_async_copy(
                src.at[pl.ds(PT, SQ)],
                squares.at[tile, pl.ds(pl.multiple_of(row, 16), SQ), lanes],
                sems.at[tile],
            ).start()

    def issue(tile):
        for px in range(4):
            for py in range(4):
                x, y = at_of(tab, 0, px), at_of(tab, 1, py)
                places = (px, py, tile)
                fetch(halves[1][px >> 1].at[block_at(1, places)], tile, x, y, 1)
                fetch(halves[2][py >> 1].at[block_at(2, places)], tile, x, y, 2)
        for half in range(2):
            @pl.when((tile >> 1) == half)
            def _():
                for px in range(4):
                    for py in range(4):
                        fetch(
                            halves[0][half].at[block_at(0, (px, py, tile))],
                            tile, at_of(tab, 0, px), at_of(tab, 1, py), 0,
                        )

    def load(h, ref):
        return pltpu.make_async_copy(ref, weights.at[pl.ds(h * VB, VB)], w_sems.at[h])

    def arrived():
        pltpu.make_async_copy(xt.at[step], xt.at[step], sems.at[step]).wait()
        pltpu.make_async_copy(squares.at[step], squares.at[step], sems.at[step]).wait()
        pltpu.make_async_copy(xt.at[step], xt_out.at[step], out_sems.at[step]).start()

    @pl.when(step == 0)
    def _():
        issue(step)
        for h, ref in enumerate((own_ref, other_ref)):
            load(h, ref).start()
        issue(step + 1)
        arrived()
        for h, ref in enumerate((own_ref, other_ref)):
            load(h, ref).wait()
            rows = pl.ds(h * VB, VB)
            acc[rows, :] = jnp.dot(weights[rows, :], xt[step], preferred_element_type=F32)

    @pl.when(step > 0)
    def _():
        @pl.when(step < 3)
        def _():
            issue(step + 1)

        arrived()
        acc[...] = jnp.dot(weights[...], xt[step], preferred_element_type=F32)

    mean = jnp.sum(squares[step].astype(F32), axis=0, keepdims=True) / D
    rinv = lax.rsqrt(mean + EPS)
    z = at_of(tab, 2, step)
    rinv_ref[z] = rinv
    tgt = tgt_ref[z]
    rows = 32
    zeros = jnp.zeros((8, 2 * TB), F32)
    sums = (zeros,) * 3
    inside = jnp.zeros((1, 2 * TB), jnp.bool_)

    def fold(v):
        return jnp.sum(v.reshape(rows // 8, 8, 2 * TB), axis=0)

    for h in range(2):
        row0 = lax.broadcasted_iota(jnp.int32, (rows, 2 * TB), 0) + tab[24 + h]
        inside = inside | ((tgt >= tab[24 + h]) & (tgt < tab[24 + h] + VB))

        def chunk(i, sums, h=h, row0=row0):
            total, slope, act_at = sums
            at = pl.multiple_of(i * rows, rows)
            here = pl.ds(h * VB + at, rows)
            act = acc[here, :] * rinv
            t = jnp.tanh(act * (1.0 / CAP))
            expo = jnp.exp(t * CAP)
            sharp = expo * (1.0 - t * t)
            expo_ref[0, here, :] = sharp
            return (
                total + fold(expo),
                slope + fold(sharp * act),
                act_at + fold(jnp.where(row0 + at == tgt, act, 0.0)),
            )

        sums = lax.fori_loop(0, VB // rows, chunk, sums)
    total, slope, act_at = [jnp.sum(s, axis=0, keepdims=True) for s in sums]
    t = jnp.tanh(act_at * (1.0 / CAP))
    bend = jnp.where(inside, 1.0 - t * t, 0.0)
    bend_ref[0] = bend
    sums = (total, t * CAP, slope, bend * act_at)
    for yhi in range(2):
        lanes = slice(yhi * TB, (yhi + 1) * TB)
        totals[pl.ds(z * 2 + yhi, 1), :] = sums[0][:, lanes]
        stats[yhi * 4 + z] = jnp.concatenate(
            [s[:, lanes] for s in sums[1:4]] + [jnp.zeros((5, TB), F32)], axis=0
        )

    @pl.when(step == 3)
    def _():
        for chip in range(64):
            stat_ref[chip, 0:8, :] = totals[...]
            stat_ref[chip, 8:16, :] = stats[chip % 8]
        for tile in range(4):
            pltpu.make_async_copy(xt.at[tile], xt_out.at[tile], out_sems.at[tile]).wait()


ANYWHERE = pl.BlockSpec(memory_space=pl.ANY)
SMEM_SPEC = pl.BlockSpec(memory_space=pltpu.SMEM)
VMEM_SPEC = pl.BlockSpec(memory_space=pltpu.VMEM)


def act_call(tab, halves, own, other, tgt):
    tile = pl.BlockSpec((1, 2 * VB, 2 * TB), lambda z, w: (z, 0, 0))
    rows = pl.BlockSpec((4, 1, 2 * TB), lambda z, w: (0, 0, 0))
    return pl.pallas_call(
        act_kernel,
        grid_spec=pltpu.PrefetchScalarGridSpec(
            num_scalar_prefetch=1,
            grid=(4,),
            in_specs=[ANYWHERE] * 8 + [rows],
            out_specs=[
                tile,
                pl.BlockSpec((1, 1, 2 * TB), lambda z, w: (z, 0, 0)),
                rows,
                pl.BlockSpec((64, 16, TB), lambda z, w: (0, 0, 0)),
                ANYWHERE,
            ],
            scratch_shapes=[
                pltpu.VMEM((4, D, 2 * TB), BF),
                pltpu.VMEM((4, 8 * SQ, 2 * TB), BF),
                pltpu.VMEM((2 * VB, D), BF),
                pltpu.VMEM((2 * VB, 2 * TB), F32),
                pltpu.VMEM((8, TB), F32),
                pltpu.VMEM((8, 8, TB), F32),
                pltpu.SemaphoreType.DMA((4,)),
                pltpu.SemaphoreType.DMA((4,)),
                pltpu.SemaphoreType.DMA((2,)),
            ],
        ),
        out_shape=[
            jax.ShapeDtypeStruct((4, 2 * VB, 2 * TB), F32),
            jax.ShapeDtypeStruct((4, 1, 2 * TB), F32),
            jax.ShapeDtypeStruct((4, 1, 2 * TB), F32),
            jax.ShapeDtypeStruct((64, 16, TB), F32),
            jax.ShapeDtypeStruct((4, D, 2 * TB), BF),
        ],
        compiler_params=pltpu.CompilerParams(vmem_limit_bytes=VMEM),
        cost_estimate=pl.CostEstimate(
            flops=2 * 1024 * 1024 * D, bytes_accessed=30_000_000, transcendentals=2 << 20
        ),
        name="act",
    )(tab, *halves, own, other, tgt)


def pieces(tab, lead, gz, gy, weights, outs, ready, done):
    w0, w1, w2 = weights
    out0, out1, out2 = outs
    ready(0)
    w = w0[...].reshape(8 * PT, 2 * VB)
    both = jnp.concatenate([gz[lead * 2], gz[lead * 2 + 1]], axis=1)
    got = jnp.dot(w, both, preferred_element_type=F32).astype(BF)
    for low in range(2):
        for x in range(4):
            for ylo in range(2):
                for yhi in range(2):
                    places = (place_of(tab, 0, x), place_of(tab, 1, yhi * 2 + ylo), lead * 2 + low)
                    row, lane = (x * 2 + ylo) * PT, (low * 2 + yhi) * TB
                    out0[block_at(0, places)] = got[row : row + PT, lane : lane + TB]
    done(0)
    ready(1)
    for low in range(2):
        place = lead * 2 + low
        x = at_of(tab, 0, place)
        w = w1[x].reshape(2 * PT, 2 * VB)
        tokens = jnp.concatenate([gz[z] for z in range(4)], axis=1)
        got = jnp.dot(w, tokens, preferred_element_type=F32).astype(BF)
        for z in range(4):
            for ylo in range(2):
                for yhi in range(2):
                    places = (place, place_of(tab, 1, yhi * 2 + ylo), z)
                    row, lane = ylo * PT, (z * 2 + yhi) * TB
                    out1[block_at(1, places)] = got[row : row + PT, lane : lane + TB]
    done(1)
    ready(2)
    for low in range(2):
        place = lead * 2 + low
        y = at_of(tab, 1, place)
        w = w2[y & 1].reshape(4 * PT, 2 * VB)
        tokens = jnp.concatenate([gy[y >> 1, pair] for pair in range(2)], axis=1)
        got = jnp.dot(w, tokens, preferred_element_type=F32).astype(BF)
        for x in range(4):
            for z in range(4):
                places = (place_of(tab, 0, x), place, z)
                out2[block_at(2, places)] = got[x * PT : (x + 1) * PT, z * TB : (z + 1) * TB]
    done(2)


def copies(pairs, sems):
    return [
        pltpu.make_async_copy(src, dst, sems.at[i]) for i, (src, dst) in enumerate(pairs)
    ]


def grad_kernel(tab, expo_ref, bend_ref, totals_ref, rinv_ref, tgt_ref, *refs):
    w_refs, out_refs = refs[:3], refs[3:9]
    expo, w0, w1, w2, gz, gr, gy, away0, away1, away2, in_sems, out_sems = refs[9:]
    weights, away = (w0, w1, w2), (away0, away1, away2)
    tiles = [(expo_ref.at[i], expo.at[i]) for i in range(4)]
    incoming = copies(tiles + list(zip(w_refs, weights)), in_sems)
    outgoing = copies(list(zip((gz, gr, gy) + away, out_refs)), out_sems)
    for copy in incoming:
        copy.start()
    rows = 32
    inv = 1.0 / jnp.sum(totals_ref[...], axis=0)[0:8]
    line = lax.broadcasted_iota(jnp.int32, (8, TB), 0)

    def chunk(i, carry, place, h, inv_z, rinv, bend, tgt, row0):
        at = pl.multiple_of(i * rows, rows)
        here = pl.ds(h * VB + at, rows)
        g = expo[place, here, :] * inv_z - jnp.where(row0 + at == tgt, bend, 0.0)
        gr[place, here, :] = (g * rinv).astype(BF)
        g = g.astype(BF)
        gz[place, here, :] = g
        for yhi in range(2):
            gy[yhi, place // 2, here, pl.ds(place % 2 * TB, TB)] = g[:, yhi * TB : (yhi + 1) * TB]
        return carry

    for place in range(4):
        z = at_of(tab, 2, place)
        inv_z = jnp.concatenate(
            [
                jnp.sum(jnp.where(line == z * 2 + yhi, inv, 0.0), axis=0, keepdims=True)
                for yhi in range(2)
            ],
            axis=1,
        )
        incoming[place].wait()
        for h in range(2):
            row0 = lax.broadcasted_iota(jnp.int32, (rows, 2 * TB), 0) + tab[24 + h]
            lax.fori_loop(
                0,
                VB // rows,
                functools.partial(
                    chunk, place=place, h=h, inv_z=inv_z, rinv=rinv_ref[z],
                    bend=bend_ref[place], tgt=tgt_ref[z], row0=row0,
                ),
                0,
            )
    for copy in outgoing[:3]:
        copy.start()
    pieces(
        tab, 1, gz, gy, weights, away,
        lambda p: incoming[4 + p].wait(), lambda p: outgoing[3 + p].start(),
    )
    for copy in outgoing:
        copy.wait()


def keep_kernel(tab, gz_ref, gy_ref, *refs):
    w_refs, out_refs = refs[:3], refs[3:6]
    gz, w0, w1, gy, w2, kept0, kept1, kept2, in_sems, out_sems = refs[6:]
    kept = (kept0, kept1, kept2)
    incoming = copies(
        [(gz_ref, gz), (w_refs[0], w0), (w_refs[1], w1), (gy_ref, gy), (w_refs[2], w2)], in_sems
    )
    outgoing = copies(list(zip(kept, out_refs)), out_sems)
    for copy in incoming:
        copy.start()

    def ready(p):
        for copy in ((0, 1), (2,), (3, 4))[p]:
            incoming[copy].wait()

    pieces(tab, 0, gz, gy, (w0, w1, w2), kept, ready, lambda p: outgoing[p].start())
    for copy in outgoing:
        copy.wait()


HALF = (32, PT, TB)
GZ = (4, 2 * VB, 2 * TB)
GY = (2, 2, 2 * VB, 2 * TB)
W_SHAPES = ((4, 2, PT, 2 * VB), (4, 2, PT, 2 * VB), (2, 4, PT, 2 * VB))


def bf16_out(*shapes):
    return [jax.ShapeDtypeStruct(shape, BF) for shape in shapes]


def bf16_vmem(*shapes):
    return [pltpu.VMEM(shape, BF) for shape in shapes]


def grad_call(tab, expo, bend, totals, rinv, tgt, turned):
    return pl.pallas_call(
        grad_kernel,
        in_specs=[SMEM_SPEC, ANYWHERE] + [VMEM_SPEC] * 4 + [ANYWHERE] * 3,
        out_specs=[ANYWHERE] * 6,
        out_shape=bf16_out(GZ, GZ, GY, HALF, HALF, HALF),
        scratch_shapes=[pltpu.VMEM(GZ, F32)]
        + bf16_vmem(*W_SHAPES, GZ, GZ, GY, HALF, HALF, HALF)
        + [pltpu.SemaphoreType.DMA((7,)), pltpu.SemaphoreType.DMA((6,))],
        compiler_params=pltpu.CompilerParams(vmem_limit_bytes=VMEM),
        cost_estimate=pl.CostEstimate(
            flops=1024 * 1024 * D, bytes_accessed=24_000_000, transcendentals=0
        ),
        name="grad",
    )(tab, expo, bend, totals, rinv, tgt, *turned)


def keep_call(tab, gz, gy, turned):
    return pl.pallas_call(
        keep_kernel,
        in_specs=[SMEM_SPEC] + [ANYWHERE] * 5,
        out_specs=[ANYWHERE] * 3,
        out_shape=bf16_out(HALF, HALF, HALF),
        scratch_shapes=bf16_vmem(
            GZ, W_SHAPES[0], W_SHAPES[1], GY, W_SHAPES[2], HALF, HALF, HALF
        )
        + [pltpu.SemaphoreType.DMA((5,)), pltpu.SemaphoreType.DMA((3,))],
        compiler_params=pltpu.CompilerParams(vmem_limit_bytes=VMEM),
        cost_estimate=pl.CostEstimate(
            flops=1024 * D, bytes_accessed=1_000_000, transcendentals=0
        ),
        name="keep",
    )(tab, gz, gy, *turned)


def head_kernel(gr, xt, own_w, other_w, own_ref, other_ref, gain_ref):
    got = lax.dot_general(
        jnp.concatenate([gr[z] for z in range(4)], axis=1),
        jnp.concatenate([xt[z] for z in range(4)], axis=1),
        (((1,), (1,)), ((), ())), preferred_element_type=F32,
    )
    own_ref[...] = got[:VB].astype(BF)
    other_ref[...] = got[VB:].astype(BF)
    gain_ref[...] = jnp.sum(
        got[:VB] * own_w[...].astype(F32) + got[VB:] * other_w[...].astype(F32),
        axis=0, keepdims=True,
    )


def head_call(gr, xt, own, other):
    tile = 768
    cols = pl.BlockSpec((VB, tile), lambda f: (0, f))
    return pl.pallas_call(
        head_kernel,
        grid=(D // tile,),
        in_specs=[
            pl.BlockSpec((4, 2 * VB, 2 * TB), lambda f: (0, 0, 0), pipeline_mode=pl.Buffered(1)),
            pl.BlockSpec((4, tile, 2 * TB), lambda f: (0, f, 0)),
            cols,
            cols,
        ],
        out_specs=[cols, cols, pl.BlockSpec((1, tile), lambda f: (0, f))],
        out_shape=bf16_out((VB, D), (VB, D)) + [jax.ShapeDtypeStruct((1, D), F32)],
        compiler_params=pltpu.CompilerParams(vmem_limit_bytes=VMEM),
        cost_estimate=pl.CostEstimate(
            flops=1024 * D, bytes_accessed=1_000_000, transcendentals=0
        ),
        name="head",
    )(gr, xt, own, other)


def last_kernel(*refs):
    out_ref = refs[-1]
    gain_ref = refs[-2]
    for p in range(3):
        here = refs[4 * p : 4 * p + 4]
        out_ref[:, p * PT : (p + 1) * PT, :] = total([a[...] for a in here]).astype(BF)
    out_ref[:, FB : FB + SQ, :] = gain_ref[...]


def last_call(here, gains):
    count = 2
    block = pl.BlockSpec((count, PT, TB), lambda i: (i, 0, 0))
    return pl.pallas_call(
        last_kernel,
        grid=(8 // count,),
        in_specs=[block] * 12 + [pl.BlockSpec((count, SQ, TB), lambda i: (i, 0, 0))],
        out_specs=pl.BlockSpec((count, FB + SQ, TB), lambda i: (i, 0, 0)),
        out_shape=jax.ShapeDtypeStruct((8, FB + SQ, TB), BF),
        compiler_params=pltpu.CompilerParams(vmem_limit_bytes=VMEM),
        cost_estimate=pl.CostEstimate(flops=4 << 20, bytes_accessed=6_000_000, transcendentals=0),
        name="last",
    )(*[a for part in here for a in part], gains)


def shards(section_output, norm_gain, head_weight, targets):
    x, ylo, yhi, z, core = (lax.axis_index(a) for a in AX)
    y = yhi * 2 + ylo
    shard = (((x * 2 + ylo) * 2 + yhi) * 4 + z) * 2 + core
    tab = table(x, y, z, core, shard)

    xt = section_output.T.astype(F32)
    gain = norm_gain.astype(F32)[:, None]
    scaled_x = (xt * gain).astype(BF)
    squares = jnp.sum(xt * xt, axis=0, keepdims=True)
    extra = jnp.concatenate(
        split3(squares) + [jnp.zeros((SQ - 3, TB), BF)], axis=0
    )
    block = jnp.concatenate([scaled_x[:PT], extra, scaled_x[PT:]], axis=0)
    other = send(head_weight, TWIN)
    turned = flip(head_weight, other)

    tgt = lax.dynamic_index_in_dim(
        targets.reshape(2, 4, 2, TB), core, axis=2, keepdims=False
    ).transpose(1, 0, 2).reshape(4, 1, 2 * TB)
    halves = gather(block)
    halves, turned, tgt, tab = lax.optimization_barrier((halves, turned, tgt, tab))

    expo, bend, rinv, stats, xt_all = act_call(tab, halves, head_weight, other, tgt)
    stats = lax.all_to_all(stats, AX[:4], 0, 0)

    gz, gr, gy, *away = grad_call(tab, expo, bend, stats, rinv, tgt, turned)

    bound = lax.optimization_barrier
    got = [send(away[p], across(ORDER[p][2])) for p in range(3)]
    own_part, other_part, gains = head_call(gr, xt_all, head_weight, other)
    gains, gz, gy = bound((gains, gz, gy))
    kept = keep_call(tab, gz, gy, turned)
    gains = gains.reshape(D // TB, TB)
    gains = gains + send(gains, TWIN)
    gains = gains + send(gains, across(2))
    got, kept, gains, own_part, other_part = bound((got, kept, gains, own_part, other_part))
    here = [[kept[p], got[p]] for p in range(3)]
    for phase, half in ((1, 16), (0, 8)):
        away = [total([a[half:2 * half] for a in here[p]]).astype(BF) for p in range(3)]
        away, gains, other_part = bound((away, gains, other_part))
        got = [send(away[p], across(ORDER[p][phase])) for p in range(3)]
        more = send(gains, across(phase))
        if phase == 1:
            other_part = send(other_part, TWIN)
        got, more, other_part = bound((got, more, other_part))
        gains = gains + more
        here = [here[p] + [got[p]] for p in range(3)]

    owner = jnp.stack([tab[ex] * 2 + (tab[4 + ey] & 1) for ex, ey, _ in BITS])
    chosen = owner[:, None, None] == jnp.arange(8, dtype=jnp.int32)[None, :, None]
    gains = jnp.sum(jnp.where(chosen, gains.reshape(1, 8, FB), 0.0), axis=1)
    gains = jnp.concatenate([gains, jnp.zeros((8, 5 * TB - FB), F32)], axis=1)
    gains = jnp.stack(split3(gains) + [jnp.zeros((8, 5 * TB), BF)], axis=1)
    gains = gains.reshape(8, 20, TB)[:, :SQ]

    blocks, own_part, other_part = bound((last_call(here, gains), own_part, other_part))
    blocks, head_grad = bound((in_cube(blocks), add(own_part, other_part)))
    blocks = jnp.sum(blocks.astype(F32), axis=0)
    grad_hidden = blocks[:FB]
    gains = jnp.sum(blocks[FB : FB + 15].reshape(3, 5 * TB), axis=0)[:FB]
    gain_grad = gains / norm_gain.astype(F32)

    row = jnp.sum(stats, axis=0)
    picked, slope, slope_at = row[8:9], row[9:10], row[10:11]
    sum_exp = lax.dynamic_slice(row, (z * 2 + yhi, 0), (1, TB))
    rinv = lax.dynamic_slice(rinv, (z, 0, yhi * TB), (1, 1, TB)).reshape(1, TB)
    token_loss = (jnp.log(sum_exp) - picked).reshape(TB)
    inner = slope / sum_exp - slope_at
    grad_input = (rinv * (grad_hidden * gain) - xt * (rinv * rinv * inner / D)).astype(BF).T
    return (token_loss, grad_input, head_grad, gain_grad)


def solution(mesh):
    fine = Mesh(mesh.devices.reshape(4, 2, 2, 4, 2), AX)
    pipe, dp = ("x", "ylo"), ("yhi", "z", "core")
    return jax.shard_map(
        shards,
        mesh=fine,
        in_specs=(P(dp, pipe), P(pipe), P(pipe + dp, None), P()),
        out_specs=(P(dp), P(dp, pipe), P(pipe + dp, None), P(pipe)),
        check_vma=False,
    )
```

time: 248 us -> 224 us (0.903)
  starting transfers between devices: 80.8 us -> 41.8 us
  blocking collectives: 0 us -> 35.4 us
  local copies, waits for them, and re-layouts: 20.1 us -> 5.05 us
  Pallas kernels: 84.1 us -> 75.5 us
  other arithmetic: 18.9 us -> 26.6 us
  waiting for transfers between devices: 42.6 us -> 35.6 us
  between operations: 1.02 us -> 3.58 us
    all_to_all x0 -> x2, blocking collectives: none -> 35.4 us  [the longest x1 18.5 us: shards(): stats = lax.all_to_all(stats, AX[:4], 0, 0)]
    ppermute x40 -> x24, starting transfers between devices: 65.5 us -> 38.2 us  [send(): return lax.ppermute(a, AX, pairs)]
    pallas_call x5 -> x4, Pallas kernels: 55.7 us -> 42.3 us  [the longest x1 16 us: head_call(): pl.pallas_call(head_kernel, grid=(D // tile,), in_specs=[pl.BlockSpec((4,...]
    all_to_all x2 -> x1, starting transfers between devices: 15.3 us -> 3.57 us  [in_cube(): return lax.all_to_all(a, AX, 0, 0, axis_index_groups=CUBES)]
    convert_element_type x0 -> x6, other arithmetic: none -> 11.4 us  [shards(): total([a[half:2 * half] for a in here[p]]).astype(BF)]
    ppermute x40 -> x24, waiting for transfers between devices: 42.3 us -> 31.7 us  [send(): return lax.ppermute(a, AX, pairs)]
    unnamed x37 -> x34, local copies, waits for them, and re-layouts: 9.39 us -> 0.67 us
    concatenate x7 -> x1, local copies, waits for them, and re-layouts: 5.74 us -> 0.16 us  [shards(): block = jnp.concatenate([scaled_x[:PT], extra, scaled_x[PT:]], axis=0)]
  transfers between devices with their start and end apart: 42 -> 25, of which waited for: 20 -> 13; matrix products, arithmetic and copies ran while one was open for 13% -> 7% of each run, Pallas kernels for 20% -> 15%
where the time goes in v1:
time: 224 us; the launch traced here: 223 us
  Pallas kernels  75.5 us (34%)
  starting transfers between devices  41.8 us (19%)
  waiting for transfers between devices  35.6 us (16%)
  blocking collectives  35.4 us (16%)
  other arithmetic  26.6 us (12%)
  local copies, waits for them, and re-layouts  5.05 us (2%)
  between operations  3.58 us (2%)
    ppermute x24, starting transfers between devices, send(): return lax.ppermute(a, AX, pairs)  38.2 us
    ppermute x24, waiting for transfers between devices, send(): return lax.ppermute(a, AX, pairs)  31.7 us
    pallas_call x1, Pallas kernels, act_call(): pl.pallas_call(act_kernel, grid_spec=pltpu.PrefetchScalarGridSpec(num_sca...  24.6 us
    all_to_all x1, blocking collectives, shards(): stats = lax.all_to_all(stats, AX[:4], 0, 0)  18.5 us
    all_to_all x1, blocking collectives, in_cube(): return lax.all_to_all(a, AX, 0, 0, axis_index_groups=CUBES)  16.9 us
    pallas_call x1, Pallas kernels, head_call(): pl.pallas_call(head_kernel, grid=(D // tile,), in_specs=[pl.BlockSpec((4,...  16 us
    pallas_call x1, Pallas kernels, grad_call(): pl.pallas_call(grad_kernel, in_specs=[SMEM_SPEC, ANYWHERE] + [VMEM_SPEC]...  11.8 us
    convert_element_type x6, other arithmetic, shards(): total([a[half:2 * half] for a in here[p]]).astype(BF)  11.4 us
  transfers between devices with their start and end apart: 25, of which 13 were waited for; matrix products, arithmetic and copies ran while one was open for 7% of the time, Pallas kernels for 15%

profile of v1, /device:TPU:0, one launch (start us, length us, event | category | flops | bytes accessed | tf_op | source)
XLA Modules:
  0.0 223.5 jit_solution(16872685979164839178)
XLA Ops:
  0.7 0.7 convert_element_type.135
  1.4 1.1 fusion.1
  2.9 16.9 %all_to_all.15 = bf16[8,592,128]{2,1,0:T(8,128)(2,1)S(1)} all-to-all(bf16[8,592,128]{2,1,0:T(8,128)(2,1)S(1)} %broadcast_in_dim.37), channel_id=1, replica_groups={{0,2,16,18,32,34,48,50},{6,4,22,20,38,36,54,52},{24,26,8,10,56,58,40,42..., dimensions={0} | all-to-all | bytes 2424832 | tf_op jit(solution)/shard_map/all_to_all | solution.py:67
  19.8 2.3 %collective-permute-start.3 = (bf16[8,192,128]{2,1,0:T(8,128)(2,1)S(1)}, bf16[8,192,128]{2,1,0:T(8,128)(2,1)S(1)}, u32[]{:S(2)}, u32[]{:S(2)}) collective-permute-start(bf16[8,192,128]{2,1,0:T(8,128)(2,1)S(1)} %get-tuple-element.141), channel_id=1, source_target_pairs={{0,24},{1,17},{2,26},{3,19},{4,28},{5,21},{6,30},{7,23},{8,16},{9,... | collective-permute-start | bytes 1179656 | tf_op jit(solution)/shard_map/ppermute | solution.py:63
  22.1 2.2 collective-permute-start
  24.3 3.0 %collective-permute-start.6 = (bf16[8,192,128]{2,1,0:T(8,128)(2,1)S(1)}, bf16[8,192,128]{2,1,0:T(8,128)(2,1)S(1)}, u32[]{:S(2)}, u32[]{:S(2)}) collective-permute-start(bf16[8,192,128]{2,1,0:T(8,128)(2,1)S(1)} %get-tuple-element.140), channel_id=1, source_target_pairs={{0,6},{1,3},{2,4},{3,1},{4,2},{5,7},{6,0},{7,5},{8,14},{9,11},{10,... | collective-permute-start | bytes 1179656 | tf_op jit(solution)/shard_map/ppermute | solution.py:63
  27.3 2.0 collective-permute-done.3
  29.4 2.8 %collective-permute-start.4 = (bf16[16,192,128]{2,1,0:T(8,128)(2,1)S(1)}, bf16[16,192,128]{2,1,0:T(8,128)(2,1)S(1)}, u32[]{:S(2)}, u32[]{:S(2)}) collective-permute-start(bf16[16,192,128]{2,1,0:T(8,128)(2,1)S(1)} %pad_maximum_fusion.4), channel_id=1, source_target_pairs={{0,6},{1,3},{2,4},{3,1},{4,2},{5,7},{6,0},{7,5},{8,14},{9,11},{10,... | collective-permute-start | bytes 2359304 | tf_op jit(solution)/shard_map/ppermute | solution.py:63
  32.2 1.8 collective-permute-start.1
  34.1 2.5 %collective-permute-start.7 = (bf16[16,192,128]{2,1,0:T(8,128)(2,1)S(1)}, bf16[16,192,128]{2,1,0:T(8,128)(2,1)S(1)}, u32[]{:S(2)}, u32[]{:S(2)}) collective-permute-start(bf16[16,192,128]{2,1,0:T(8,128)(2,1)S(1)} %pad_maximum_fusion.5), channel_id=1, source_target_pairs={{0,96},{1,33},{2,98},{3,35},{4,100},{5,37},{6,102},{7,39},{8,104},... | collective-permute-start | bytes 2359304 | tf_op jit(solution)/shard_map/ppermute | solution.py:63
  36.6 6.0 %collective-permute-done.4 = bf16[16,192,128]{2,1,0:T(8,128)(2,1)S(1)} collective-permute-done((bf16[16,192,128]{2,1,0:T(8,128)(2,1)S(1)}, bf16[16,192,128]{2,1,0:T(8,128)(2,1)S(1)}, u32[]{:S(2)}, u32[]{:S(2)}) %collective-permute-start.4) | collective-permute-done | bytes 786464 | tf_op jit(solution)/shard_map/ppermute | solution.py:63
  42.8 1.7 collective-permute-start.5
  44.6 1.6 collective-permute-done.1
  46.4 2.1 collective-permute-start.2
  48.5 1.3 pad_maximum_fusion.2.refs_4_
  49.8 1.5 collective-permute-start.8
  51.3 0.6 copy.13
  52.0 0.6 concatenate.37.tab
  52.6 8.6 %flip.1 = (bf16[4,2,192,1024]{3,2,1,0:T(8,128)(2,1)}, bf16[4,2,192,1024]{3,2,1,0:T(8,128)(2,1)}, bf16[2,4,192,1024]{3,2,1,0:T(8,128)(2,1)}) custom-call(bf16[512,4608]{1,0:T(8,128)(2,1)} %own_w.1, bf16[512,4608]{1,0:T(8,128)(2,1)} %collective-permute-done.9.other_ref.refs_7_.other_w), custom_call_target="tpu_custom_call" | custom-call | bytes 18874368 | tf_op jit(solution)/shard_map/flip/pallas_call | solution.py:141
  61.2 3.4 %collective-permute-done.5.refs_3_ = bf16[32,192,128]{2,1,0:T(8,128)(2,1)} collective-permute-done((bf16[32,192,128]{2,1,0:T(8,128)(2,1)S(1)}, bf16[32,192,128]{2,1,0:T(8,128)(2,1)}, u32[]{:S(2)}, u32[]{:S(2)}) %collective-permute-start.5) | collective-permute-done | bytes 1572896 | tf_op jit(solution)/shard_map/ppermute | solution.py:63
  64.6 7.1 %collective-permute-done.8.refs_5_ = bf16[32,192,128]{2,1,0:T(8,128)(2,1)} collective-permute-done((bf16[32,192,128]{2,1,0:T(8,128)(2,1)}, bf16[32,192,128]{2,1,0:T(8,128)(2,1)}, u32[]{:S(2)}, u32[]{:S(2)}) %collective-permute-start.8) | collective-permute-done | bytes 1572896 | tf_op jit(solution)/shard_map/ppermute | solution.py:63
  71.8 24.6 %act.1 = (f32[4,1024,256]{2,1,0:T(8,128)}, f32[4,1,256]{2,1,0:T(1,128)}, f32[4,1,256]{2,1,0:T(1,128)}, f32[64,16,128]{2,1,0:T(8,128)}, bf16[4,4608,256]{2,1,0:T(8,128)(2,1)}) custom-call(s32[26]{0:T(128)} %concatenate.37.tab, bf16[32,208,128]{2,1,0:T(8,128)(2,1)} %copy-done.7, bf16[32,208,128]{2,1,0:T(8,128)(2,1)} %collective-permute-done.2.refs_1_, ...), custom_call_target="tpu_custom_call" | custom-call | flops 9663676416 | bytes 30000000 | tf_op jit(solution)/shard_map/act/pallas_call | solution.py:294
  96.4 18.5 %all_to_all.16.totals_ref = f32[64,16,128]{2,1,0:T(8,128)} all-to-all(f32[64,16,128]{2,1,0:T(8,128)} %get-tuple-element.83), channel_id=1, replica_groups=mesh['x'=4,'ylo'=2,'yhi'=2,'z'=4,'core'=2] {'x','ylo','yhi','z'}, dimensions={0} | all-to-all | bytes 1048576 | tf_op jit(solution)/shard_map/all_to_all | solution.py:591
  114.9 11.8 %grad.1 = (bf16[4,1024,256]{2,1,0:T(8,128)(2,1)}, bf16[4,1024,256]{2,1,0:T(8,128)(2,1)}, bf16[2,2,1024,256]{3,2,1,0:T(8,128)(2,1)}, bf16[32,192,128]{2,1,0:T(8,1...) custom-call(s32[26]{0:T(128)} %concatenate.37.tab, f32[4,1024,256]{2,1,0:T(8,128)} %get-tuple-element.85.expo_ref, ...), custom_call_target="tpu_custom_call" | custom-call | flops 4831838208 | bytes 24000000 | tf_op jit(solution)/shard_map/grad/pallas_call | solution.py:473
  126.7 1.5 collective-permute-start.10
  128.2 0.8 collective-permute-start.11
  129.1 1.0 collective-permute-start.12
  130.0 16.0 %head.1 = (bf16[512,4608]{1,0:T(8,128)(2,1)}, bf16[512,4608]{1,0:T(8,128)(2,1)}, f32[1,4608]{1,0:T(1,128)}) custom-call(bf16[4,1024,256]{2,1,0:T(8,128)(2,1)} %get-tuple-element.93.gr, bf16[4,4608,256]{2,1,0:T(8,128)(2,1)} %get-tuple-element.94.xt, bf16[512,4608]{1,0:T(8,128)(2,1)} %own_w.1, bf16[512,4608]{1,0:T(8,128)(2,1)} %collective-permute-done.9.other_ref.refs_7_.other_w), custom_call_target="tpu_custom_call" | custom-call | flops 4718592 | bytes 1000000 | tf_op jit(solution)/shard_map/head/pallas_call | solution.py:524
  146.0 0.8 reduce.1
  146.9 1.2 collective-permute-done.13
  148.0 2.1 collective-permute-start.14
  150.1 10.1 %keep.1 = (bf16[32,192,128]{2,1,0:T(8,128)(2,1)}, bf16[32,192,128]{2,1,0:T(8,128)(2,1)}, bf16[32,192,128]{2,1,0:T(8,128)(2,1)}) custom-call(s32[26]{0:T(128)} %concatenate.37.tab, bf16[4,1024,256]{2,1,0:T(8,128)(2,1)} %get-tuple-element.98.gz_ref, bf16[2,2,1024,256]{3,2,1,0:T(8,128)(2,1)} %get-tuple-element.99.gy_ref, ...), custom_call_target="tpu_custom_call" | custom-call | flops 4718592 | bytes 1000000 | tf_op jit(solution)/shard_map/keep/pallas_call | solution.py:490
  160.3 3.1 %add_convert_fusion.3 = bf16[16,192,128]{2,1,0:T(8,128)(2,1)} fusion(bf16[32,192,128]{2,1,0:T(8,128)(2,1)S(1)} %collective-permute-done.10.refs_1_, bf16[32,192,128]{2,1,0:T(8,128)(2,1)} %get-tuple-element.106.refs_0_), kind=kLoop, calls=%fused_computation.7 | loop fusion | flops 1572864 | bytes 2359296 | tf_op jit(solution)/shard_map/convert_element_type | solution.py:606
  163.4 1.1 add_convert_fusion.2
  164.5 0.6 copy-done.5
  165.1 2.3 %add_convert_fusion.1 = bf16[16,192,128]{2,1,0:T(8,128)(2,1)} fusion(bf16[32,192,128]{2,1,0:T(8,128)(2,1)} %collective-permute-done.12.refs_9_, bf16[32,192,128]{2,1,0:T(8,128)(2,1)S(1)} %copy-done.5), kind=kLoop, calls=%fused_computation.5 | loop fusion | flops 1572864 | bytes 2359296 | tf_op jit(solution)/shard_map/convert_element_type | solution.py:606
  167.4 2.2 collective-permute-start.15
  169.6 1.2 collective-permute-start.16
  170.8 2.4 %collective-permute-start.17 = (bf16[16,192,128]{2,1,0:T(8,128)(2,1)}, bf16[16,192,128]{2,1,0:T(8,128)(2,1)}, u32[]{:S(2)}, u32[]{:S(2)}) collective-permute-start(bf16[16,192,128]{2,1,0:T(8,128)(2,1)} %add_convert_fusion.1), channel_id=1, source_target_pairs={{0,96},{1,33},{2,98},{3,35},{4,100},{5,37},{6,102},{7,39},{8,104},... | collective-permute-start | bytes 2359304 | tf_op jit(solution)/shard_map/ppermute | solution.py:63
  173.2 0.7 pad.4.clone
  173.9 0.6 fusion.17
  174.5 0.5 collective-permute-start.18
  174.9 0.7 fusion.15
  178.3 2.7 %collective-permute-done.18 = f32[36,128]{1,0:T(8,128)S(1)} collective-permute-done((f32[36,128]{1,0:T(8,128)S(1)}, f32[36,128]{1,0:T(8,128)S(1)}, u32[]{:S(2)}, u32[]{:S(2)}) %collective-permute-start.18) | collective-permute-done | bytes 18464 | tf_op jit(solution)/shard_map/ppermute | solution.py:63
  181.0 2.1 collective-permute-done.16.refs_6_
  183.1 1.2 collective-permute-done.17.refs_10_
  184.3 0.6 add.146
  184.9 2.1 add_convert_fusion.6
  187.0 1.4 add_convert_fusion.5
  188.4 1.4 add_convert_fusion.4
  189.8 2.5 %collective-permute-start.20 = (bf16[8,192,128]{2,1,0:T(8,128)(2,1)}, bf16[8,192,128]{2,1,0:T(8,128)(2,1)S(1)}, u32[]{:S(2)}, u32[]{:S(2)}) collective-permute-start(bf16[8,192,128]{2,1,0:T(8,128)(2,1)} %add_convert_fusion.6), channel_id=1, source_target_pairs={{0,96},{1,33},{2,98},{3,35},{4,100},{5,37},{6,102},{7,39},{8,104},... | collective-permute-start | bytes 1179656 | tf_op jit(solution)/shard_map/ppermute | solution.py:63
  192.3 0.5 collective-permute-start.21
  192.8 2.4 %collective-permute-start.22 = (bf16[8,192,128]{2,1,0:T(8,128)(2,1)S(1)}, bf16[8,192,128]{2,1,0:T(8,128)(2,1)S(1)}, u32[]{:S(2)}, u32[]{:S(2)}) collective-permute-start(bf16[8,192,128]{2,1,0:T(8,128)(2,1)S(1)} %add_convert_fusion.4), channel_id=1, source_target_pairs={{0,6},{1,3},{2,4},{3,1},{4,2},{5,7},{6,0},{7,5},{8,14},{9,11},{10,... | collective-permute-start | bytes 1179656 | tf_op jit(solution)/shard_map/ppermute | solution.py:63
  195.3 1.1 collective-permute-start.23
  196.4 1.2 multiply_bitcast_fusion
  197.6 2.8 %collective-permute-done.23 = f32[36,128]{1,0:T(8,128)S(1)} collective-permute-done((f32[36,128]{1,0:T(8,128)S(1)}, f32[36,128]{1,0:T(8,128)S(1)}, u32[]{:S(2)}, u32[]{:S(2)}) %collective-permute-start.23) | collective-permute-done | bytes 18464 | tf_op jit(solution)/shard_map/ppermute | solution.py:63
  200.4 0.9 collective-permute-done.21.refs_7_
  202.1 0.6 slice.142.refs_12_
  202.8 4.4 %last.1 = bf16[8,592,128]{2,1,0:T(8,128)(2,1)} custom-call(bf16[32,192,128]{2,1,0:T(8,128)(2,1)} %get-tuple-element.106.refs_0_, bf16[32,192,128]{2,1,0:T(8,128)(2,1)} %copy-done.2, bf16[16,192,128]{2,1,0:T(8,128)(2,1)} %collective-permute-done.15.refs_2_, bf16[8,192,128]{2,1,0:T(8,128)(2,1)} %copy-done.10, ...), custom_call_target="tpu_custom_call" | custom-call | flops 4194304 | bytes 6000000 | tf_op jit(solution)/shard_map/last/pallas_call | solution.py:555
  207.2 3.6 %all-to-all-start.2 = ((bf16[8,592,128]{2,1,0:T(8,128)(2,1)}), bf16[8,592,128]{2,1,0:T(8,128)(2,1)S(1)}, u32[]{:S(2)}, u32[]{:S(2)}) async-start(bf16[8,592,128]{2,1,0:T(8,128)(2,1)} %last.1), calls=%async_computation.2 | async-start | bytes 2424832 | tf_op jit(solution)/shard_map/all_to_all | solution.py:67
  210.8 7.1 %add_convert_fusion = bf16[512,4608]{1,0:T(8,128)(2,1)} fusion(bf16[512,4608]{1,0:T(8,128)(2,1)} %collective-permute-done.19, bf16[512,4608]{1,0:T(8,128)(2,1)} %get-tuple-element.136), kind=kLoop, calls=%fused_computation | loop fusion | flops 9437184 | bytes 14155776 | tf_op jit(solution)/shard_map/convert_element_type | solution.py:100
  217.9 4.0 %all-to-all-done.2 = bf16[8,592,128]{2,1,0:T(8,128)(2,1)S(1)} async-done(((bf16[8,592,128]{2,1,0:T(8,128)(2,1)}), bf16[8,592,128]{2,1,0:T(8,128)(2,1)S(1)}, u32[]{:S(2)}, u32[]{:S(2)}) %all-to-all-start.2) | async-done | bytes 1212448 | tf_op jit(solution)/shard_map/all_to_all | solution.py:67
  222.1 0.6 slice_divide_fusion
  222.7 0.8 fusion.6
  (82 shorter events, 2.5 us)
Async XLA Ops:
  0.6 50.7 %copy-start = (s32[2048]{0:T(1024)S(1)}, s32[2048]{0:T(1024)}, u32[]{:S(2)}) copy-start(s32[2048]{0:T(1024)} %param.7) | copy-start | bytes 24580
  0.6 51.9 %collective-permute-start.9 = (bf16[512,4608]{1,0:T(8,128)(2,1)}, bf16[512,4608]{1,0:T(8,128)(2,1)}, u32[]{:S(2)}, u32[]{:S(2)}) collective-permute-start(bf16[512,4608]{1,0:T(8,128)(2,1)} %own_w.1), channel_id=1, source_target_pairs={{0,1},{1,0},{2,3},{3,2},{4,5},{5,4},{6,7},{7,6},{8,9},{9,8},{10,11... | collective-permute-start | bytes 14155784 | tf_op jit(solution)/shard_map/ppermute | solution.py:63
  19.8 9.5 %collective-permute-start.3 = (bf16[8,192,128]{2,1,0:T(8,128)(2,1)S(1)}, bf16[8,192,128]{2,1,0:T(8,128)(2,1)S(1)}, u32[]{:S(2)}, u32[]{:S(2)}) collective-permute-start(bf16[8,192,128]{2,1,0:T(8,128)(2,1)S(1)} %get-tuple-element.141), channel_id=1, source_target_pairs={{0,24},{1,17},{2,26},{3,19},{4,28},{5,21},{6,30},{7,23},{8,16},{9,... | collective-permute-start | bytes 1179656 | tf_op jit(solution)/shard_map/ppermute | solution.py:63
  22.1 10.1 %collective-permute-start = (bf16[8,208,128]{2,1,0:T(8,128)(2,1)S(1)}, bf16[8,208,128]{2,1,0:T(8,128)(2,1)S(1)}, u32[]{:S(2)}, u32[]{:S(2)}) collective-permute-start(bf16[8,208,128]{2,1,0:T(8,128)(2,1)S(1)} %slice.138), channel_id=1, source_target_pairs={{0,96},{1,33},{2,98},{3,35},{4,100},{5,37},{6,102},{7,39},{8,104},... | collective-permute-start | bytes 1277960 | tf_op jit(solution)/shard_map/ppermute | solution.py:63
  24.3 9.8 %collective-permute-start.6 = (bf16[8,192,128]{2,1,0:T(8,128)(2,1)S(1)}, bf16[8,192,128]{2,1,0:T(8,128)(2,1)S(1)}, u32[]{:S(2)}, u32[]{:S(2)}) collective-permute-start(bf16[8,192,128]{2,1,0:T(8,128)(2,1)S(1)} %get-tuple-element.140), channel_id=1, source_target_pairs={{0,6},{1,3},{2,4},{3,1},{4,2},{5,7},{6,0},{7,5},{8,14},{9,11},{10,... | collective-permute-start | bytes 1179656 | tf_op jit(solution)/shard_map/ppermute | solution.py:63
  29.4 13.3 %collective-permute-start.4 = (bf16[16,192,128]{2,1,0:T(8,128)(2,1)S(1)}, bf16[16,192,128]{2,1,0:T(8,128)(2,1)S(1)}, u32[]{:S(2)}, u32[]{:S(2)}) collective-permute-start(bf16[16,192,128]{2,1,0:T(8,128)(2,1)S(1)} %pad_maximum_fusion.4), channel_id=1, source_target_pairs={{0,6},{1,3},{2,4},{3,1},{4,2},{5,7},{6,0},{7,5},{8,14},{9,11},{10,... | collective-permute-start | bytes 2359304 | tf_op jit(solution)/shard_map/ppermute | solution.py:63
  32.2 14.0 %collective-permute-start.1 = (bf16[16,208,128]{2,1,0:T(8,128)(2,1)S(1)}, bf16[16,208,128]{2,1,0:T(8,128)(2,1)S(1)}, u32[]{:S(2)}, u32[]{:S(2)}) collective-permute-start(bf16[16,208,128]{2,1,0:T(8,128)(2,1)S(1)} %pad_maximum_fusion.3), channel_id=1, source_target_pairs={{0,24},{1,17},{2,26},{3,19},{4,28},{5,21},{6,30},{7,23},{8,16},{9,... | collective-permute-start | bytes 2555912 | tf_op jit(solution)/shard_map/ppermute | solution.py:63
  34.1 14.4 %collective-permute-start.7 = (bf16[16,192,128]{2,1,0:T(8,128)(2,1)S(1)}, bf16[16,192,128]{2,1,0:T(8,128)(2,1)S(1)}, u32[]{:S(2)}, u32[]{:S(2)}) collective-permute-start(bf16[16,192,128]{2,1,0:T(8,128)(2,1)S(1)} %pad_maximum_fusion.5), channel_id=1, source_target_pairs={{0,96},{1,33},{2,98},{3,35},{4,100},{5,37},{6,102},{7,39},{8,104},... | collective-permute-start | bytes 2359304 | tf_op jit(solution)/shard_map/ppermute | solution.py:63
  42.8 3.6 %copy-start.8 = (bf16[32,192,128]{2,1,0:T(8,128)(2,1)}, bf16[32,192,128]{2,1,0:T(8,128)(2,1)S(1)}, u32[]{:S(2)}) copy-start(bf16[32,192,128]{2,1,0:T(8,128)(2,1)S(1)} %pad_maximum_fusion.1.refs_2_) | copy-start | bytes 4718596
  42.8 21.8 %collective-permute-start.5 = (bf16[32,192,128]{2,1,0:T(8,128)(2,1)S(1)}, bf16[32,192,128]{2,1,0:T(8,128)(2,1)}, u32[]{:S(2)}, u32[]{:S(2)}) collective-permute-start(bf16[32,192,128]{2,1,0:T(8,128)(2,1)S(1)} %pad_maximum_fusion.1.refs_2_), channel_id=1, source_target_pairs={{0,96},{1,33},{2,98},{3,35},{4,100},{5,37},{6,102},{7,39},{8,104},... | collective-permute-start | bytes 4718600 | tf_op jit(solution)/shard_map/ppermute | solution.py:63
  46.4 5.0 %copy-start.7 = (bf16[32,208,128]{2,1,0:T(8,128)(2,1)}, bf16[32,208,128]{2,1,0:T(8,128)(2,1)S(1)}, u32[]{:S(2)}) copy-start(bf16[32,208,128]{2,1,0:T(8,128)(2,1)S(1)} %pad_maximum_fusion.refs_0_) | copy-start | bytes 5111812
  46.4 25.4 %collective-permute-start.2 = (bf16[32,208,128]{2,1,0:T(8,128)(2,1)S(1)}, bf16[32,208,128]{2,1,0:T(8,128)(2,1)}, u32[]{:S(2)}, u32[]{:S(2)}) collective-permute-start(bf16[32,208,128]{2,1,0:T(8,128)(2,1)S(1)} %pad_maximum_fusion.refs_0_), channel_id=1, source_target_pairs={{0,6},{1,3},{2,4},{3,1},{4,2},{5,7},{6,0},{7,5},{8,14},{9,11},{10,... | collective-permute-start | bytes 5111816 | tf_op jit(solution)/shard_map/ppermute | solution.py:63
  49.8 21.9 %collective-permute-start.8 = (bf16[32,192,128]{2,1,0:T(8,128)(2,1)}, bf16[32,192,128]{2,1,0:T(8,128)(2,1)}, u32[]{:S(2)}, u32[]{:S(2)}) collective-permute-start(bf16[32,192,128]{2,1,0:T(8,128)(2,1)} %pad_maximum_fusion.2.refs_4_), channel_id=1, source_target_pairs={{0,24},{1,17},{2,26},{3,19},{4,28},{5,21},{6,30},{7,23},{8,16},{9,... | collective-permute-start | bytes 4718600 | tf_op jit(solution)/shard_map/ppermute | solution.py:63
  126.7 33.5 %collective-permute-start.10 = (bf16[32,192,128]{2,1,0:T(8,128)(2,1)}, bf16[32,192,128]{2,1,0:T(8,128)(2,1)S(1)}, u32[]{:S(2)}, u32[]{:S(2)}) collective-permute-start(bf16[32,192,128]{2,1,0:T(8,128)(2,1)} %get-tuple-element.90), channel_id=1, source_target_pairs={{0,6},{1,3},{2,4},{3,1},{4,2},{5,7},{6,0},{7,5},{8,14},{9,11},{10,... | collective-permute-start | bytes 4718600 | tf_op jit(solution)/shard_map/ppermute | solution.py:63
  128.2 32.0 %collective-permute-start.11 = (bf16[32,192,128]{2,1,0:T(8,128)(2,1)}, bf16[32,192,128]{2,1,0:T(8,128)(2,1)S(1)}, u32[]{:S(2)}, u32[]{:S(2)}) collective-permute-start(bf16[32,192,128]{2,1,0:T(8,128)(2,1)} %get-tuple-element.91), channel_id=1, source_target_pairs={{0,96},{1,33},{2,98},{3,35},{4,100},{5,37},{6,102},{7,39},{8,104},... | collective-permute-start | bytes 4718600 | tf_op jit(solution)/shard_map/ppermute | solution.py:63
  129.1 31.2 %collective-permute-start.12 = (bf16[32,192,128]{2,1,0:T(8,128)(2,1)}, bf16[32,192,128]{2,1,0:T(8,128)(2,1)}, u32[]{:S(2)}, u32[]{:S(2)}) collective-permute-start(bf16[32,192,128]{2,1,0:T(8,128)(2,1)} %get-tuple-element.92), channel_id=1, source_target_pairs={{0,24},{1,17},{2,26},{3,19},{4,28},{5,21},{6,30},{7,23},{8,16},{9,... | collective-permute-start | bytes 4718600 | tf_op jit(solution)/shard_map/ppermute | solution.py:63
  146.8 1.3 collective-permute-start.13
  148.0 12.2 %collective-permute-start.14 = (f32[36,128]{1,0:T(8,128)S(1)}, f32[36,128]{1,0:T(8,128)S(1)}, u32[]{:S(2)}, u32[]{:S(2)}) collective-permute-start(f32[36,128]{1,0:T(8,128)S(1)} %bitcast_add_fusion), channel_id=1, source_target_pairs={{0,6},{1,3},{2,4},{3,1},{4,2},{5,7},{6,0},{7,5},{8,14},{9,11},{10,... | collective-permute-start | bytes 55304 | tf_op jit(solution)/shard_map/ppermute | solution.py:63
  160.2 3.2 %copy-start.4 = (bf16[32,192,128]{2,1,0:T(8,128)(2,1)S(1)}, bf16[32,192,128]{2,1,0:T(8,128)(2,1)}, u32[]{:S(2)}) copy-start(bf16[32,192,128]{2,1,0:T(8,128)(2,1)} %get-tuple-element.108.refs_4_) | copy-start | bytes 4718596
  160.2 24.7 %copy-start.2 = (bf16[32,192,128]{2,1,0:T(8,128)(2,1)}, bf16[32,192,128]{2,1,0:T(8,128)(2,1)S(1)}, u32[]{:S(2)}) copy-start(bf16[32,192,128]{2,1,0:T(8,128)(2,1)S(1)} %collective-permute-done.10.refs_1_) | copy-start | bytes 4718596
  160.2 26.8 %copy-start.3 = (bf16[32,192,128]{2,1,0:T(8,128)(2,1)}, bf16[32,192,128]{2,1,0:T(8,128)(2,1)S(1)}, u32[]{:S(2)}) copy-start(bf16[32,192,128]{2,1,0:T(8,128)(2,1)S(1)} %collective-permute-done.11.refs_5_) | copy-start | bytes 4718596
  163.4 1.7 copy-start.5
  165.1 8.8 %copy-start.14 = (s32[26]{0:T(128)S(1)}, s32[26]{0:T(128)}, u32[]{:S(2)}) copy-start(s32[26]{0:T(128)} %concatenate.37.tab) | copy-start | bytes 316
  167.4 16.9 %collective-permute-start.19 = (bf16[512,4608]{1,0:T(8,128)(2,1)}, bf16[512,4608]{1,0:T(8,128)(2,1)}, u32[]{:S(2)}, u32[]{:S(2)}) collective-permute-start(bf16[512,4608]{1,0:T(8,128)(2,1)} %get-tuple-element.118), channel_id=1, source_target_pairs={{0,1},{1,0},{2,3},{3,2},{4,5},{5,4},{6,7},{7,6},{8,9},{9,8},{10,11... | collective-permute-start | bytes 14155784 | tf_op jit(solution)/shard_map/ppermute | solution.py:63
  167.4 13.6 %collective-permute-start.15 = (bf16[16,192,128]{2,1,0:T(8,128)(2,1)}, bf16[16,192,128]{2,1,0:T(8,128)(2,1)}, u32[]{:S(2)}, u32[]{:S(2)}) collective-permute-start(bf16[16,192,128]{2,1,0:T(8,128)(2,1)} %add_convert_fusion.3), channel_id=1, source_target_pairs={{0,24},{1,17},{2,26},{3,19},{4,28},{5,21},{6,30},{7,23},{8,16},{9,... | collective-permute-start | bytes 2359304 | tf_op jit(solution)/shard_map/ppermute | solution.py:63
  169.6 13.5 %collective-permute-start.16 = (bf16[16,192,128]{2,1,0:T(8,128)(2,1)}, bf16[16,192,128]{2,1,0:T(8,128)(2,1)}, u32[]{:S(2)}, u32[]{:S(2)}) collective-permute-start(bf16[16,192,128]{2,1,0:T(8,128)(2,1)} %add_convert_fusion.2), channel_id=1, source_target_pairs={{0,6},{1,3},{2,4},{3,1},{4,2},{5,7},{6,0},{7,5},{8,14},{9,11},{10,... | collective-permute-start | bytes 2359304 | tf_op jit(solution)/shard_map/ppermute | solution.py:63
  170.8 13.5 %collective-permute-start.17 = (bf16[16,192,128]{2,1,0:T(8,128)(2,1)}, bf16[16,192,128]{2,1,0:T(8,128)(2,1)}, u32[]{:S(2)}, u32[]{:S(2)}) collective-permute-start(bf16[16,192,128]{2,1,0:T(8,128)(2,1)} %add_convert_fusion.1), channel_id=1, source_target_pairs={{0,96},{1,33},{2,98},{3,35},{4,100},{5,37},{6,102},{7,39},{8,104},... | collective-permute-start | bytes 2359304 | tf_op jit(solution)/shard_map/ppermute | solution.py:63
  174.5 6.5 %collective-permute-start.18 = (f32[36,128]{1,0:T(8,128)S(1)}, f32[36,128]{1,0:T(8,128)S(1)}, u32[]{:S(2)}, u32[]{:S(2)}) collective-permute-start(f32[36,128]{1,0:T(8,128)S(1)} %fusion.18), channel_id=1, source_target_pairs={{0,24},{1,17},{2,26},{3,19},{4,28},{5,21},{6,30},{7,23},{8,16},{9,... | collective-permute-start | bytes 55304 | tf_op jit(solution)/shard_map/ppermute | solution.py:63
  187.0 8.2 %copy-start.6 = (f32[64,16,128]{2,1,0:T(8,128)S(1)}, f32[64,16,128]{2,1,0:T(8,128)}, u32[]{:S(2)}) copy-start(f32[64,16,128]{2,1,0:T(8,128)} %all_to_all.16.totals_ref) | copy-start | bytes 1572868
  188.4 6.9 %copy-start.13 = (f32[36,128]{1,0:T(8,128)S(1)}, f32[36,128]{1,0:T(8,128)}, u32[]{:S(2)}) copy-start(f32[36,128]{1,0:T(8,128)} %add.146) | copy-start | bytes 55300
  188.4 13.6 %copy-start.16 = (bf16[4]{0:T(256)(128)(2,1)S(1)}, bf16[4]{0:T(256)(128)(2,1)}, u32[]{:S(2)}) copy-start(bf16[4]{0:T(256)(128)(2,1)} %pad.4.clone) | copy-start | bytes 28
  189.8 10.6 %collective-permute-start.20 = (bf16[8,192,128]{2,1,0:T(8,128)(2,1)}, bf16[8,192,128]{2,1,0:T(8,128)(2,1)S(1)}, u32[]{:S(2)}, u32[]{:S(2)}) collective-permute-start(bf16[8,192,128]{2,1,0:T(8,128)(2,1)} %add_convert_fusion.6), channel_id=1, source_target_pairs={{0,96},{1,33},{2,98},{3,35},{4,100},{5,37},{6,102},{7,39},{8,104},... | collective-permute-start | bytes 1179656 | tf_op jit(solution)/shard_map/ppermute | solution.py:63
  192.3 9.0 %collective-permute-start.21 = (bf16[8,192,128]{2,1,0:T(8,128)(2,1)S(1)}, bf16[8,192,128]{2,1,0:T(8,128)(2,1)S(1)}, u32[]{:S(2)}, u32[]{:S(2)}) collective-permute-start(bf16[8,192,128]{2,1,0:T(8,128)(2,1)S(1)} %add_convert_fusion.5), channel_id=1, source_target_pairs={{0,24},{1,17},{2,26},{3,19},{4,28},{5,21},{6,30},{7,23},{8,16},{9,... | collective-permute-start | bytes 1179656 | tf_op jit(solution)/shard_map/ppermute | solution.py:63
  192.8 9.0 %collective-permute-start.22 = (bf16[8,192,128]{2,1,0:T(8,128)(2,1)S(1)}, bf16[8,192,128]{2,1,0:T(8,128)(2,1)S(1)}, u32[]{:S(2)}, u32[]{:S(2)}) collective-permute-start(bf16[8,192,128]{2,1,0:T(8,128)(2,1)S(1)} %add_convert_fusion.4), channel_id=1, source_target_pairs={{0,6},{1,3},{2,4},{3,1},{4,2},{5,7},{6,0},{7,5},{8,14},{9,11},{10,... | collective-permute-start | bytes 1179656 | tf_op jit(solution)/shard_map/ppermute | solution.py:63
  195.3 5.1 %collective-permute-start.23 = (f32[36,128]{1,0:T(8,128)S(1)}, f32[36,128]{1,0:T(8,128)S(1)}, u32[]{:S(2)}, u32[]{:S(2)}) collective-permute-start(f32[36,128]{1,0:T(8,128)S(1)} %copy-done.13), channel_id=1, source_target_pairs={{0,96},{1,33},{2,98},{3,35},{4,100},{5,37},{6,102},{7,39},{8,104},... | collective-permute-start | bytes 55304 | tf_op jit(solution)/shard_map/ppermute | solution.py:63
  200.4 2.4 %copy-start.10 = (bf16[8,192,128]{2,1,0:T(8,128)(2,1)}, bf16[8,192,128]{2,1,0:T(8,128)(2,1)S(1)}, u32[]{:S(2)}) copy-start(bf16[8,192,128]{2,1,0:T(8,128)(2,1)S(1)} %collective-permute-done.20.refs_3_) | copy-start | bytes 1179652
  201.3 1.5 copy-start.11
  201.8 1.0 copy-start.12
  207.2 14.7 %all-to-all-start.2 = ((bf16[8,592,128]{2,1,0:T(8,128)(2,1)}), bf16[8,592,128]{2,1,0:T(8,128)(2,1)S(1)}, u32[]{:S(2)}, u32[]{:S(2)}) async-start(bf16[8,592,128]{2,1,0:T(8,128)(2,1)} %last.1), calls=%async_computation.2 | async-start | bytes 2424832 | tf_op jit(solution)/shard_map/all_to_all | solution.py:67
  210.8 11.3 %copy-start.15 = (bf16[576]{0:T(1024)(128)(2,1)S(1)}, bf16[576]{0:T(1024)(128)(2,1)}, u32[]{:S(2)}) copy-start(bf16[576]{0:T(1024)(128)(2,1)} %param.5) | copy-start | bytes 3460
  210.8 12.7 %copy-start.1 = (s32[2048]{0:T(1024)S(1)}, s32[2048]{0:T(1024)}, u32[]{:S(2)}) copy-start(s32[2048]{0:T(1024)} %param.7) | copy-start | bytes 24580
  217.9 4.8 %copy-start.9 = (bf16[128,576]{0,1:T(8,128)(2,1)S(1)}, bf16[128,576]{0,1:T(8,128)(2,1)}, u32[]{:S(2)}) copy-start(bf16[128,576]{0,1:T(8,128)(2,1)} %param.4) | copy-start | bytes 442372

commit v2 on v1

--- a/solution.py
+++ b/solution.py
@@ -96,10 +96,6 @@
     return [hi.astype(BF), mid.astype(BF), lo.astype(BF)]
 
 
-def add(a, b):
-    return (a.astype(F32) + b.astype(F32)).astype(a.dtype)
-
-
 def table(x, y, z, core, shard):
     out = []
     place = jnp.arange(4, dtype=jnp.int32)
@@ -131,7 +127,7 @@
         cols = pl.ds(h * VB, VB)
         for ylo in range(2):
             at = ylo * FB
-            a_ref[0, ylo, :, cols] = turned[at : at + PT]
+            a_ref[ylo, 0, :, cols] = turned[at : at + PT]
             b_ref[0, ylo, :, cols] = turned[at + PT : at + 2 * PT]
             c_ref[ylo, 0, :, cols] = turned[at + 2 * PT : at + 3 * PT]
 
@@ -143,12 +139,12 @@
         grid=(4,),
         in_specs=[block, block],
         out_specs=[
-            pl.BlockSpec((1, 2, PT, 2 * VB), lambda x: (x, 0, 0, 0)),
+            pl.BlockSpec((2, 1, PT, 2 * VB), lambda x: (0, x, 0, 0)),
             pl.BlockSpec((1, 2, PT, 2 * VB), lambda x: (x, 0, 0, 0)),
             pl.BlockSpec((2, 1, PT, 2 * VB), lambda x: (0, x, 0, 0)),
         ],
         out_shape=[
-            jax.ShapeDtypeStruct((4, 2, PT, 2 * VB), BF),
+            jax.ShapeDtypeStruct((2, 4, PT, 2 * VB), BF),
             jax.ShapeDtypeStruct((4, 2, PT, 2 * VB), BF),
             jax.ShapeDtypeStruct((2, 4, PT, 2 * VB), BF),
         ],
@@ -343,7 +339,7 @@
             for ylo in range(2):
                 for yhi in range(2):
                     places = (place_of(tab, 0, x), place_of(tab, 1, yhi * 2 + ylo), lead * 2 + low)
-                    row, lane = (x * 2 + ylo) * PT, (low * 2 + yhi) * TB
+                    row, lane = (ylo * 4 + x) * PT, (low * 2 + yhi) * TB
                     out0[block_at(0, places)] = got[row : row + PT, lane : lane + TB]
     done(0)
     ready(1)
@@ -381,12 +377,13 @@
 
 
 def grad_kernel(tab, expo_ref, bend_ref, totals_ref, rinv_ref, tgt_ref, *refs):
-    w_refs, out_refs = refs[:3], refs[3:9]
-    expo, w0, w1, w2, gz, gr, gy, away0, away1, away2, in_sems, out_sems = refs[9:]
+    w_refs, out_refs = refs[:3], refs[3:10]
+    expo, w0, w1, w2, gz, gr, gy, away0, away1, away2, in_sems, out_sems = refs[10:]
     weights, away = (w0, w1, w2), (away0, away1, away2)
     tiles = [(expo_ref.at[i], expo.at[i]) for i in range(4)]
     incoming = copies(tiles + list(zip(w_refs, weights)), in_sems)
-    outgoing = copies(list(zip((gz, gr, gy) + away, out_refs)), out_sems)
+    by_rows = (gr.at[:, pl.ds(0, VB)], gr.at[:, pl.ds(VB, VB)])
+    outgoing = copies(list(zip(by_rows + (gz, gy) + away, out_refs)), out_sems)
     for copy in incoming:
         copy.start()
     rows = 32
@@ -425,11 +422,11 @@
                 ),
                 0,
             )
-    for copy in outgoing[:3]:
+    for copy in outgoing[:4]:
         copy.start()
     pieces(
         tab, 1, gz, gy, weights, away,
-        lambda p: incoming[4 + p].wait(), lambda p: outgoing[3 + p].start(),
+        lambda p: incoming[4 + p].wait(), lambda p: outgoing[4 + p].start(),
     )
     for copy in outgoing:
         copy.wait()
@@ -457,8 +454,9 @@
 
 HALF = (32, PT, TB)
 GZ = (4, 2 * VB, 2 * TB)
+GR = (4, VB, 2 * TB)
 GY = (2, 2, 2 * VB, 2 * TB)
-W_SHAPES = ((4, 2, PT, 2 * VB), (4, 2, PT, 2 * VB), (2, 4, PT, 2 * VB))
+W_SHAPES = ((2, 4, PT, 2 * VB), (4, 2, PT, 2 * VB), (2, 4, PT, 2 * VB))
 
 
 def bf16_out(*shapes):
@@ -473,11 +471,11 @@
     return pl.pallas_call(
         grad_kernel,
         in_specs=[SMEM_SPEC, ANYWHERE] + [VMEM_SPEC] * 4 + [ANYWHERE] * 3,
-        out_specs=[ANYWHERE] * 6,
-        out_shape=bf16_out(GZ, GZ, GY, HALF, HALF, HALF),
+        out_specs=[ANYWHERE] * 7,
+        out_shape=bf16_out(GR, GR, GZ, GY, HALF, HALF, HALF),
         scratch_shapes=[pltpu.VMEM(GZ, F32)]
         + bf16_vmem(*W_SHAPES, GZ, GZ, GY, HALF, HALF, HALF)
-        + [pltpu.SemaphoreType.DMA((7,)), pltpu.SemaphoreType.DMA((6,))],
+        + [pltpu.SemaphoreType.DMA((7,)), pltpu.SemaphoreType.DMA((7,))],
         compiler_params=pltpu.CompilerParams(vmem_limit_bytes=VMEM),
         cost_estimate=pl.CostEstimate(
             flops=1024 * 1024 * D, bytes_accessed=24_000_000, transcendentals=0
@@ -504,64 +502,81 @@
     )(tab, gz, gy, *turned)
 
 
-def head_kernel(gr, xt, own_w, other_w, own_ref, other_ref, gain_ref):
+def head_kernel(own_gr, twin_gr, own_xt, twin_xt, w, *refs):
+    head_ref, gain_ref = refs[-2:]
     got = lax.dot_general(
-        jnp.concatenate([gr[z] for z in range(4)], axis=1),
-        jnp.concatenate([xt[z] for z in range(4)], axis=1),
+        jnp.concatenate([gr[z] for gr in (own_gr, twin_gr) for z in range(4)], axis=1),
+        jnp.concatenate([xt[z] for xt in (own_xt, twin_xt) for z in range(4)], axis=1),
         (((1,), (1,)), ((), ())), preferred_element_type=F32,
     )
-    own_ref[...] = got[:VB].astype(BF)
-    other_ref[...] = got[VB:].astype(BF)
-    gain_ref[...] = jnp.sum(
-        got[:VB] * own_w[...].astype(F32) + got[VB:] * other_w[...].astype(F32),
-        axis=0, keepdims=True,
-    )
-
-
-def head_call(gr, xt, own, other):
-    tile = 768
-    cols = pl.BlockSpec((VB, tile), lambda f: (0, f))
+    head_ref[...] = got.astype(BF)
+    gain = jnp.sum(got * w[...].astype(F32), axis=0, keepdims=True)
+    for i in range(gain_ref.shape[1]):
+        gain_ref[0, i : i + 1, :] = gain[:, i * TB : (i + 1) * TB]
+
+
+TILE = 768
+
+
+def head_call(grs, xts, w, first, count, held=()):
+    cols = pl.BlockSpec((VB, TILE), lambda f: (0, f + first))
+    rows = pl.BlockSpec(GR, lambda f: (0, 0, 0), pipeline_mode=pl.Buffered(1))
+    tokens = pl.BlockSpec((4, TILE, 2 * TB), lambda f: (0, f + first, 0))
     return pl.pallas_call(
         head_kernel,
-        grid=(D // tile,),
-        in_specs=[
-            pl.BlockSpec((4, 2 * VB, 2 * TB), lambda f: (0, 0, 0), pipeline_mode=pl.Buffered(1)),
-            pl.BlockSpec((4, tile, 2 * TB), lambda f: (0, f, 0)),
-            cols,
-            cols,
-        ],
-        out_specs=[cols, cols, pl.BlockSpec((1, tile), lambda f: (0, f))],
-        out_shape=bf16_out((VB, D), (VB, D)) + [jax.ShapeDtypeStruct((1, D), F32)],
+        grid=(count,),
+        in_specs=[rows, rows, tokens, tokens, cols] + [ANYWHERE] * len(held),
+        out_specs=[cols, pl.BlockSpec((1, TILE // TB, TB), lambda f: (f, 0, 0))],
+        out_shape=bf16_out((VB, D)) + [jax.ShapeDtypeStruct((count, TILE // TB, TB), F32)],
+        input_output_aliases={5 + i: i for i in range(len(held))},
         compiler_params=pltpu.CompilerParams(vmem_limit_bytes=VMEM),
         cost_estimate=pl.CostEstimate(
             flops=1024 * D, bytes_accessed=1_000_000, transcendentals=0
         ),
         name="head",
-    )(gr, xt, own, other)
-
-
-def last_kernel(*refs):
-    out_ref = refs[-1]
-    gain_ref = refs[-2]
+    )(*grs, *xts, w, *held)
+
+
+def sum_kernel(terms, *refs):
+    ins, outs = refs[: 3 * terms], refs[3 * terms :]
     for p in range(3):
-        here = refs[4 * p : 4 * p + 4]
-        out_ref[:, p * PT : (p + 1) * PT, :] = total([a[...] for a in here]).astype(BF)
-    out_ref[:, FB : FB + SQ, :] = gain_ref[...]
-
-
-def last_call(here, gains):
-    count = 2
-    block = pl.BlockSpec((count, PT, TB), lambda i: (i, 0, 0))
+        blocks = [a[...] for a in ins[terms * p : terms * (p + 1)]]
+        got = blocks[0] + blocks[1] if terms == 2 else total(blocks).astype(BF)
+        if len(outs) == 3:
+            outs[p][...] = got
+        else:
+            outs[-1][:, p * PT : (p + 1) * PT, :] = got
+    if len(outs) == 2:
+        outs[-1][:, FB : FB + SQ, :] = outs[0][...]
+
+
+def sum_call(here, count, gains=None):
+    step = count // 2
+    terms = len(here[0])
+    specs = [
+        pl.BlockSpec((step, PT, TB), lambda i, first=first // step: (i + first, 0, 0))
+        for part in here
+        for _, first in part
+    ]
+    arrays = [a for part in here for a, _ in part]
+    if gains is None:
+        out_specs = [pl.BlockSpec((step, PT, TB), lambda i: (i, 0, 0))] * 3
+        out_shape = bf16_out(*[(count, PT, TB)] * 3)
+    else:
+        specs.append(pl.BlockSpec((step, SQ, TB), lambda i: (i, 0, 0)))
+        arrays.append(gains)
+        out_specs = pl.BlockSpec((step, FB + SQ, TB), lambda i: (i, 0, 0))
+        out_shape = bf16_out((count, FB + SQ, TB))[0]
     return pl.pallas_call(
-        last_kernel,
-        grid=(8 // count,),
-        in_specs=[block] * 12 + [pl.BlockSpec((count, SQ, TB), lambda i: (i, 0, 0))],
-        out_specs=pl.BlockSpec((count, FB + SQ, TB), lambda i: (i, 0, 0)),
-        out_shape=jax.ShapeDtypeStruct((8, FB + SQ, TB), BF),
+        functools.partial(sum_kernel, terms),
+        grid=(count // step,),
+        in_specs=specs,
+        out_specs=out_specs,
+        out_shape=out_shape,
         compiler_params=pltpu.CompilerParams(vmem_limit_bytes=VMEM),
         cost_estimate=pl.CostEstimate(flops=4 << 20, bytes_accessed=6_000_000, transcendentals=0),
-        name="last",
-    )(*[a for part in here for a in part], gains)
+        name="sum%d" % terms,
+    )(*arrays)
 
 
 def shards(section_output, norm_gain, head_weight, targets):
@@ -585,47 +600,56 @@
         targets.reshape(2, 4, 2, TB), core, axis=2, keepdims=False
     ).transpose(1, 0, 2).reshape(4, 1, 2 * TB)
     halves = gather(block)
-    halves, turned, tgt, tab = lax.optimization_barrier((halves, turned, tgt, tab))
+    owner = jnp.stack([tab[ex] * 2 + (tab[4 + ey] & 1) for ex, ey, _ in BITS])
+    owner = (owner[:, None, None] == jnp.arange(8, dtype=jnp.int32)[None, :, None]).astype(F32)
+    halves, turned, tgt, tab, owner = lax.optimization_barrier((halves, turned, tgt, tab, owner))
 
     expo, bend, rinv, stats, xt_all = act_call(tab, halves, head_weight, other, tgt)
+    xts = (xt_all, send(xt_all, TWIN))
     stats = lax.all_to_all(stats, AX[:4], 0, 0)
 
-    gz, gr, gy, *away = grad_call(tab, expo, bend, stats, rinv, tgt, turned)
+    own_gr, other_gr, gz, gy, *away = grad_call(tab, expo, bend, stats, rinv, tgt, turned)
 
     bound = lax.optimization_barrier
-    got = [send(away[p], across(ORDER[p][2])) for p in range(3)]
-    own_part, other_part, gains = head_call(gr, xt_all, head_weight, other)
-    gains, gz, gy = bound((gains, gz, gy))
+
+    def exchange(away, phase):
+        return [send(away[p], across(ORDER[p][phase])) for p in range(3)]
+
+    got1 = exchange(away, 2)
+    grs = (own_gr, send(other_gr, TWIN))
     kept = keep_call(tab, gz, gy, turned)
-    gains = gains.reshape(D // TB, TB)
-    gains = gains + send(gains, TWIN)
-    gains = gains + send(gains, across(2))
-    got, kept, gains, own_part, other_part = bound((got, kept, gains, own_part, other_part))
-    here = [[kept[p], got[p]] for p in range(3)]
-    for phase, half in ((1, 16), (0, 8)):
-        away = [total([a[half:2 * half] for a in here[p]]).astype(BF) for p in range(3)]
-        away, gains, other_part = bound((away, gains, other_part))
-        got = [send(away[p], across(ORDER[p][phase])) for p in range(3)]
-        more = send(gains, across(phase))
-        if phase == 1:
-            other_part = send(other_part, TWIN)
-        got, more, other_part = bound((got, more, other_part))
-        gains = gains + more
-        here = [here[p] + [got[p]] for p in range(3)]
-
-    owner = jnp.stack([tab[ex] * 2 + (tab[4 + ey] & 1) for ex, ey, _ in BITS])
-    chosen = owner[:, None, None] == jnp.arange(8, dtype=jnp.int32)[None, :, None]
-    gains = jnp.sum(jnp.where(chosen, gains.reshape(1, 8, FB), 0.0), axis=1)
+    kept, grs = bound((kept, grs))
+    head_grad, gain0 = head_call(grs, xts, head_weight, 0, 4)
+    got1, kept, grs, head_grad, gain0 = bound((got1, kept, grs, head_grad, gain0))
+    away = sum_call([[(kept[p], 16), (got1[p], 16)] for p in range(3)], 16)
+
+    away, grs, head_grad = bound((away, grs, head_grad))
+    got2 = exchange(away, 1)
+    head_grad, gain1 = head_call(grs, xts, head_weight, 4, 2, (head_grad,))
+    gains = jnp.concatenate([gain0, gain1])
+    gains = gains + send(gains, across(1))
+    got2, gains = bound((got2, gains))
+    more = send(gains, across(0))
+    away = sum_call([[(kept[p], 8), (got1[p], 8), (got2[p], 8)] for p in range(3)], 8)
+
+    away, more, gains = bound((away, more, gains))
+    got3 = exchange(away, 0)
+    gains = gains + more
+    more = send(gains, across(2))
+    got3, more = bound((got3, more))
+    gains = gains + more
+    here = [[(a[p], 0) for a in (kept, got1, got2, got3)] for p in range(3)]
+
+    gains = jnp.sum(owner * gains.reshape(1, 8, FB), axis=1)
     gains = jnp.concatenate([gains, jnp.zeros((8, 5 * TB - FB), F32)], axis=1)
     gains = jnp.stack(split3(gains) + [jnp.zeros((8, 5 * TB), BF)], axis=1)
     gains = gains.reshape(8, 20, TB)[:, :SQ]
 
-    blocks, own_part, other_part = bound((last_call(here, gains), own_part, other_part))
-    blocks, head_grad = bound((in_cube(blocks), add(own_part, other_part)))
+    blocks = in_cube(sum_call(here, 8, gains))
     blocks = jnp.sum(blocks.astype(F32), axis=0)
     grad_hidden = blocks[:FB]
     gains = jnp.sum(blocks[FB : FB + 15].reshape(3, 5 * TB), axis=0)[:FB]
-    gain_grad = gains / norm_gain.astype(F32)
+    gain_grad = (gains + send(gains, TWIN)) / norm_gain.astype(F32)
 
     row = jnp.sum(stats, axis=0)
     picked, slope, slope_at = row[8:9], row[9:10], row[10:11]

time: 224 us -> 219 us (0.978)
  other arithmetic: 26.6 us -> 6.75 us
  Pallas kernels: 75.5 us -> 84.2 us
    convert_element_type x7 -> x1, other arithmetic: 18.5 us -> 0.07 us  [shards(): (owner[:, None, None] == jnp.arange(8, dtype=jnp.int32)[None, :, None]).a...]
    pallas_call x2 -> x5, Pallas kernels: 20.4 us -> 29.2 us  [the longest x2 19 us: head_call(): pl.pallas_call(head_kernel, grid=(count,), in_specs=[rows, rows, tokens,...]
    all_to_all x1, waiting for transfers between devices: 3.95 us -> 9.11 us  [in_cube(): return lax.all_to_all(a, AX, 0, 0, axis_index_groups=CUBES)]
    ppermute x24 -> x25, waiting for transfers between devices: 31.7 us -> 27.3 us  [send(): return lax.ppermute(a, AX, pairs)]
    ppermute x24 -> x25, starting transfers between devices: 38.2 us -> 37.9 us  [send(): return lax.ppermute(a, AX, pairs)]
  transfers between devices with their start and end apart: 25 -> 26, of which waited for: 13 -> 9; matrix products, arithmetic and copies ran while one was open for 7% -> 5% of each run, Pallas kernels for 15% -> 24%
where the time goes in v2:
time: 219 us; the launch traced here: 217 us
  Pallas kernels  84.2 us (38%)
  starting transfers between devices  41.6 us (19%)
  blocking collectives  37.4 us (17%)
  waiting for transfers between devices  36.4 us (17%)
  local copies, waits for them, and re-layouts  7.18 us (3%)
  other arithmetic  6.75 us (3%)
  between operations  3.71 us (2%)
    ppermute x25, starting transfers between devices, send(): return lax.ppermute(a, AX, pairs)  37.9 us
    ppermute x25, waiting for transfers between devices, send(): return lax.ppermute(a, AX, pairs)  27.3 us
    pallas_call x1, Pallas kernels, act_call(): pl.pallas_call(act_kernel, grid_spec=pltpu.PrefetchScalarGridSpec(num_sca...  24.6 us
    all_to_all x1, blocking collectives, shards(): stats = lax.all_to_all(stats, AX[:4], 0, 0)  20.5 us
    pallas_call x2, Pallas kernels, head_call(): pl.pallas_call(head_kernel, grid=(count,), in_specs=[rows, rows, tokens,...  19 us
    all_to_all x1, blocking collectives, in_cube(): return lax.all_to_all(a, AX, 0, 0, axis_index_groups=CUBES)  16.9 us
    pallas_call x1, Pallas kernels, grad_call(): pl.pallas_call(grad_kernel, in_specs=[SMEM_SPEC, ANYWHERE] + [VMEM_SPEC]...  11.8 us
    pallas_call x3, Pallas kernels, sum_call(): pl.pallas_call(functools.partial(sum_kernel, terms), grid=(count // step,...  10.2 us
  transfers between devices with their start and end apart: 26, of which 9 were waited for; matrix products, arithmetic and copies ran while one was open for 5% of the time, Pallas kernels for 24%

profile of v2, /device:TPU:0, one launch (start us, length us, event | category | flops | bytes accessed | tf_op | source)
XLA Modules:
  0.0 217.3 jit_solution(1700244512038380494)
XLA Ops:
  0.7 0.7 convert_element_type.74
  1.4 1.1 fusion.1
  2.5 0.2 concatenate.33
  2.7 0.2 broadcast_in_dim.5
  2.9 16.9 %all_to_all.15 = bf16[8,592,128]{2,1,0:T(8,128)(2,1)S(1)} all-to-all(bf16[8,592,128]{2,1,0:T(8,128)(2,1)S(1)} %broadcast_in_dim.5), channel_id=1, replica_groups={{0,2,16,18,32,34,48,50},{6,4,22,20,38,36,54,52},{24,26,8,10,56,58,40,42..., dimensions={0} | all-to-all | bytes 2424832 | tf_op jit(solution)/shard_map/all_to_all | solution.py:67
  19.8 2.3 %collective-permute-start.3 = (bf16[8,192,128]{2,1,0:T(8,128)(2,1)S(1)}, bf16[8,192,128]{2,1,0:T(8,128)(2,1)S(1)}, u32[]{:S(2)}, u32[]{:S(2)}) collective-permute-start(bf16[8,192,128]{2,1,0:T(8,128)(2,1)S(1)} %get-tuple-element.153), channel_id=1, source_target_pairs={{0,24},{1,17},{2,26},{3,19},{4,28},{5,21},{6,30},{7,23},{8,16},{9,... | collective-permute-start | bytes 1179656 | tf_op jit(solution)/shard_map/ppermute | solution.py:63
  22.1 2.2 %collective-permute-start = (bf16[8,208,128]{2,1,0:T(8,128)(2,1)S(1)}, bf16[8,208,128]{2,1,0:T(8,128)(2,1)S(1)}, u32[]{:S(2)}, u32[]{:S(2)}) collective-permute-start(bf16[8,208,128]{2,1,0:T(8,128)(2,1)S(1)} %slice.78), channel_id=1, source_target_pairs={{0,96},{1,33},{2,98},{3,35},{4,100},{5,37},{6,102},{7,39},{8,104},... | collective-permute-start | bytes 1277960 | tf_op jit(solution)/shard_map/ppermute | solution.py:63
  24.3 3.0 %collective-permute-start.6 = (bf16[8,192,128]{2,1,0:T(8,128)(2,1)S(1)}, bf16[8,192,128]{2,1,0:T(8,128)(2,1)S(1)}, u32[]{:S(2)}, u32[]{:S(2)}) collective-permute-start(bf16[8,192,128]{2,1,0:T(8,128)(2,1)S(1)} %get-tuple-element.152), channel_id=1, source_target_pairs={{0,6},{1,3},{2,4},{3,1},{4,2},{5,7},{6,0},{7,5},{8,14},{9,11},{10,... | collective-permute-start | bytes 1179656 | tf_op jit(solution)/shard_map/ppermute | solution.py:63
  27.3 2.0 collective-permute-done.3
  29.4 2.8 %collective-permute-start.4 = (bf16[16,192,128]{2,1,0:T(8,128)(2,1)S(1)}, bf16[16,192,128]{2,1,0:T(8,128)(2,1)S(1)}, u32[]{:S(2)}, u32[]{:S(2)}) collective-permute-start(bf16[16,192,128]{2,1,0:T(8,128)(2,1)S(1)} %pad_maximum_fusion.4), channel_id=1, source_target_pairs={{0,6},{1,3},{2,4},{3,1},{4,2},{5,7},{6,0},{7,5},{8,14},{9,11},{10,... | collective-permute-start | bytes 2359304 | tf_op jit(solution)/shard_map/ppermute | solution.py:63
  32.2 1.8 collective-permute-start.1
  34.1 2.5 %collective-permute-start.7 = (bf16[16,192,128]{2,1,0:T(8,128)(2,1)S(1)}, bf16[16,192,128]{2,1,0:T(8,128)(2,1)S(1)}, u32[]{:S(2)}, u32[]{:S(2)}) collective-permute-start(bf16[16,192,128]{2,1,0:T(8,128)(2,1)S(1)} %pad_maximum_fusion.5), channel_id=1, source_target_pairs={{0,96},{1,33},{2,98},{3,35},{4,100},{5,37},{6,102},{7,39},{8,104},... | collective-permute-start | bytes 2359304 | tf_op jit(solution)/shard_map/ppermute | solution.py:63
  36.6 6.0 %collective-permute-done.4 = bf16[16,192,128]{2,1,0:T(8,128)(2,1)S(1)} collective-permute-done((bf16[16,192,128]{2,1,0:T(8,128)(2,1)S(1)}, bf16[16,192,128]{2,1,0:T(8,128)(2,1)S(1)}, u32[]{:S(2)}, u32[]{:S(2)}) %collective-permute-start.4) | collective-permute-done | bytes 786464 | tf_op jit(solution)/shard_map/ppermute | solution.py:63
  42.6 0.2 pad_maximum_fusion.1.refs_2_
  42.8 1.7 collective-permute-start.5
  44.6 1.6 collective-permute-done.1
  46.2 0.2 pad_maximum_fusion.refs_0_
  46.4 2.1 collective-permute-start.2
  48.5 1.3 pad_maximum_fusion.2.refs_4_
  49.8 1.5 collective-permute-start.8
  51.3 0.6 fusion.19
  53.2 0.6 fusion.18
  55.2 0.6 copy.14
  55.9 0.7 concatenate.40.tab
  56.6 8.7 %flip.1 = (bf16[2,4,192,1024]{3,2,1,0:T(8,128)(2,1)}, bf16[4,2,192,1024]{3,2,1,0:T(8,128)(2,1)}, bf16[2,4,192,1024]{3,2,1,0:T(8,128)(2,1)}) custom-call(bf16[512,4608]{1,0:T(8,128)(2,1)} %w.3, bf16[512,4608]{1,0:T(8,128)(2,1)} %collective-permute-done.9.other_ref.refs_7_), custom_call_target="tpu_custom_call" | custom-call | bytes 18874368 | tf_op jit(solution)/shard_map/flip/pallas_call | solution.py:137
  65.3 6.5 %collective-permute-done.8.refs_5_ = bf16[32,192,128]{2,1,0:T(8,128)(2,1)} collective-permute-done((bf16[32,192,128]{2,1,0:T(8,128)(2,1)}, bf16[32,192,128]{2,1,0:T(8,128)(2,1)}, u32[]{:S(2)}, u32[]{:S(2)}) %collective-permute-start.8) | collective-permute-done | bytes 1572896 | tf_op jit(solution)/shard_map/ppermute | solution.py:63
  71.8 24.6 %act.1 = (f32[4,1024,256]{2,1,0:T(8,128)}, f32[4,1,256]{2,1,0:T(1,128)}, f32[4,1,256]{2,1,0:T(1,128)}, f32[64,16,128]{2,1,0:T(8,128)}, bf16[4,4608,256]{2,1,0:T(8,128)(2,1)}) custom-call(s32[26]{0:T(128)} %concatenate.40.tab, bf16[32,208,128]{2,1,0:T(8,128)(2,1)} %copy-done.8, bf16[32,208,128]{2,1,0:T(8,128)(2,1)} %collective-permute-done.2.refs_1_, ...), custom_call_target="tpu_custom_call" | custom-call | flops 9663676416 | bytes 30000000 | tf_op jit(solution)/shard_map/act/pallas_call | solution.py:290
  96.5 20.5 %all_to_all.16.totals_ref = f32[64,16,128]{2,1,0:T(8,128)} all-to-all(f32[64,16,128]{2,1,0:T(8,128)} %get-tuple-element.89), channel_id=1, replica_groups=mesh['x'=4,'ylo'=2,'yhi'=2,'z'=4,'core'=2] {'x','ylo','yhi','z'}, dimensions={0} | all-to-all | bytes 1048576 | tf_op jit(solution)/shard_map/all_to_all | solution.py:609
  117.0 11.8 %grad.1 = (bf16[4,512,256]{2,1,0:T(8,128)(2,1)}, bf16[4,512,256]{2,1,0:T(8,128)(2,1)}, bf16[4,1024,256]{2,1,0:T(8,128)(2,1)}, bf16[2,2,1024,256]{3,2,1,0:T(8,128...) custom-call(s32[26]{0:T(128)} %concatenate.40.tab, ...), custom_call_target="tpu_custom_call" | custom-call | flops 4831838208 | bytes 24000000 | tf_op jit(solution)/shard_map/grad/pallas_call | solution.py:471
  128.8 1.5 collective-permute-start.10
  130.4 0.8 collective-permute-start.11
  131.2 1.0 collective-permute-start.12
  132.1 10.0 %keep.1 = (bf16[32,192,128]{2,1,0:T(8,128)(2,1)}, bf16[32,192,128]{2,1,0:T(8,128)(2,1)}, bf16[32,192,128]{2,1,0:T(8,128)(2,1)}) custom-call(s32[26]{0:T(128)} %concatenate.40.tab, bf16[4,1024,256]{2,1,0:T(8,128)(2,1)} %get-tuple-element.99.gz_ref, bf16[2,2,1024,256]{3,2,1,0:T(8,128)(2,1)} %get-tuple-element.100.gy_ref, ...), custom_call_target="tpu_custom_call" | custom-call | flops 4718592 | bytes 1000000 | tf_op jit(solution)/shard_map/keep/pallas_call | solution.py:488
  142.2 11.7 %head.2 = (bf16[512,4608]{1,0:T(8,128)(2,1)}, f32[4,6,128]{2,1,0:T(8,128)}) custom-call(bf16[4,512,256]{2,1,0:T(8,128)(2,1)} %get-tuple-element.130.own_gr, bf16[4,512,256]{2,1,0:T(8,128)(2,1)} %collective-permute-done.13.twin_gr, bf16[4,4608,256]{2,1,0:T(8,128)(2,1)} %get-tuple-element.111.own_xt, bf16[4,4608,256]{2,1,0:T(8,128)(2,1)} %collective-permute-done.14.twin_xt, ...), custom_call_target="tpu_custom_call" | custom-call | flops 4718592 | bytes 1000000 | tf_op jit(solution)/shard_map/head/pallas_call | solution.py:525
  153.9 1.1 copy-done.2
  155.0 0.5 copy-done.3
  155.6 3.6 %sum2.1 = (bf16[16,192,128]{2,1,0:T(8,128)(2,1)}, bf16[16,192,128]{2,1,0:T(8,128)(2,1)}, bf16[16,192,128]{2,1,0:T(8,128)(2,1)}) custom-call(bf16[32,192,128]{2,1,0:T(8,128)(2,1)} %get-tuple-element.114.refs_0_, bf16[32,192,128]{2,1,0:T(8,128)(2,1)} %copy-done.2, bf16[32,192,128]{2,1,0:T(8,128)(2,1)} %get-tuple-element.116.refs_2_.refs_3_.refs_4_, ...), custom_call_target="tpu_custom_call" | custom-call | flops 4194304 | bytes 6000000 | tf_op jit(solution)/shard_map/sum2/pallas_call | solution.py:570
  159.1 2.4 %collective-permute-start.15 = (bf16[16,192,128]{2,1,0:T(8,128)(2,1)}, bf16[16,192,128]{2,1,0:T(8,128)(2,1)S(1)}, u32[]{:S(2)}, u32[]{:S(2)}) collective-permute-start(bf16[16,192,128]{2,1,0:T(8,128)(2,1)} %get-tuple-element.126), channel_id=1, source_target_pairs={{0,24},{1,17},{2,26},{3,19},{4,28},{5,21},{6,30},{7,23},{8,16},{9,... | collective-permute-start | bytes 2359304 | tf_op jit(solution)/shard_map/ppermute | solution.py:63
  161.5 2.0 collective-permute-start.16
  163.5 2.2 %collective-permute-start.17 = (bf16[16,192,128]{2,1,0:T(8,128)(2,1)}, bf16[16,192,128]{2,1,0:T(8,128)(2,1)S(1)}, u32[]{:S(2)}, u32[]{:S(2)}) collective-permute-start(bf16[16,192,128]{2,1,0:T(8,128)(2,1)} %get-tuple-element.128), channel_id=1, source_target_pairs={{0,96},{1,33},{2,98},{3,35},{4,100},{5,37},{6,102},{7,39},{8,104},... | collective-permute-start | bytes 2359304 | tf_op jit(solution)/shard_map/ppermute | solution.py:63
  165.7 7.3 %head.3 = (bf16[512,4608]{1,0:T(8,128)(2,1)}, f32[2,6,128]{2,1,0:T(8,128)}) custom-call(bf16[4,512,256]{2,1,0:T(8,128)(2,1)} %get-tuple-element.130.own_gr, bf16[4,512,256]{2,1,0:T(8,128)(2,1)} %collective-permute-done.13.twin_gr, bf16[4,4608,256]{2,1,0:T(8,128)(2,1)} %get-tuple-element.111.own_xt, ...), custom_call_target="tpu_custom_call", output_to_operand_aliasing={{0}: (5, {})} | custom-call | flops 4718592 | bytes 1000000 | tf_op jit(solution)/shard_map/head/pallas_call | solution.py:525
  173.0 0.7 constant_dynamic-update-slice_fusion
  173.7 1.1 collective-permute-start.18
  174.8 4.0 %collective-permute-done.18 = f32[6,6,128]{2,1,0:T(8,128)S(1)} collective-permute-done((f32[6,6,128]{2,1,0:T(8,128)S(1)}, f32[6,6,128]{2,1,0:T(8,128)S(1)}, u32[]{:S(2)}, u32[]{:S(2)}) %collective-permute-start.18) | collective-permute-done | bytes 18464 | tf_op jit(solution)/shard_map/ppermute | solution.py:63
  178.8 1.1 collective-permute-start.19
  180.0 0.3 copy-done.6
  180.2 3.0 %sum3.1 = (bf16[8,192,128]{2,1,0:T(8,128)(2,1)}, bf16[8,192,128]{2,1,0:T(8,128)(2,1)}, bf16[8,192,128]{2,1,0:T(8,128)(2,1)}) custom-call(bf16[32,192,128]{2,1,0:T(8,128)(2,1)} %get-tuple-element.114.refs_0_, bf16[32,192,128]{2,1,0:T(8,128)(2,1)} %copy-done.2, bf16[16,192,128]{2,1,0:T(8,128)(2,1)} %copy-done.4, ...), custom_call_target="tpu_custom_call" | custom-call | flops 4194304 | bytes 6000000 | tf_op jit(solution)/shard_map/sum3/pallas_call | solution.py:570
  183.3 0.7 collective-permute-done.19
  183.9 1.3 collective-permute-start.20
  185.3 1.1 collective-permute-start.21
  186.3 0.8 collective-permute-start.22
  187.2 2.4 %collective-permute-start.23 = (f32[6,6,128]{2,1,0:T(8,128)S(1)}, f32[6,6,128]{2,1,0:T(8,128)S(1)}, u32[]{:S(2)}, u32[]{:S(2)}) collective-permute-start(f32[6,6,128]{2,1,0:T(8,128)S(1)} %add.110), channel_id=1, source_target_pairs={{0,6},{1,3},{2,4},{3,1},{4,2},{5,7},{6,0},{7,5},{8,14},{9,11},{10,... | collective-permute-start | bytes 55304 | tf_op jit(solution)/shard_map/ppermute | solution.py:63
  189.7 6.1 %collective-permute-done.23 = f32[6,6,128]{2,1,0:T(8,128)S(1)} collective-permute-done((f32[6,6,128]{2,1,0:T(8,128)S(1)}, f32[6,6,128]{2,1,0:T(8,128)S(1)}, u32[]{:S(2)}, u32[]{:S(2)}) %collective-permute-start.23) | collective-permute-done | bytes 18464 | tf_op jit(solution)/shard_map/ppermute | solution.py:63
  195.9 0.1 multiply_reduce_fusion
  196.2 0.6 slice.82.refs_12_
  196.8 3.6 %sum4.1 = bf16[8,592,128]{2,1,0:T(8,128)(2,1)} custom-call(bf16[32,192,128]{2,1,0:T(8,128)(2,1)} %get-tuple-element.114.refs_0_, bf16[32,192,128]{2,1,0:T(8,128)(2,1)} %copy-done.2, bf16[16,192,128]{2,1,0:T(8,128)(2,1)} %copy-done.4, bf16[8,192,128]{2,1,0:T(8,128)(2,1)} %copy-done.11, bf16[32,192,128]{2,1,0:T(8,128)(2,1)} %get-tuple-element.116.refs_2_.refs_3_.refs_4_, ...), custom_call_target="tpu_custom_call" | custom-call | flops 4194304 | bytes 6000000 | tf_op jit(solution)/shard_map/sum4/pallas_call | solution.py:570
  200.4 3.7 %all-to-all-start.2 = ((bf16[8,592,128]{2,1,0:T(8,128)(2,1)}), bf16[8,592,128]{2,1,0:T(8,128)(2,1)S(1)}, u32[]{:S(2)}, u32[]{:S(2)}) async-start(bf16[8,592,128]{2,1,0:T(8,128)(2,1)} %sum4.1), calls=%async_computation.2 | async-start | bytes 2424832 | tf_op jit(solution)/shard_map/all_to_all | solution.py:67
  204.2 0.7 fusion.16
  204.9 1.2 multiply_bitcast_fusion
  206.1 9.1 %all-to-all-done.2 = bf16[8,592,128]{2,1,0:T(8,128)(2,1)S(1)} async-done(((bf16[8,592,128]{2,1,0:T(8,128)(2,1)}), bf16[8,592,128]{2,1,0:T(8,128)(2,1)S(1)}, u32[]{:S(2)}, u32[]{:S(2)}) %all-to-all-start.2) | async-done | bytes 1212448 | tf_op jit(solution)/shard_map/all_to_all | solution.py:67
  215.2 0.2 convert_reduce_fusion
  215.5 0.8 fusion.6
  216.4 0.3 collective-permute-done.24
  216.7 0.6 add_divide_fusion
  (79 shorter events, 1.3 us)
Async XLA Ops:
  0.6 54.5 %copy-start = (s32[2048]{0:T(1024)S(1)}, s32[2048]{0:T(1024)}, u32[]{:S(2)}) copy-start(s32[2048]{0:T(1024)} %param.7) | copy-start | bytes 24580
  0.6 56.0 %collective-permute-start.9 = (bf16[512,4608]{1,0:T(8,128)(2,1)}, bf16[512,4608]{1,0:T(8,128)(2,1)}, u32[]{:S(2)}, u32[]{:S(2)}) collective-permute-start(bf16[512,4608]{1,0:T(8,128)(2,1)} %w.3), channel_id=1, source_target_pairs={{0,1},{1,0},{2,3},{3,2},{4,5},{5,4},{6,7},{7,6},{8,9},{9,8},{10,11... | collective-permute-start | bytes 14155784 | tf_op jit(solution)/shard_map/ppermute | solution.py:63
  19.8 9.5 %collective-permute-start.3 = (bf16[8,192,128]{2,1,0:T(8,128)(2,1)S(1)}, bf16[8,192,128]{2,1,0:T(8,128)(2,1)S(1)}, u32[]{:S(2)}, u32[]{:S(2)}) collective-permute-start(bf16[8,192,128]{2,1,0:T(8,128)(2,1)S(1)} %get-tuple-element.153), channel_id=1, source_target_pairs={{0,24},{1,17},{2,26},{3,19},{4,28},{5,21},{6,30},{7,23},{8,16},{9,... | collective-permute-start | bytes 1179656 | tf_op jit(solution)/shard_map/ppermute | solution.py:63
  22.1 10.1 %collective-permute-start = (bf16[8,208,128]{2,1,0:T(8,128)(2,1)S(1)}, bf16[8,208,128]{2,1,0:T(8,128)(2,1)S(1)}, u32[]{:S(2)}, u32[]{:S(2)}) collective-permute-start(bf16[8,208,128]{2,1,0:T(8,128)(2,1)S(1)} %slice.78), channel_id=1, source_target_pairs={{0,96},{1,33},{2,98},{3,35},{4,100},{5,37},{6,102},{7,39},{8,104},... | collective-permute-start | bytes 1277960 | tf_op jit(solution)/shard_map/ppermute | solution.py:63
  24.3 9.8 %collective-permute-start.6 = (bf16[8,192,128]{2,1,0:T(8,128)(2,1)S(1)}, bf16[8,192,128]{2,1,0:T(8,128)(2,1)S(1)}, u32[]{:S(2)}, u32[]{:S(2)}) collective-permute-start(bf16[8,192,128]{2,1,0:T(8,128)(2,1)S(1)} %get-tuple-element.152), channel_id=1, source_target_pairs={{0,6},{1,3},{2,4},{3,1},{4,2},{5,7},{6,0},{7,5},{8,14},{9,11},{10,... | collective-permute-start | bytes 1179656 | tf_op jit(solution)/shard_map/ppermute | solution.py:63
  29.4 13.3 %collective-permute-start.4 = (bf16[16,192,128]{2,1,0:T(8,128)(2,1)S(1)}, bf16[16,192,128]{2,1,0:T(8,128)(2,1)S(1)}, u32[]{:S(2)}, u32[]{:S(2)}) collective-permute-start(bf16[16,192,128]{2,1,0:T(8,128)(2,1)S(1)} %pad_maximum_fusion.4), channel_id=1, source_target_pairs={{0,6},{1,3},{2,4},{3,1},{4,2},{5,7},{6,0},{7,5},{8,14},{9,11},{10,... | collective-permute-start | bytes 2359304 | tf_op jit(solution)/shard_map/ppermute | solution.py:63
  32.2 14.0 %collective-permute-start.1 = (bf16[16,208,128]{2,1,0:T(8,128)(2,1)S(1)}, bf16[16,208,128]{2,1,0:T(8,128)(2,1)S(1)}, u32[]{:S(2)}, u32[]{:S(2)}) collective-permute-start(bf16[16,208,128]{2,1,0:T(8,128)(2,1)S(1)} %pad_maximum_fusion.3), channel_id=1, source_target_pairs={{0,24},{1,17},{2,26},{3,19},{4,28},{5,21},{6,30},{7,23},{8,16},{9,... | collective-permute-start | bytes 2555912 | tf_op jit(solution)/shard_map/ppermute | solution.py:63
  34.1 14.4 %collective-permute-start.7 = (bf16[16,192,128]{2,1,0:T(8,128)(2,1)S(1)}, bf16[16,192,128]{2,1,0:T(8,128)(2,1)S(1)}, u32[]{:S(2)}, u32[]{:S(2)}) collective-permute-start(bf16[16,192,128]{2,1,0:T(8,128)(2,1)S(1)} %pad_maximum_fusion.5), channel_id=1, source_target_pairs={{0,96},{1,33},{2,98},{3,35},{4,100},{5,37},{6,102},{7,39},{8,104},... | collective-permute-start | bytes 2359304 | tf_op jit(solution)/shard_map/ppermute | solution.py:63
  42.8 3.6 %copy-start.9 = (bf16[32,192,128]{2,1,0:T(8,128)(2,1)}, bf16[32,192,128]{2,1,0:T(8,128)(2,1)S(1)}, u32[]{:S(2)}) copy-start(bf16[32,192,128]{2,1,0:T(8,128)(2,1)S(1)} %pad_maximum_fusion.1.refs_2_) | copy-start | bytes 4718596
  42.8 22.5 %collective-permute-start.5 = (bf16[32,192,128]{2,1,0:T(8,128)(2,1)S(1)}, bf16[32,192,128]{2,1,0:T(8,128)(2,1)}, u32[]{:S(2)}, u32[]{:S(2)}) collective-permute-start(bf16[32,192,128]{2,1,0:T(8,128)(2,1)S(1)} %pad_maximum_fusion.1.refs_2_), channel_id=1, source_target_pairs={{0,96},{1,33},{2,98},{3,35},{4,100},{5,37},{6,102},{7,39},{8,104},... | collective-permute-start | bytes 4718600 | tf_op jit(solution)/shard_map/ppermute | solution.py:63
  46.4 5.0 %copy-start.8 = (bf16[32,208,128]{2,1,0:T(8,128)(2,1)}, bf16[32,208,128]{2,1,0:T(8,128)(2,1)S(1)}, u32[]{:S(2)}) copy-start(bf16[32,208,128]{2,1,0:T(8,128)(2,1)S(1)} %pad_maximum_fusion.refs_0_) | copy-start | bytes 5111812
  46.4 25.4 %collective-permute-start.2 = (bf16[32,208,128]{2,1,0:T(8,128)(2,1)S(1)}, bf16[32,208,128]{2,1,0:T(8,128)(2,1)}, u32[]{:S(2)}, u32[]{:S(2)}) collective-permute-start(bf16[32,208,128]{2,1,0:T(8,128)(2,1)S(1)} %pad_maximum_fusion.refs_0_), channel_id=1, source_target_pairs={{0,6},{1,3},{2,4},{3,1},{4,2},{5,7},{6,0},{7,5},{8,14},{9,11},{10,... | collective-permute-start | bytes 5111816 | tf_op jit(solution)/shard_map/ppermute | solution.py:63
  49.8 21.9 %collective-permute-start.8 = (bf16[32,192,128]{2,1,0:T(8,128)(2,1)}, bf16[32,192,128]{2,1,0:T(8,128)(2,1)}, u32[]{:S(2)}, u32[]{:S(2)}) collective-permute-start(bf16[32,192,128]{2,1,0:T(8,128)(2,1)} %pad_maximum_fusion.2.refs_4_), channel_id=1, source_target_pairs={{0,24},{1,17},{2,26},{3,19},{4,28},{5,21},{6,30},{7,23},{8,16},{9,... | collective-permute-start | bytes 4718600 | tf_op jit(solution)/shard_map/ppermute | solution.py:63
  96.4 45.8 %collective-permute-start.14 = (bf16[4,4608,256]{2,1,0:T(8,128)(2,1)}, bf16[4,4608,256]{2,1,0:T(8,128)(2,1)}, u32[]{:S(2)}, u32[]{:S(2)}) collective-permute-start(bf16[4,4608,256]{2,1,0:T(8,128)(2,1)} %get-tuple-element.111.own_xt), channel_id=1, source_target_pairs={{0,1},{1,0},{2,3},{3,2},{4,5},{5,4},{6,7},{7,6},{8,9},{9,8},{10,11... | collective-permute-start | bytes 28311560 | tf_op jit(solution)/shard_map/ppermute | solution.py:63
  128.8 25.0 %collective-permute-start.10 = (bf16[32,192,128]{2,1,0:T(8,128)(2,1)}, bf16[32,192,128]{2,1,0:T(8,128)(2,1)S(1)}, u32[]{:S(2)}, u32[]{:S(2)}) collective-permute-start(bf16[32,192,128]{2,1,0:T(8,128)(2,1)} %get-tuple-element.96), channel_id=1, source_target_pairs={{0,6},{1,3},{2,4},{3,1},{4,2},{5,7},{6,0},{7,5},{8,14},{9,11},{10,... | collective-permute-start | bytes 4718600 | tf_op jit(solution)/shard_map/ppermute | solution.py:63
  130.4 23.5 %collective-permute-start.11 = (bf16[32,192,128]{2,1,0:T(8,128)(2,1)}, bf16[32,192,128]{2,1,0:T(8,128)(2,1)S(1)}, u32[]{:S(2)}, u32[]{:S(2)}) collective-permute-start(bf16[32,192,128]{2,1,0:T(8,128)(2,1)} %get-tuple-element.97), channel_id=1, source_target_pairs={{0,96},{1,33},{2,98},{3,35},{4,100},{5,37},{6,102},{7,39},{8,104},... | collective-permute-start | bytes 4718600 | tf_op jit(solution)/shard_map/ppermute | solution.py:63
  131.2 22.7 %collective-permute-start.12 = (bf16[32,192,128]{2,1,0:T(8,128)(2,1)}, bf16[32,192,128]{2,1,0:T(8,128)(2,1)}, u32[]{:S(2)}, u32[]{:S(2)}) collective-permute-start(bf16[32,192,128]{2,1,0:T(8,128)(2,1)} %get-tuple-element.98), channel_id=1, source_target_pairs={{0,24},{1,17},{2,26},{3,19},{4,28},{5,21},{6,30},{7,23},{8,16},{9,... | collective-permute-start | bytes 4718600 | tf_op jit(solution)/shard_map/ppermute | solution.py:63
  132.1 10.0 %collective-permute-start.13 = (bf16[4,512,256]{2,1,0:T(8,128)(2,1)}, bf16[4,512,256]{2,1,0:T(8,128)(2,1)}, u32[]{:S(2)}, u32[]{:S(2)}) collective-permute-start(bf16[4,512,256]{2,1,0:T(8,128)(2,1)} %get-tuple-element.105), channel_id=1, source_target_pairs={{0,1},{1,0},{2,3},{3,2},{4,5},{5,4},{6,7},{7,6},{8,9},{9,8},{10,11... | collective-permute-start | bytes 3145736 | tf_op jit(solution)/shard_map/ppermute | solution.py:63
  153.8 1.2 copy-start.2
  153.9 1.7 copy-start.3
  159.1 13.9 %copy-start.14 = (f32[4,6,128]{2,1,0:T(8,128)S(1)}, f32[4,6,128]{2,1,0:T(8,128)}, u32[]{:S(2)}) copy-start(f32[4,6,128]{2,1,0:T(8,128)} %get-tuple-element.129) | copy-start | bytes 36868
  159.1 19.6 %collective-permute-start.15 = (bf16[16,192,128]{2,1,0:T(8,128)(2,1)}, bf16[16,192,128]{2,1,0:T(8,128)(2,1)S(1)}, u32[]{:S(2)}, u32[]{:S(2)}) collective-permute-start(bf16[16,192,128]{2,1,0:T(8,128)(2,1)} %get-tuple-element.126), channel_id=1, source_target_pairs={{0,24},{1,17},{2,26},{3,19},{4,28},{5,21},{6,30},{7,23},{8,16},{9,... | collective-permute-start | bytes 2359304 | tf_op jit(solution)/shard_map/ppermute | solution.py:63
  161.5 17.3 %collective-permute-start.16 = (bf16[16,192,128]{2,1,0:T(8,128)(2,1)}, bf16[16,192,128]{2,1,0:T(8,128)(2,1)S(1)}, u32[]{:S(2)}, u32[]{:S(2)}) collective-permute-start(bf16[16,192,128]{2,1,0:T(8,128)(2,1)} %get-tuple-element.127), channel_id=1, source_target_pairs={{0,6},{1,3},{2,4},{3,1},{4,2},{5,7},{6,0},{7,5},{8,14},{9,11},{10,... | collective-permute-start | bytes 2359304 | tf_op jit(solution)/shard_map/ppermute | solution.py:63
  163.5 15.3 %collective-permute-start.17 = (bf16[16,192,128]{2,1,0:T(8,128)(2,1)}, bf16[16,192,128]{2,1,0:T(8,128)(2,1)S(1)}, u32[]{:S(2)}, u32[]{:S(2)}) collective-permute-start(bf16[16,192,128]{2,1,0:T(8,128)(2,1)} %get-tuple-element.128), channel_id=1, source_target_pairs={{0,96},{1,33},{2,98},{3,35},{4,100},{5,37},{6,102},{7,39},{8,104},... | collective-permute-start | bytes 2359304 | tf_op jit(solution)/shard_map/ppermute | solution.py:63
  173.7 5.0 %collective-permute-start.18 = (f32[6,6,128]{2,1,0:T(8,128)S(1)}, f32[6,6,128]{2,1,0:T(8,128)S(1)}, u32[]{:S(2)}, u32[]{:S(2)}) collective-permute-start(f32[6,6,128]{2,1,0:T(8,128)S(1)} %constant_dynamic-update-slice_fusion), channel_id=1, source_target_pairs={{0,24},{1,17},{2,26},{3,19},{4,28},{5,21},{6,30},{7,23},{8,16},{9,... | collective-permute-start | bytes 55304 | tf_op jit(solution)/shard_map/ppermute | solution.py:63
  178.8 1.2 copy-start.4
  178.8 1.2 copy-start.5
  178.8 1.4 copy-start.6
  178.8 5.1 %collective-permute-start.19 = (f32[6,6,128]{2,1,0:T(8,128)S(1)}, f32[6,6,128]{2,1,0:T(8,128)S(1)}, u32[]{:S(2)}, u32[]{:S(2)}) collective-permute-start(f32[6,6,128]{2,1,0:T(8,128)S(1)} %add.109), channel_id=1, source_target_pairs={{0,96},{1,33},{2,98},{3,35},{4,100},{5,37},{6,102},{7,39},{8,104},... | collective-permute-start | bytes 55304 | tf_op jit(solution)/shard_map/ppermute | solution.py:63
  183.9 11.9 %collective-permute-start.20 = (bf16[8,192,128]{2,1,0:T(8,128)(2,1)}, bf16[8,192,128]{2,1,0:T(8,128)(2,1)S(1)}, u32[]{:S(2)}, u32[]{:S(2)}) collective-permute-start(bf16[8,192,128]{2,1,0:T(8,128)(2,1)} %get-tuple-element.141), channel_id=1, source_target_pairs={{0,96},{1,33},{2,98},{3,35},{4,100},{5,37},{6,102},{7,39},{8,104},... | collective-permute-start | bytes 1179656 | tf_op jit(solution)/shard_map/ppermute | solution.py:63
  185.3 10.5 %collective-permute-start.21 = (bf16[8,192,128]{2,1,0:T(8,128)(2,1)}, bf16[8,192,128]{2,1,0:T(8,128)(2,1)S(1)}, u32[]{:S(2)}, u32[]{:S(2)}) collective-permute-start(bf16[8,192,128]{2,1,0:T(8,128)(2,1)} %get-tuple-element.142), channel_id=1, source_target_pairs={{0,24},{1,17},{2,26},{3,19},{4,28},{5,21},{6,30},{7,23},{8,16},{9,... | collective-permute-start | bytes 1179656 | tf_op jit(solution)/shard_map/ppermute | solution.py:63
  186.3 9.5 %collective-permute-start.22 = (bf16[8,192,128]{2,1,0:T(8,128)(2,1)}, bf16[8,192,128]{2,1,0:T(8,128)(2,1)S(1)}, u32[]{:S(2)}, u32[]{:S(2)}) collective-permute-start(bf16[8,192,128]{2,1,0:T(8,128)(2,1)} %get-tuple-element.143), channel_id=1, source_target_pairs={{0,6},{1,3},{2,4},{3,1},{4,2},{5,7},{6,0},{7,5},{8,14},{9,11},{10,... | collective-permute-start | bytes 1179656 | tf_op jit(solution)/shard_map/ppermute | solution.py:63
  187.2 8.6 %collective-permute-start.23 = (f32[6,6,128]{2,1,0:T(8,128)S(1)}, f32[6,6,128]{2,1,0:T(8,128)S(1)}, u32[]{:S(2)}, u32[]{:S(2)}) collective-permute-start(f32[6,6,128]{2,1,0:T(8,128)S(1)} %add.110), channel_id=1, source_target_pairs={{0,6},{1,3},{2,4},{3,1},{4,2},{5,7},{6,0},{7,5},{8,14},{9,11},{10,... | collective-permute-start | bytes 55304 | tf_op jit(solution)/shard_map/ppermute | solution.py:63
  195.8 1.0 copy-start.11
  195.8 1.0 copy-start.12
  195.8 1.0 copy-start.13
  200.4 4.5 %copy-start.7 = (f32[64,16,128]{2,1,0:T(8,128)S(1)}, f32[64,16,128]{2,1,0:T(8,128)}, u32[]{:S(2)}) copy-start(f32[64,16,128]{2,1,0:T(8,128)} %all_to_all.16.totals_ref) | copy-start | bytes 1572868
  200.4 14.8 %all-to-all-start.2 = ((bf16[8,592,128]{2,1,0:T(8,128)(2,1)}), bf16[8,592,128]{2,1,0:T(8,128)(2,1)S(1)}, u32[]{:S(2)}, u32[]{:S(2)}) async-start(bf16[8,592,128]{2,1,0:T(8,128)(2,1)} %sum4.1), calls=%async_computation.2 | async-start | bytes 2424832 | tf_op jit(solution)/shard_map/all_to_all | solution.py:67
  204.1 11.4 %copy-start.10 = (bf16[128,576]{0,1:T(8,128)(2,1)S(1)}, bf16[128,576]{0,1:T(8,128)(2,1)}, u32[]{:S(2)}) copy-start(bf16[128,576]{0,1:T(8,128)(2,1)} %param.4) | copy-start | bytes 442372
  204.1 12.5 %copy-start.15 = (bf16[576]{0:T(1024)(128)(2,1)S(1)}, bf16[576]{0:T(1024)(128)(2,1)}, u32[]{:S(2)}) copy-start(bf16[576]{0:T(1024)(128)(2,1)} %param.5) | copy-start | bytes 3460
  204.2 13.1 %copy-start.1 = (s32[2048]{0:T(1024)S(1)}, s32[2048]{0:T(1024)}, u32[]{:S(2)}) copy-start(s32[2048]{0:T(1024)} %param.7) | copy-start | bytes 24580
  215.4 1.2 collective-permute-start.24

commit v3 on v2

--- a/solution.py
+++ b/solution.py
@@ -83,10 +83,6 @@
     early = [place & 1 for place in places]
     first, second, _ = ORDER[part]
     return (late[second] * 2 + late[first]) * 8 + early[0] * 4 + early[1] * 2 + early[2]
-
-
-def total(arrays):
-    return functools.reduce(lambda a, b: a + b, [a.astype(F32) for a in arrays])
 
 
 def split3(v):
@@ -230,7 +226,7 @@
     z = at_of(tab, 2, step)
     rinv_ref[z] = rinv
     tgt = tgt_ref[z]
-    rows = 32
+    rows = 64
     zeros = jnp.zeros((8, 2 * TB), F32)
     sums = (zeros,) * 3
     inside = jnp.zeros((1, 2 * TB), jnp.bool_)
@@ -541,7 +537,7 @@
     ins, outs = refs[: 3 * terms], refs[3 * terms :]
     for p in range(3):
         blocks = [a[...] for a in ins[terms * p : terms * (p + 1)]]
-        got = blocks[0] + blocks[1] if terms == 2 else total(blocks).astype(BF)
+        got = functools.reduce(lambda a, b: a + b, blocks)
         if len(outs) == 3:
             outs[p][...] = got
         else:
@@ -605,8 +601,9 @@
     halves, turned, tgt, tab, owner = lax.optimization_barrier((halves, turned, tgt, tab, owner))
 
     expo, bend, rinv, stats, xt_all = act_call(tab, halves, head_weight, other, tgt)
+    stats = lax.all_to_all(stats, AX[:4], 0, 0)
+    stats, xt_all = lax.optimization_barrier((stats, xt_all))
     xts = (xt_all, send(xt_all, TWIN))
-    stats = lax.all_to_all(stats, AX[:4], 0, 0)
 
     own_gr, other_gr, gz, gy, *away = grad_call(tab, expo, bend, stats, rinv, tgt, turned)
 

time: 219 us -> 216 us (0.986)
  no operation moved by 1% of the time
where the time goes in v3:
time: 216 us; the launch traced here: 215 us
  Pallas kernels  83.9 us (39%)
  starting transfers between devices  41.5 us (19%)
  waiting for transfers between devices  36.4 us (17%)
  blocking collectives  35.4 us (16%)
  local copies, waits for them, and re-layouts  7.17 us (3%)
  other arithmetic  6.75 us (3%)
  between operations  3.7 us (2%)
    ppermute x25, starting transfers between devices, send(): return lax.ppermute(a, AX, pairs)  37.8 us
    ppermute x25, waiting for transfers between devices, send(): return lax.ppermute(a, AX, pairs)  27.3 us
    pallas_call x1, Pallas kernels, act_call(): pl.pallas_call(act_kernel, grid_spec=pltpu.PrefetchScalarGridSpec(num_sca...  24.3 us
    pallas_call x2, Pallas kernels, head_call(): pl.pallas_call(head_kernel, grid=(count,), in_specs=[rows, rows, tokens,...  19 us
    all_to_all x1, blocking collectives, shards(): stats = lax.all_to_all(stats, AX[:4], 0, 0)  18.5 us
    all_to_all x1, blocking collectives, in_cube(): return lax.all_to_all(a, AX, 0, 0, axis_index_groups=CUBES)  16.9 us
    pallas_call x1, Pallas kernels, grad_call(): pl.pallas_call(grad_kernel, in_specs=[SMEM_SPEC, ANYWHERE] + [VMEM_SPEC]...  11.8 us
    pallas_call x3, Pallas kernels, sum_call(): pl.pallas_call(functools.partial(sum_kernel, terms), grid=(count // step,...  10.2 us
  transfers between devices with their start and end apart: 26, of which 9 were waited for; matrix products, arithmetic and copies ran while one was open for 5% of the time, Pallas kernels for 24%

profile of v3, /device:TPU:0, one launch (start us, length us, event | category | flops | bytes accessed | tf_op | source)
XLA Modules:
  0.0 214.8 jit_solution(14877232754821385007)
XLA Ops:
  0.7 0.7 convert_element_type.74
  1.4 1.1 fusion.1
  2.5 0.2 concatenate.33
  2.7 0.2 broadcast_in_dim.5
  2.9 16.9 %all_to_all.15 = bf16[8,592,128]{2,1,0:T(8,128)(2,1)S(1)} all-to-all(bf16[8,592,128]{2,1,0:T(8,128)(2,1)S(1)} %broadcast_in_dim.5), channel_id=1, replica_groups={{0,2,16,18,32,34,48,50},{6,4,22,20,38,36,54,52},{24,26,8,10,56,58,40,42..., dimensions={0} | all-to-all | bytes 2424832 | tf_op jit(solution)/shard_map/all_to_all | solution.py:67
  19.8 2.3 %collective-permute-start.3 = (bf16[8,192,128]{2,1,0:T(8,128)(2,1)S(1)}, bf16[8,192,128]{2,1,0:T(8,128)(2,1)S(1)}, u32[]{:S(2)}, u32[]{:S(2)}) collective-permute-start(bf16[8,192,128]{2,1,0:T(8,128)(2,1)S(1)} %get-tuple-element.157), channel_id=1, source_target_pairs={{0,24},{1,17},{2,26},{3,19},{4,28},{5,21},{6,30},{7,23},{8,16},{9,... | collective-permute-start | bytes 1179656 | tf_op jit(solution)/shard_map/ppermute | solution.py:63
  22.1 2.2 %collective-permute-start = (bf16[8,208,128]{2,1,0:T(8,128)(2,1)S(1)}, bf16[8,208,128]{2,1,0:T(8,128)(2,1)S(1)}, u32[]{:S(2)}, u32[]{:S(2)}) collective-permute-start(bf16[8,208,128]{2,1,0:T(8,128)(2,1)S(1)} %slice.78), channel_id=1, source_target_pairs={{0,96},{1,33},{2,98},{3,35},{4,100},{5,37},{6,102},{7,39},{8,104},... | collective-permute-start | bytes 1277960 | tf_op jit(solution)/shard_map/ppermute | solution.py:63
  24.3 3.0 %collective-permute-start.6 = (bf16[8,192,128]{2,1,0:T(8,128)(2,1)S(1)}, bf16[8,192,128]{2,1,0:T(8,128)(2,1)S(1)}, u32[]{:S(2)}, u32[]{:S(2)}) collective-permute-start(bf16[8,192,128]{2,1,0:T(8,128)(2,1)S(1)} %get-tuple-element.156), channel_id=1, source_target_pairs={{0,6},{1,3},{2,4},{3,1},{4,2},{5,7},{6,0},{7,5},{8,14},{9,11},{10,... | collective-permute-start | bytes 1179656 | tf_op jit(solution)/shard_map/ppermute | solution.py:63
  27.3 2.0 collective-permute-done.3
  29.4 2.8 %collective-permute-start.4 = (bf16[16,192,128]{2,1,0:T(8,128)(2,1)S(1)}, bf16[16,192,128]{2,1,0:T(8,128)(2,1)S(1)}, u32[]{:S(2)}, u32[]{:S(2)}) collective-permute-start(bf16[16,192,128]{2,1,0:T(8,128)(2,1)S(1)} %pad_maximum_fusion.4), channel_id=1, source_target_pairs={{0,6},{1,3},{2,4},{3,1},{4,2},{5,7},{6,0},{7,5},{8,14},{9,11},{10,... | collective-permute-start | bytes 2359304 | tf_op jit(solution)/shard_map/ppermute | solution.py:63
  32.2 1.8 collective-permute-start.1
  34.1 2.5 %collective-permute-start.7 = (bf16[16,192,128]{2,1,0:T(8,128)(2,1)S(1)}, bf16[16,192,128]{2,1,0:T(8,128)(2,1)S(1)}, u32[]{:S(2)}, u32[]{:S(2)}) collective-permute-start(bf16[16,192,128]{2,1,0:T(8,128)(2,1)S(1)} %pad_maximum_fusion.5), channel_id=1, source_target_pairs={{0,96},{1,33},{2,98},{3,35},{4,100},{5,37},{6,102},{7,39},{8,104},... | collective-permute-start | bytes 2359304 | tf_op jit(solution)/shard_map/ppermute | solution.py:63
  36.6 6.0 %collective-permute-done.4 = bf16[16,192,128]{2,1,0:T(8,128)(2,1)S(1)} collective-permute-done((bf16[16,192,128]{2,1,0:T(8,128)(2,1)S(1)}, bf16[16,192,128]{2,1,0:T(8,128)(2,1)S(1)}, u32[]{:S(2)}, u32[]{:S(2)}) %collective-permute-start.4) | collective-permute-done | bytes 786464 | tf_op jit(solution)/shard_map/ppermute | solution.py:63
  42.6 0.2 pad_maximum_fusion.1.refs_2_
  42.8 1.7 collective-permute-start.5
  44.6 1.6 collective-permute-done.1
  46.2 0.2 pad_maximum_fusion.refs_0_
  46.4 2.1 collective-permute-start.2
  48.5 1.3 pad_maximum_fusion.2.refs_4_
  49.8 1.5 collective-permute-start.8
  51.3 0.6 fusion.19
  53.2 0.6 fusion.18
  55.2 0.6 copy.14
  55.9 0.7 concatenate.40.tab
  56.6 8.7 %flip.1 = (bf16[2,4,192,1024]{3,2,1,0:T(8,128)(2,1)}, bf16[4,2,192,1024]{3,2,1,0:T(8,128)(2,1)}, bf16[2,4,192,1024]{3,2,1,0:T(8,128)(2,1)}) custom-call(bf16[512,4608]{1,0:T(8,128)(2,1)} %w.3, bf16[512,4608]{1,0:T(8,128)(2,1)} %collective-permute-done.9.other_ref.refs_7_), custom_call_target="tpu_custom_call" | custom-call | bytes 18874368 | tf_op jit(solution)/shard_map/flip/pallas_call | solution.py:133
  65.3 6.5 %collective-permute-done.8.refs_5_ = bf16[32,192,128]{2,1,0:T(8,128)(2,1)} collective-permute-done((bf16[32,192,128]{2,1,0:T(8,128)(2,1)}, bf16[32,192,128]{2,1,0:T(8,128)(2,1)}, u32[]{:S(2)}, u32[]{:S(2)}) %collective-permute-start.8) | collective-permute-done | bytes 1572896 | tf_op jit(solution)/shard_map/ppermute | solution.py:63
  71.8 24.3 %act.1 = (f32[4,1024,256]{2,1,0:T(8,128)}, f32[4,1,256]{2,1,0:T(1,128)}, f32[4,1,256]{2,1,0:T(1,128)}, f32[64,16,128]{2,1,0:T(8,128)}, bf16[4,4608,256]{2,1,0:T(8,128)(2,1)}) custom-call(s32[26]{0:T(128)} %concatenate.40.tab, bf16[32,208,128]{2,1,0:T(8,128)(2,1)} %copy-done.8, bf16[32,208,128]{2,1,0:T(8,128)(2,1)} %collective-permute-done.2.refs_1_, ...), custom_call_target="tpu_custom_call" | custom-call | flops 9663676416 | bytes 30000000 | tf_op jit(solution)/shard_map/act/pallas_call | solution.py:286
  96.0 18.5 %all_to_all.16.totals_ref = f32[64,16,128]{2,1,0:T(8,128)} all-to-all(f32[64,16,128]{2,1,0:T(8,128)} %get-tuple-element.91), channel_id=1, replica_groups=mesh['x'=4,'ylo'=2,'yhi'=2,'z'=4,'core'=2] {'x','ylo','yhi','z'}, dimensions={0} | all-to-all | bytes 1048576 | tf_op jit(solution)/shard_map/all_to_all | solution.py:604
  114.5 11.8 %grad.1 = (bf16[4,512,256]{2,1,0:T(8,128)(2,1)}, bf16[4,512,256]{2,1,0:T(8,128)(2,1)}, bf16[4,1024,256]{2,1,0:T(8,128)(2,1)}, bf16[2,2,1024,256]{3,2,1,0:T(8,128...) custom-call(s32[26]{0:T(128)} %concatenate.40.tab, ...), custom_call_target="tpu_custom_call" | custom-call | flops 4831838208 | bytes 24000000 | tf_op jit(solution)/shard_map/grad/pallas_call | solution.py:467
  126.4 1.5 collective-permute-start.10
  127.9 0.8 collective-permute-start.11
  128.7 1.0 collective-permute-start.12
  129.7 10.0 %keep.1 = (bf16[32,192,128]{2,1,0:T(8,128)(2,1)}, bf16[32,192,128]{2,1,0:T(8,128)(2,1)}, bf16[32,192,128]{2,1,0:T(8,128)(2,1)}) custom-call(s32[26]{0:T(128)} %concatenate.40.tab, bf16[4,1024,256]{2,1,0:T(8,128)(2,1)} %get-tuple-element.103.gz_ref, bf16[2,2,1024,256]{3,2,1,0:T(8,128)(2,1)} %get-tuple-element.104.gy_ref, ...), custom_call_target="tpu_custom_call" | custom-call | flops 4718592 | bytes 1000000 | tf_op jit(solution)/shard_map/keep/pallas_call | solution.py:484
  139.7 11.7 %head.2 = (bf16[512,4608]{1,0:T(8,128)(2,1)}, f32[4,6,128]{2,1,0:T(8,128)}) custom-call(bf16[4,512,256]{2,1,0:T(8,128)(2,1)} %get-tuple-element.134.own_gr, bf16[4,512,256]{2,1,0:T(8,128)(2,1)} %collective-permute-done.13.twin_gr, bf16[4,4608,256]{2,1,0:T(8,128)(2,1)} %get-tuple-element.115.own_xt, bf16[4,4608,256]{2,1,0:T(8,128)(2,1)} %collective-permute-done.14.twin_xt, ...), custom_call_target="tpu_custom_call" | custom-call | flops 4718592 | bytes 1000000 | tf_op jit(solution)/shard_map/head/pallas_call | solution.py:521
  151.4 1.1 copy-done.2
  152.6 0.5 copy-done.3
  153.1 3.6 %sum2.1 = (bf16[16,192,128]{2,1,0:T(8,128)(2,1)}, bf16[16,192,128]{2,1,0:T(8,128)(2,1)}, bf16[16,192,128]{2,1,0:T(8,128)(2,1)}) custom-call(bf16[32,192,128]{2,1,0:T(8,128)(2,1)} %get-tuple-element.118.refs_0_, bf16[32,192,128]{2,1,0:T(8,128)(2,1)} %copy-done.2, bf16[32,192,128]{2,1,0:T(8,128)(2,1)} %get-tuple-element.120.refs_2_.refs_3_.refs_4_, ...), custom_call_target="tpu_custom_call" | custom-call | flops 4194304 | bytes 6000000 | tf_op jit(solution)/shard_map/sum2/pallas_call | solution.py:566
  156.7 2.3 %collective-permute-start.15 = (bf16[16,192,128]{2,1,0:T(8,128)(2,1)}, bf16[16,192,128]{2,1,0:T(8,128)(2,1)S(1)}, u32[]{:S(2)}, u32[]{:S(2)}) collective-permute-start(bf16[16,192,128]{2,1,0:T(8,128)(2,1)} %get-tuple-element.130), channel_id=1, source_target_pairs={{0,24},{1,17},{2,26},{3,19},{4,28},{5,21},{6,30},{7,23},{8,16},{9,... | collective-permute-start | bytes 2359304 | tf_op jit(solution)/shard_map/ppermute | solution.py:63
  159.0 2.0 collective-permute-start.16
  161.0 2.2 %collective-permute-start.17 = (bf16[16,192,128]{2,1,0:T(8,128)(2,1)}, bf16[16,192,128]{2,1,0:T(8,128)(2,1)S(1)}, u32[]{:S(2)}, u32[]{:S(2)}) collective-permute-start(bf16[16,192,128]{2,1,0:T(8,128)(2,1)} %get-tuple-element.132), channel_id=1, source_target_pairs={{0,96},{1,33},{2,98},{3,35},{4,100},{5,37},{6,102},{7,39},{8,104},... | collective-permute-start | bytes 2359304 | tf_op jit(solution)/shard_map/ppermute | solution.py:63
  163.2 7.3 %head.3 = (bf16[512,4608]{1,0:T(8,128)(2,1)}, f32[2,6,128]{2,1,0:T(8,128)}) custom-call(bf16[4,512,256]{2,1,0:T(8,128)(2,1)} %get-tuple-element.134.own_gr, bf16[4,512,256]{2,1,0:T(8,128)(2,1)} %collective-permute-done.13.twin_gr, bf16[4,4608,256]{2,1,0:T(8,128)(2,1)} %get-tuple-element.115.own_xt, ...), custom_call_target="tpu_custom_call", output_to_operand_aliasing={{0}: (5, {})} | custom-call | flops 4718592 | bytes 1000000 | tf_op jit(solution)/shard_map/head/pallas_call | solution.py:521
  170.6 0.7 constant_dynamic-update-slice_fusion
  171.3 1.1 collective-permute-start.18
  172.3 4.0 %collective-permute-done.18 = f32[6,6,128]{2,1,0:T(8,128)S(1)} collective-permute-done((f32[6,6,128]{2,1,0:T(8,128)S(1)}, f32[6,6,128]{2,1,0:T(8,128)S(1)}, u32[]{:S(2)}, u32[]{:S(2)}) %collective-permute-start.18) | collective-permute-done | bytes 18464 | tf_op jit(solution)/shard_map/ppermute | solution.py:63
  176.4 1.1 collective-permute-start.19
  177.5 0.3 copy-done.6
  177.8 3.1 %sum3.1 = (bf16[8,192,128]{2,1,0:T(8,128)(2,1)}, bf16[8,192,128]{2,1,0:T(8,128)(2,1)}, bf16[8,192,128]{2,1,0:T(8,128)(2,1)}) custom-call(bf16[32,192,128]{2,1,0:T(8,128)(2,1)} %get-tuple-element.118.refs_0_, bf16[32,192,128]{2,1,0:T(8,128)(2,1)} %copy-done.2, bf16[16,192,128]{2,1,0:T(8,128)(2,1)} %copy-done.4, ...), custom_call_target="tpu_custom_call" | custom-call | flops 4194304 | bytes 6000000 | tf_op jit(solution)/shard_map/sum3/pallas_call | solution.py:566
  180.8 0.6 collective-permute-done.19
  181.5 1.4 collective-permute-start.20
  182.9 1.1 collective-permute-start.21
  183.9 0.9 collective-permute-start.22
  184.8 2.4 %collective-permute-start.23 = (f32[6,6,128]{2,1,0:T(8,128)S(1)}, f32[6,6,128]{2,1,0:T(8,128)S(1)}, u32[]{:S(2)}, u32[]{:S(2)}) collective-permute-start(f32[6,6,128]{2,1,0:T(8,128)S(1)} %add.110), channel_id=1, source_target_pairs={{0,6},{1,3},{2,4},{3,1},{4,2},{5,7},{6,0},{7,5},{8,14},{9,11},{10,... | collective-permute-start | bytes 55304 | tf_op jit(solution)/shard_map/ppermute | solution.py:63
  187.2 6.1 %collective-permute-done.23 = f32[6,6,128]{2,1,0:T(8,128)S(1)} collective-permute-done((f32[6,6,128]{2,1,0:T(8,128)S(1)}, f32[6,6,128]{2,1,0:T(8,128)S(1)}, u32[]{:S(2)}, u32[]{:S(2)}) %collective-permute-start.23) | collective-permute-done | bytes 18464 | tf_op jit(solution)/shard_map/ppermute | solution.py:63
  193.5 0.1 multiply_reduce_fusion
  193.8 0.6 slice.82.refs_12_
  194.4 3.5 %sum4.1 = bf16[8,592,128]{2,1,0:T(8,128)(2,1)} custom-call(bf16[32,192,128]{2,1,0:T(8,128)(2,1)} %get-tuple-element.118.refs_0_, bf16[32,192,128]{2,1,0:T(8,128)(2,1)} %copy-done.2, bf16[16,192,128]{2,1,0:T(8,128)(2,1)} %copy-done.4, bf16[8,192,128]{2,1,0:T(8,128)(2,1)} %copy-done.11, bf16[32,192,128]{2,1,0:T(8,128)(2,1)} %get-tuple-element.120.refs_2_.refs_3_.refs_4_, ...), custom_call_target="tpu_custom_call" | custom-call | flops 4194304 | bytes 6000000 | tf_op jit(solution)/shard_map/sum4/pallas_call | solution.py:566
  197.9 3.7 %all-to-all-start.2 = ((bf16[8,592,128]{2,1,0:T(8,128)(2,1)}), bf16[8,592,128]{2,1,0:T(8,128)(2,1)S(1)}, u32[]{:S(2)}, u32[]{:S(2)}) async-start(bf16[8,592,128]{2,1,0:T(8,128)(2,1)} %sum4.1), calls=%async_computation.2 | async-start | bytes 2424832 | tf_op jit(solution)/shard_map/all_to_all | solution.py:67
  201.7 0.7 fusion.16
  202.4 1.2 multiply_bitcast_fusion
  203.6 9.1 %all-to-all-done.2 = bf16[8,592,128]{2,1,0:T(8,128)(2,1)S(1)} async-done(((bf16[8,592,128]{2,1,0:T(8,128)(2,1)}), bf16[8,592,128]{2,1,0:T(8,128)(2,1)S(1)}, u32[]{:S(2)}, u32[]{:S(2)}) %all-to-all-start.2) | async-done | bytes 1212448 | tf_op jit(solution)/shard_map/all_to_all | solution.py:67
  212.7 0.2 convert_reduce_fusion
  213.0 0.8 fusion.6
  213.9 0.3 collective-permute-done.24
  214.2 0.6 add_divide_fusion
  (79 shorter events, 1.2 us)
Async XLA Ops:
  0.6 54.5 %copy-start = (s32[2048]{0:T(1024)S(1)}, s32[2048]{0:T(1024)}, u32[]{:S(2)}) copy-start(s32[2048]{0:T(1024)} %param.7) | copy-start | bytes 24580
  0.6 56.0 %collective-permute-start.9 = (bf16[512,4608]{1,0:T(8,128)(2,1)}, bf16[512,4608]{1,0:T(8,128)(2,1)}, u32[]{:S(2)}, u32[]{:S(2)}) collective-permute-start(bf16[512,4608]{1,0:T(8,128)(2,1)} %w.3), channel_id=1, source_target_pairs={{0,1},{1,0},{2,3},{3,2},{4,5},{5,4},{6,7},{7,6},{8,9},{9,8},{10,11... | collective-permute-start | bytes 14155784 | tf_op jit(solution)/shard_map/ppermute | solution.py:63
  19.8 9.5 %collective-permute-start.3 = (bf16[8,192,128]{2,1,0:T(8,128)(2,1)S(1)}, bf16[8,192,128]{2,1,0:T(8,128)(2,1)S(1)}, u32[]{:S(2)}, u32[]{:S(2)}) collective-permute-start(bf16[8,192,128]{2,1,0:T(8,128)(2,1)S(1)} %get-tuple-element.157), channel_id=1, source_target_pairs={{0,24},{1,17},{2,26},{3,19},{4,28},{5,21},{6,30},{7,23},{8,16},{9,... | collective-permute-start | bytes 1179656 | tf_op jit(solution)/shard_map/ppermute | solution.py:63
  22.1 10.1 %collective-permute-start = (bf16[8,208,128]{2,1,0:T(8,128)(2,1)S(1)}, bf16[8,208,128]{2,1,0:T(8,128)(2,1)S(1)}, u32[]{:S(2)}, u32[]{:S(2)}) collective-permute-start(bf16[8,208,128]{2,1,0:T(8,128)(2,1)S(1)} %slice.78), channel_id=1, source_target_pairs={{0,96},{1,33},{2,98},{3,35},{4,100},{5,37},{6,102},{7,39},{8,104},... | collective-permute-start | bytes 1277960 | tf_op jit(solution)/shard_map/ppermute | solution.py:63
  24.3 9.8 %collective-permute-start.6 = (bf16[8,192,128]{2,1,0:T(8,128)(2,1)S(1)}, bf16[8,192,128]{2,1,0:T(8,128)(2,1)S(1)}, u32[]{:S(2)}, u32[]{:S(2)}) collective-permute-start(bf16[8,192,128]{2,1,0:T(8,128)(2,1)S(1)} %get-tuple-element.156), channel_id=1, source_target_pairs={{0,6},{1,3},{2,4},{3,1},{4,2},{5,7},{6,0},{7,5},{8,14},{9,11},{10,... | collective-permute-start | bytes 1179656 | tf_op jit(solution)/shard_map/ppermute | solution.py:63
  29.4 13.3 %collective-permute-start.4 = (bf16[16,192,128]{2,1,0:T(8,128)(2,1)S(1)}, bf16[16,192,128]{2,1,0:T(8,128)(2,1)S(1)}, u32[]{:S(2)}, u32[]{:S(2)}) collective-permute-start(bf16[16,192,128]{2,1,0:T(8,128)(2,1)S(1)} %pad_maximum_fusion.4), channel_id=1, source_target_pairs={{0,6},{1,3},{2,4},{3,1},{4,2},{5,7},{6,0},{7,5},{8,14},{9,11},{10,... | collective-permute-start | bytes 2359304 | tf_op jit(solution)/shard_map/ppermute | solution.py:63
  32.2 14.0 %collective-permute-start.1 = (bf16[16,208,128]{2,1,0:T(8,128)(2,1)S(1)}, bf16[16,208,128]{2,1,0:T(8,128)(2,1)S(1)}, u32[]{:S(2)}, u32[]{:S(2)}) collective-permute-start(bf16[16,208,128]{2,1,0:T(8,128)(2,1)S(1)} %pad_maximum_fusion.3), channel_id=1, source_target_pairs={{0,24},{1,17},{2,26},{3,19},{4,28},{5,21},{6,30},{7,23},{8,16},{9,... | collective-permute-start | bytes 2555912 | tf_op jit(solution)/shard_map/ppermute | solution.py:63
  34.1 14.4 %collective-permute-start.7 = (bf16[16,192,128]{2,1,0:T(8,128)(2,1)S(1)}, bf16[16,192,128]{2,1,0:T(8,128)(2,1)S(1)}, u32[]{:S(2)}, u32[]{:S(2)}) collective-permute-start(bf16[16,192,128]{2,1,0:T(8,128)(2,1)S(1)} %pad_maximum_fusion.5), channel_id=1, source_target_pairs={{0,96},{1,33},{2,98},{3,35},{4,100},{5,37},{6,102},{7,39},{8,104},... | collective-permute-start | bytes 2359304 | tf_op jit(solution)/shard_map/ppermute | solution.py:63
  42.8 3.6 %copy-start.9 = (bf16[32,192,128]{2,1,0:T(8,128)(2,1)}, bf16[32,192,128]{2,1,0:T(8,128)(2,1)S(1)}, u32[]{:S(2)}) copy-start(bf16[32,192,128]{2,1,0:T(8,128)(2,1)S(1)} %pad_maximum_fusion.1.refs_2_) | copy-start | bytes 4718596
  42.8 22.5 %collective-permute-start.5 = (bf16[32,192,128]{2,1,0:T(8,128)(2,1)S(1)}, bf16[32,192,128]{2,1,0:T(8,128)(2,1)}, u32[]{:S(2)}, u32[]{:S(2)}) collective-permute-start(bf16[32,192,128]{2,1,0:T(8,128)(2,1)S(1)} %pad_maximum_fusion.1.refs_2_), channel_id=1, source_target_pairs={{0,96},{1,33},{2,98},{3,35},{4,100},{5,37},{6,102},{7,39},{8,104},... | collective-permute-start | bytes 4718600 | tf_op jit(solution)/shard_map/ppermute | solution.py:63
  46.4 5.0 %copy-start.8 = (bf16[32,208,128]{2,1,0:T(8,128)(2,1)}, bf16[32,208,128]{2,1,0:T(8,128)(2,1)S(1)}, u32[]{:S(2)}) copy-start(bf16[32,208,128]{2,1,0:T(8,128)(2,1)S(1)} %pad_maximum_fusion.refs_0_) | copy-start | bytes 5111812
  46.4 25.4 %collective-permute-start.2 = (bf16[32,208,128]{2,1,0:T(8,128)(2,1)S(1)}, bf16[32,208,128]{2,1,0:T(8,128)(2,1)}, u32[]{:S(2)}, u32[]{:S(2)}) collective-permute-start(bf16[32,208,128]{2,1,0:T(8,128)(2,1)S(1)} %pad_maximum_fusion.refs_0_), channel_id=1, source_target_pairs={{0,6},{1,3},{2,4},{3,1},{4,2},{5,7},{6,0},{7,5},{8,14},{9,11},{10,... | collective-permute-start | bytes 5111816 | tf_op jit(solution)/shard_map/ppermute | solution.py:63
  49.8 21.9 %collective-permute-start.8 = (bf16[32,192,128]{2,1,0:T(8,128)(2,1)}, bf16[32,192,128]{2,1,0:T(8,128)(2,1)}, u32[]{:S(2)}, u32[]{:S(2)}) collective-permute-start(bf16[32,192,128]{2,1,0:T(8,128)(2,1)} %pad_maximum_fusion.2.refs_4_), channel_id=1, source_target_pairs={{0,24},{1,17},{2,26},{3,19},{4,28},{5,21},{6,30},{7,23},{8,16},{9,... | collective-permute-start | bytes 4718600 | tf_op jit(solution)/shard_map/ppermute | solution.py:63
  114.5 25.2 %collective-permute-start.14 = (bf16[4,4608,256]{2,1,0:T(8,128)(2,1)}, bf16[4,4608,256]{2,1,0:T(8,128)(2,1)}, u32[]{:S(2)}, u32[]{:S(2)}) collective-permute-start(bf16[4,4608,256]{2,1,0:T(8,128)(2,1)} %get-tuple-element.115.own_xt), channel_id=1, source_target_pairs={{0,1},{1,0},{2,3},{3,2},{4,5},{5,4},{6,7},{7,6},{8,9},{9,8},{10,11... | collective-permute-start | bytes 28311560 | tf_op jit(solution)/shard_map/ppermute | solution.py:63
  126.4 25.0 %collective-permute-start.10 = (bf16[32,192,128]{2,1,0:T(8,128)(2,1)}, bf16[32,192,128]{2,1,0:T(8,128)(2,1)S(1)}, u32[]{:S(2)}, u32[]{:S(2)}) collective-permute-start(bf16[32,192,128]{2,1,0:T(8,128)(2,1)} %get-tuple-element.100), channel_id=1, source_target_pairs={{0,6},{1,3},{2,4},{3,1},{4,2},{5,7},{6,0},{7,5},{8,14},{9,11},{10,... | collective-permute-start | bytes 4718600 | tf_op jit(solution)/shard_map/ppermute | solution.py:63
  127.9 23.5 %collective-permute-start.11 = (bf16[32,192,128]{2,1,0:T(8,128)(2,1)}, bf16[32,192,128]{2,1,0:T(8,128)(2,1)S(1)}, u32[]{:S(2)}, u32[]{:S(2)}) collective-permute-start(bf16[32,192,128]{2,1,0:T(8,128)(2,1)} %get-tuple-element.101), channel_id=1, source_target_pairs={{0,96},{1,33},{2,98},{3,35},{4,100},{5,37},{6,102},{7,39},{8,104},... | collective-permute-start | bytes 4718600 | tf_op jit(solution)/shard_map/ppermute | solution.py:63
  128.7 22.7 %collective-permute-start.12 = (bf16[32,192,128]{2,1,0:T(8,128)(2,1)}, bf16[32,192,128]{2,1,0:T(8,128)(2,1)}, u32[]{:S(2)}, u32[]{:S(2)}) collective-permute-start(bf16[32,192,128]{2,1,0:T(8,128)(2,1)} %get-tuple-element.102), channel_id=1, source_target_pairs={{0,24},{1,17},{2,26},{3,19},{4,28},{5,21},{6,30},{7,23},{8,16},{9,... | collective-permute-start | bytes 4718600 | tf_op jit(solution)/shard_map/ppermute | solution.py:63
  129.7 10.0 %collective-permute-start.13 = (bf16[4,512,256]{2,1,0:T(8,128)(2,1)}, bf16[4,512,256]{2,1,0:T(8,128)(2,1)}, u32[]{:S(2)}, u32[]{:S(2)}) collective-permute-start(bf16[4,512,256]{2,1,0:T(8,128)(2,1)} %get-tuple-element.109), channel_id=1, source_target_pairs={{0,1},{1,0},{2,3},{3,2},{4,5},{5,4},{6,7},{7,6},{8,9},{9,8},{10,11... | collective-permute-start | bytes 3145736 | tf_op jit(solution)/shard_map/ppermute | solution.py:63
  151.4 1.2 copy-start.2
  151.4 1.7 copy-start.3
  156.7 13.9 %copy-start.14 = (f32[4,6,128]{2,1,0:T(8,128)S(1)}, f32[4,6,128]{2,1,0:T(8,128)}, u32[]{:S(2)}) copy-start(f32[4,6,128]{2,1,0:T(8,128)} %get-tuple-element.133) | copy-start | bytes 36868
  156.7 19.6 %collective-permute-start.15 = (bf16[16,192,128]{2,1,0:T(8,128)(2,1)}, bf16[16,192,128]{2,1,0:T(8,128)(2,1)S(1)}, u32[]{:S(2)}, u32[]{:S(2)}) collective-permute-start(bf16[16,192,128]{2,1,0:T(8,128)(2,1)} %get-tuple-element.130), channel_id=1, source_target_pairs={{0,24},{1,17},{2,26},{3,19},{4,28},{5,21},{6,30},{7,23},{8,16},{9,... | collective-permute-start | bytes 2359304 | tf_op jit(solution)/shard_map/ppermute | solution.py:63
  159.0 17.3 %collective-permute-start.16 = (bf16[16,192,128]{2,1,0:T(8,128)(2,1)}, bf16[16,192,128]{2,1,0:T(8,128)(2,1)S(1)}, u32[]{:S(2)}, u32[]{:S(2)}) collective-permute-start(bf16[16,192,128]{2,1,0:T(8,128)(2,1)} %get-tuple-element.131), channel_id=1, source_target_pairs={{0,6},{1,3},{2,4},{3,1},{4,2},{5,7},{6,0},{7,5},{8,14},{9,11},{10,... | collective-permute-start | bytes 2359304 | tf_op jit(solution)/shard_map/ppermute | solution.py:63
  161.0 15.3 %collective-permute-start.17 = (bf16[16,192,128]{2,1,0:T(8,128)(2,1)}, bf16[16,192,128]{2,1,0:T(8,128)(2,1)S(1)}, u32[]{:S(2)}, u32[]{:S(2)}) collective-permute-start(bf16[16,192,128]{2,1,0:T(8,128)(2,1)} %get-tuple-element.132), channel_id=1, source_target_pairs={{0,96},{1,33},{2,98},{3,35},{4,100},{5,37},{6,102},{7,39},{8,104},... | collective-permute-start | bytes 2359304 | tf_op jit(solution)/shard_map/ppermute | solution.py:63
  171.3 5.0 %collective-permute-start.18 = (f32[6,6,128]{2,1,0:T(8,128)S(1)}, f32[6,6,128]{2,1,0:T(8,128)S(1)}, u32[]{:S(2)}, u32[]{:S(2)}) collective-permute-start(f32[6,6,128]{2,1,0:T(8,128)S(1)} %constant_dynamic-update-slice_fusion), channel_id=1, source_target_pairs={{0,24},{1,17},{2,26},{3,19},{4,28},{5,21},{6,30},{7,23},{8,16},{9,... | collective-permute-start | bytes 55304 | tf_op jit(solution)/shard_map/ppermute | solution.py:63
  176.3 1.2 copy-start.4
  176.3 1.2 copy-start.5
  176.3 1.4 copy-start.6
  176.4 5.1 %collective-permute-start.19 = (f32[6,6,128]{2,1,0:T(8,128)S(1)}, f32[6,6,128]{2,1,0:T(8,128)S(1)}, u32[]{:S(2)}, u32[]{:S(2)}) collective-permute-start(f32[6,6,128]{2,1,0:T(8,128)S(1)} %add.109), channel_id=1, source_target_pairs={{0,96},{1,33},{2,98},{3,35},{4,100},{5,37},{6,102},{7,39},{8,104},... | collective-permute-start | bytes 55304 | tf_op jit(solution)/shard_map/ppermute | solution.py:63
  181.5 11.9 %collective-permute-start.20 = (bf16[8,192,128]{2,1,0:T(8,128)(2,1)}, bf16[8,192,128]{2,1,0:T(8,128)(2,1)S(1)}, u32[]{:S(2)}, u32[]{:S(2)}) collective-permute-start(bf16[8,192,128]{2,1,0:T(8,128)(2,1)} %get-tuple-element.145), channel_id=1, source_target_pairs={{0,96},{1,33},{2,98},{3,35},{4,100},{5,37},{6,102},{7,39},{8,104},... | collective-permute-start | bytes 1179656 | tf_op jit(solution)/shard_map/ppermute | solution.py:63
  182.9 10.5 %collective-permute-start.21 = (bf16[8,192,128]{2,1,0:T(8,128)(2,1)}, bf16[8,192,128]{2,1,0:T(8,128)(2,1)S(1)}, u32[]{:S(2)}, u32[]{:S(2)}) collective-permute-start(bf16[8,192,128]{2,1,0:T(8,128)(2,1)} %get-tuple-element.146), channel_id=1, source_target_pairs={{0,24},{1,17},{2,26},{3,19},{4,28},{5,21},{6,30},{7,23},{8,16},{9,... | collective-permute-start | bytes 1179656 | tf_op jit(solution)/shard_map/ppermute | solution.py:63
  183.9 9.5 %collective-permute-start.22 = (bf16[8,192,128]{2,1,0:T(8,128)(2,1)}, bf16[8,192,128]{2,1,0:T(8,128)(2,1)S(1)}, u32[]{:S(2)}, u32[]{:S(2)}) collective-permute-start(bf16[8,192,128]{2,1,0:T(8,128)(2,1)} %get-tuple-element.147), channel_id=1, source_target_pairs={{0,6},{1,3},{2,4},{3,1},{4,2},{5,7},{6,0},{7,5},{8,14},{9,11},{10,... | collective-permute-start | bytes 1179656 | tf_op jit(solution)/shard_map/ppermute | solution.py:63
  184.8 8.6 %collective-permute-start.23 = (f32[6,6,128]{2,1,0:T(8,128)S(1)}, f32[6,6,128]{2,1,0:T(8,128)S(1)}, u32[]{:S(2)}, u32[]{:S(2)}) collective-permute-start(f32[6,6,128]{2,1,0:T(8,128)S(1)} %add.110), channel_id=1, source_target_pairs={{0,6},{1,3},{2,4},{3,1},{4,2},{5,7},{6,0},{7,5},{8,14},{9,11},{10,... | collective-permute-start | bytes 55304 | tf_op jit(solution)/shard_map/ppermute | solution.py:63
  193.4 1.0 copy-start.11
  193.4 1.0 copy-start.12
  193.4 1.0 copy-start.13
  197.9 4.5 %copy-start.7 = (f32[64,16,128]{2,1,0:T(8,128)S(1)}, f32[64,16,128]{2,1,0:T(8,128)}, u32[]{:S(2)}) copy-start(f32[64,16,128]{2,1,0:T(8,128)} %all_to_all.16.totals_ref) | copy-start | bytes 1572868
  197.9 14.8 %all-to-all-start.2 = ((bf16[8,592,128]{2,1,0:T(8,128)(2,1)}), bf16[8,592,128]{2,1,0:T(8,128)(2,1)S(1)}, u32[]{:S(2)}, u32[]{:S(2)}) async-start(bf16[8,592,128]{2,1,0:T(8,128)(2,1)} %sum4.1), calls=%async_computation.2 | async-start | bytes 2424832 | tf_op jit(solution)/shard_map/all_to_all | solution.py:67
  201.6 11.4 %copy-start.10 = (bf16[128,576]{0,1:T(8,128)(2,1)S(1)}, bf16[128,576]{0,1:T(8,128)(2,1)}, u32[]{:S(2)}) copy-start(bf16[128,576]{0,1:T(8,128)(2,1)} %param.4) | copy-start | bytes 442372
  201.7 12.5 %copy-start.15 = (bf16[576]{0:T(1024)(128)(2,1)S(1)}, bf16[576]{0:T(1024)(128)(2,1)}, u32[]{:S(2)}) copy-start(bf16[576]{0:T(1024)(128)(2,1)} %param.5) | copy-start | bytes 3460
  201.7 13.1 %copy-start.1 = (s32[2048]{0:T(1024)S(1)}, s32[2048]{0:T(1024)}, u32[]{:S(2)}) copy-start(s32[2048]{0:T(1024)} %param.7) | copy-start | bytes 24580
  212.9 1.2 collective-permute-start.24

commit v4 on v3

--- a/solution.py
+++ b/solution.py
@@ -202,9 +202,9 @@
 
     @pl.when(step == 0)
     def _():
+        load(0, own_ref).start()
         issue(step)
-        for h, ref in enumerate((own_ref, other_ref)):
-            load(h, ref).start()
+        load(1, other_ref).start()
         issue(step + 1)
         arrived()
         for h, ref in enumerate((own_ref, other_ref)):
@@ -382,7 +382,7 @@
     outgoing = copies(list(zip(by_rows + (gz, gy) + away, out_refs)), out_sems)
     for copy in incoming:
         copy.start()
-    rows = 32
+    rows = 64
     inv = 1.0 / jnp.sum(totals_ref[...], axis=0)[0:8]
     line = lax.broadcasted_iota(jnp.int32, (8, TB), 0)
 

time: 216 us -> 215 us (level)
  transfers between devices with their start and end apart: 26 -> 26, of which waited for: 9 -> 9; matrix products, arithmetic and copies ran while one was open for 5% -> 5% of each run, Pallas kernels for 24% -> 25%
where the time goes in v4:
time: 215 us; the launch traced here: 214 us
  Pallas kernels  82.7 us (38%)
  starting transfers between devices  41.5 us (19%)
  waiting for transfers between devices  36.4 us (17%)
  blocking collectives  35.4 us (16%)
  local copies, waits for them, and re-layouts  7.18 us (3%)
  other arithmetic  6.75 us (3%)
  between operations  3.7 us (2%)
    ppermute x25, starting transfers between devices, send(): return lax.ppermute(a, AX, pairs)  37.8 us
    ppermute x25, waiting for transfers between devices, send(): return lax.ppermute(a, AX, pairs)  27.3 us
    pallas_call x1, Pallas kernels, act_call(): pl.pallas_call(act_kernel, grid_spec=pltpu.PrefetchScalarGridSpec(num_sca...  23 us
    pallas_call x2, Pallas kernels, head_call(): pl.pallas_call(head_kernel, grid=(count,), in_specs=[rows, rows, tokens,...  19 us
    all_to_all x1, blocking collectives, shards(): stats = lax.all_to_all(stats, AX[:4], 0, 0)  18.5 us
    all_to_all x1, blocking collectives, in_cube(): return lax.all_to_all(a, AX, 0, 0, axis_index_groups=CUBES)  16.9 us
    pallas_call x1, Pallas kernels, grad_call(): pl.pallas_call(grad_kernel, in_specs=[SMEM_SPEC, ANYWHERE] + [VMEM_SPEC]...  11.9 us
    pallas_call x3, Pallas kernels, sum_call(): pl.pallas_call(functools.partial(sum_kernel, terms), grid=(count // step,...  10.2 us
  transfers between devices with their start and end apart: 26, of which 9 were waited for; matrix products, arithmetic and copies ran while one was open for 5% of the time, Pallas kernels for 25%

profile of v4, /device:TPU:0, one launch (start us, length us, event | category | flops | bytes accessed | tf_op | source)
XLA Modules:
  0.0 213.6 jit_solution(512213861024273645)
XLA Ops:
  0.7 0.7 convert_element_type.74
  1.4 1.1 fusion.1
  2.5 0.2 concatenate.33
  2.7 0.2 broadcast_in_dim.5
  2.9 16.9 %all_to_all.15 = bf16[8,592,128]{2,1,0:T(8,128)(2,1)S(1)} all-to-all(bf16[8,592,128]{2,1,0:T(8,128)(2,1)S(1)} %broadcast_in_dim.5), channel_id=1, replica_groups={{0,2,16,18,32,34,48,50},{6,4,22,20,38,36,54,52},{24,26,8,10,56,58,40,42..., dimensions={0} | all-to-all | bytes 2424832 | tf_op jit(solution)/shard_map/all_to_all | solution.py:67
  19.8 2.3 %collective-permute-start.3 = (bf16[8,192,128]{2,1,0:T(8,128)(2,1)S(1)}, bf16[8,192,128]{2,1,0:T(8,128)(2,1)S(1)}, u32[]{:S(2)}, u32[]{:S(2)}) collective-permute-start(bf16[8,192,128]{2,1,0:T(8,128)(2,1)S(1)} %get-tuple-element.157), channel_id=1, source_target_pairs={{0,24},{1,17},{2,26},{3,19},{4,28},{5,21},{6,30},{7,23},{8,16},{9,... | collective-permute-start | bytes 1179656 | tf_op jit(solution)/shard_map/ppermute | solution.py:63
  22.1 2.2 %collective-permute-start = (bf16[8,208,128]{2,1,0:T(8,128)(2,1)S(1)}, bf16[8,208,128]{2,1,0:T(8,128)(2,1)S(1)}, u32[]{:S(2)}, u32[]{:S(2)}) collective-permute-start(bf16[8,208,128]{2,1,0:T(8,128)(2,1)S(1)} %slice.78), channel_id=1, source_target_pairs={{0,96},{1,33},{2,98},{3,35},{4,100},{5,37},{6,102},{7,39},{8,104},... | collective-permute-start | bytes 1277960 | tf_op jit(solution)/shard_map/ppermute | solution.py:63
  24.3 3.0 %collective-permute-start.6 = (bf16[8,192,128]{2,1,0:T(8,128)(2,1)S(1)}, bf16[8,192,128]{2,1,0:T(8,128)(2,1)S(1)}, u32[]{:S(2)}, u32[]{:S(2)}) collective-permute-start(bf16[8,192,128]{2,1,0:T(8,128)(2,1)S(1)} %get-tuple-element.156), channel_id=1, source_target_pairs={{0,6},{1,3},{2,4},{3,1},{4,2},{5,7},{6,0},{7,5},{8,14},{9,11},{10,... | collective-permute-start | bytes 1179656 | tf_op jit(solution)/shard_map/ppermute | solution.py:63
  27.3 2.0 collective-permute-done.3
  29.4 2.8 %collective-permute-start.4 = (bf16[16,192,128]{2,1,0:T(8,128)(2,1)S(1)}, bf16[16,192,128]{2,1,0:T(8,128)(2,1)S(1)}, u32[]{:S(2)}, u32[]{:S(2)}) collective-permute-start(bf16[16,192,128]{2,1,0:T(8,128)(2,1)S(1)} %pad_maximum_fusion.4), channel_id=1, source_target_pairs={{0,6},{1,3},{2,4},{3,1},{4,2},{5,7},{6,0},{7,5},{8,14},{9,11},{10,... | collective-permute-start | bytes 2359304 | tf_op jit(solution)/shard_map/ppermute | solution.py:63
  32.2 1.8 collective-permute-start.1
  34.1 2.5 %collective-permute-start.7 = (bf16[16,192,128]{2,1,0:T(8,128)(2,1)S(1)}, bf16[16,192,128]{2,1,0:T(8,128)(2,1)S(1)}, u32[]{:S(2)}, u32[]{:S(2)}) collective-permute-start(bf16[16,192,128]{2,1,0:T(8,128)(2,1)S(1)} %pad_maximum_fusion.5), channel_id=1, source_target_pairs={{0,96},{1,33},{2,98},{3,35},{4,100},{5,37},{6,102},{7,39},{8,104},... | collective-permute-start | bytes 2359304 | tf_op jit(solution)/shard_map/ppermute | solution.py:63
  36.6 6.0 %collective-permute-done.4 = bf16[16,192,128]{2,1,0:T(8,128)(2,1)S(1)} collective-permute-done((bf16[16,192,128]{2,1,0:T(8,128)(2,1)S(1)}, bf16[16,192,128]{2,1,0:T(8,128)(2,1)S(1)}, u32[]{:S(2)}, u32[]{:S(2)}) %collective-permute-start.4) | collective-permute-done | bytes 786464 | tf_op jit(solution)/shard_map/ppermute | solution.py:63
  42.6 0.2 pad_maximum_fusion.1.refs_2_
  42.8 1.7 collective-permute-start.5
  44.6 1.6 collective-permute-done.1
  46.2 0.2 pad_maximum_fusion.refs_0_
  46.4 2.1 collective-permute-start.2
  48.5 1.3 pad_maximum_fusion.2.refs_4_
  49.8 1.5 collective-permute-start.8
  51.3 0.6 fusion.19
  53.2 0.6 fusion.18
  55.2 0.6 copy.14
  55.9 0.7 concatenate.40.tab
  56.6 8.7 %flip.1 = (bf16[2,4,192,1024]{3,2,1,0:T(8,128)(2,1)}, bf16[4,2,192,1024]{3,2,1,0:T(8,128)(2,1)}, bf16[2,4,192,1024]{3,2,1,0:T(8,128)(2,1)}) custom-call(bf16[512,4608]{1,0:T(8,128)(2,1)} %w.3, bf16[512,4608]{1,0:T(8,128)(2,1)} %collective-permute-done.9.other_ref.refs_7_), custom_call_target="tpu_custom_call" | custom-call | bytes 18874368 | tf_op jit(solution)/shard_map/flip/pallas_call | solution.py:133
  65.3 6.5 %collective-permute-done.8.refs_5_ = bf16[32,192,128]{2,1,0:T(8,128)(2,1)} collective-permute-done((bf16[32,192,128]{2,1,0:T(8,128)(2,1)}, bf16[32,192,128]{2,1,0:T(8,128)(2,1)}, u32[]{:S(2)}, u32[]{:S(2)}) %collective-permute-start.8) | collective-permute-done | bytes 1572896 | tf_op jit(solution)/shard_map/ppermute | solution.py:63
  71.8 23.0 %act.1 = (f32[4,1024,256]{2,1,0:T(8,128)}, f32[4,1,256]{2,1,0:T(1,128)}, f32[4,1,256]{2,1,0:T(1,128)}, f32[64,16,128]{2,1,0:T(8,128)}, bf16[4,4608,256]{2,1,0:T(8,128)(2,1)}) custom-call(s32[26]{0:T(128)} %concatenate.40.tab, bf16[32,208,128]{2,1,0:T(8,128)(2,1)} %copy-done.8, bf16[32,208,128]{2,1,0:T(8,128)(2,1)} %collective-permute-done.2.refs_1_, ...), custom_call_target="tpu_custom_call" | custom-call | flops 9663676416 | bytes 30000000 | tf_op jit(solution)/shard_map/act/pallas_call | solution.py:286
  94.8 18.5 %all_to_all.16.totals_ref = f32[64,16,128]{2,1,0:T(8,128)} all-to-all(f32[64,16,128]{2,1,0:T(8,128)} %get-tuple-element.91), channel_id=1, replica_groups=mesh['x'=4,'ylo'=2,'yhi'=2,'z'=4,'core'=2] {'x','ylo','yhi','z'}, dimensions={0} | all-to-all | bytes 1048576 | tf_op jit(solution)/shard_map/all_to_all | solution.py:604
  113.3 11.9 %grad.1 = (bf16[4,512,256]{2,1,0:T(8,128)(2,1)}, bf16[4,512,256]{2,1,0:T(8,128)(2,1)}, bf16[4,1024,256]{2,1,0:T(8,128)(2,1)}, bf16[2,2,1024,256]{3,2,1,0:T(8,128...) custom-call(s32[26]{0:T(128)} %concatenate.40.tab, ...), custom_call_target="tpu_custom_call" | custom-call | flops 4831838208 | bytes 24000000 | tf_op jit(solution)/shard_map/grad/pallas_call | solution.py:467
  125.2 1.5 collective-permute-start.10
  126.7 0.8 collective-permute-start.11
  127.5 1.0 collective-permute-start.12
  128.5 10.0 %keep.1 = (bf16[32,192,128]{2,1,0:T(8,128)(2,1)}, bf16[32,192,128]{2,1,0:T(8,128)(2,1)}, bf16[32,192,128]{2,1,0:T(8,128)(2,1)}) custom-call(s32[26]{0:T(128)} %concatenate.40.tab, bf16[4,1024,256]{2,1,0:T(8,128)(2,1)} %get-tuple-element.103.gz_ref, bf16[2,2,1024,256]{3,2,1,0:T(8,128)(2,1)} %get-tuple-element.104.gy_ref, ...), custom_call_target="tpu_custom_call" | custom-call | flops 4718592 | bytes 1000000 | tf_op jit(solution)/shard_map/keep/pallas_call | solution.py:484
  138.5 11.7 %head.2 = (bf16[512,4608]{1,0:T(8,128)(2,1)}, f32[4,6,128]{2,1,0:T(8,128)}) custom-call(bf16[4,512,256]{2,1,0:T(8,128)(2,1)} %get-tuple-element.134.own_gr, bf16[4,512,256]{2,1,0:T(8,128)(2,1)} %collective-permute-done.13.twin_gr, bf16[4,4608,256]{2,1,0:T(8,128)(2,1)} %get-tuple-element.115.own_xt, bf16[4,4608,256]{2,1,0:T(8,128)(2,1)} %collective-permute-done.14.twin_xt, ...), custom_call_target="tpu_custom_call" | custom-call | flops 4718592 | bytes 1000000 | tf_op jit(solution)/shard_map/head/pallas_call | solution.py:521
  150.2 1.1 copy-done.2
  151.4 0.5 copy-done.3
  151.9 3.6 %sum2.1 = (bf16[16,192,128]{2,1,0:T(8,128)(2,1)}, bf16[16,192,128]{2,1,0:T(8,128)(2,1)}, bf16[16,192,128]{2,1,0:T(8,128)(2,1)}) custom-call(bf16[32,192,128]{2,1,0:T(8,128)(2,1)} %get-tuple-element.118.refs_0_, bf16[32,192,128]{2,1,0:T(8,128)(2,1)} %copy-done.2, bf16[32,192,128]{2,1,0:T(8,128)(2,1)} %get-tuple-element.120.refs_2_.refs_3_.refs_4_, ...), custom_call_target="tpu_custom_call" | custom-call | flops 4194304 | bytes 6000000 | tf_op jit(solution)/shard_map/sum2/pallas_call | solution.py:566
  155.5 2.3 %collective-permute-start.15 = (bf16[16,192,128]{2,1,0:T(8,128)(2,1)}, bf16[16,192,128]{2,1,0:T(8,128)(2,1)S(1)}, u32[]{:S(2)}, u32[]{:S(2)}) collective-permute-start(bf16[16,192,128]{2,1,0:T(8,128)(2,1)} %get-tuple-element.130), channel_id=1, source_target_pairs={{0,24},{1,17},{2,26},{3,19},{4,28},{5,21},{6,30},{7,23},{8,16},{9,... | collective-permute-start | bytes 2359304 | tf_op jit(solution)/shard_map/ppermute | solution.py:63
  157.8 2.0 collective-permute-start.16
  159.9 2.2 %collective-permute-start.17 = (bf16[16,192,128]{2,1,0:T(8,128)(2,1)}, bf16[16,192,128]{2,1,0:T(8,128)(2,1)S(1)}, u32[]{:S(2)}, u32[]{:S(2)}) collective-permute-start(bf16[16,192,128]{2,1,0:T(8,128)(2,1)} %get-tuple-element.132), channel_id=1, source_target_pairs={{0,96},{1,33},{2,98},{3,35},{4,100},{5,37},{6,102},{7,39},{8,104},... | collective-permute-start | bytes 2359304 | tf_op jit(solution)/shard_map/ppermute | solution.py:63
  162.0 7.3 %head.3 = (bf16[512,4608]{1,0:T(8,128)(2,1)}, f32[2,6,128]{2,1,0:T(8,128)}) custom-call(bf16[4,512,256]{2,1,0:T(8,128)(2,1)} %get-tuple-element.134.own_gr, bf16[4,512,256]{2,1,0:T(8,128)(2,1)} %collective-permute-done.13.twin_gr, bf16[4,4608,256]{2,1,0:T(8,128)(2,1)} %get-tuple-element.115.own_xt, ...), custom_call_target="tpu_custom_call", output_to_operand_aliasing={{0}: (5, {})} | custom-call | flops 4718592 | bytes 1000000 | tf_op jit(solution)/shard_map/head/pallas_call | solution.py:521
  169.4 0.7 constant_dynamic-update-slice_fusion
  170.1 1.0 collective-permute-start.18
  171.1 4.0 %collective-permute-done.18 = f32[6,6,128]{2,1,0:T(8,128)S(1)} collective-permute-done((f32[6,6,128]{2,1,0:T(8,128)S(1)}, f32[6,6,128]{2,1,0:T(8,128)S(1)}, u32[]{:S(2)}, u32[]{:S(2)}) %collective-permute-start.18) | collective-permute-done | bytes 18464 | tf_op jit(solution)/shard_map/ppermute | solution.py:63
  175.2 1.1 collective-permute-start.19
  176.3 0.3 copy-done.6
  176.6 3.1 %sum3.1 = (bf16[8,192,128]{2,1,0:T(8,128)(2,1)}, bf16[8,192,128]{2,1,0:T(8,128)(2,1)}, bf16[8,192,128]{2,1,0:T(8,128)(2,1)}) custom-call(bf16[32,192,128]{2,1,0:T(8,128)(2,1)} %get-tuple-element.118.refs_0_, bf16[32,192,128]{2,1,0:T(8,128)(2,1)} %copy-done.2, bf16[16,192,128]{2,1,0:T(8,128)(2,1)} %copy-done.4, ...), custom_call_target="tpu_custom_call" | custom-call | flops 4194304 | bytes 6000000 | tf_op jit(solution)/shard_map/sum3/pallas_call | solution.py:566
  179.7 0.6 collective-permute-done.19
  180.3 1.4 collective-permute-start.20
  181.7 1.0 collective-permute-start.21
  182.7 0.9 collective-permute-start.22
  183.6 2.4 %collective-permute-start.23 = (f32[6,6,128]{2,1,0:T(8,128)S(1)}, f32[6,6,128]{2,1,0:T(8,128)S(1)}, u32[]{:S(2)}, u32[]{:S(2)}) collective-permute-start(f32[6,6,128]{2,1,0:T(8,128)S(1)} %add.110), channel_id=1, source_target_pairs={{0,6},{1,3},{2,4},{3,1},{4,2},{5,7},{6,0},{7,5},{8,14},{9,11},{10,... | collective-permute-start | bytes 55304 | tf_op jit(solution)/shard_map/ppermute | solution.py:63
  186.0 6.1 %collective-permute-done.23 = f32[6,6,128]{2,1,0:T(8,128)S(1)} collective-permute-done((f32[6,6,128]{2,1,0:T(8,128)S(1)}, f32[6,6,128]{2,1,0:T(8,128)S(1)}, u32[]{:S(2)}, u32[]{:S(2)}) %collective-permute-start.23) | collective-permute-done | bytes 18464 | tf_op jit(solution)/shard_map/ppermute | solution.py:63
  192.3 0.1 multiply_reduce_fusion
  192.6 0.6 slice.82.refs_12_
  193.2 3.5 %sum4.1 = bf16[8,592,128]{2,1,0:T(8,128)(2,1)} custom-call(bf16[32,192,128]{2,1,0:T(8,128)(2,1)} %get-tuple-element.118.refs_0_, bf16[32,192,128]{2,1,0:T(8,128)(2,1)} %copy-done.2, bf16[16,192,128]{2,1,0:T(8,128)(2,1)} %copy-done.4, bf16[8,192,128]{2,1,0:T(8,128)(2,1)} %copy-done.11, bf16[32,192,128]{2,1,0:T(8,128)(2,1)} %get-tuple-element.120.refs_2_.refs_3_.refs_4_, ...), custom_call_target="tpu_custom_call" | custom-call | flops 4194304 | bytes 6000000 | tf_op jit(solution)/shard_map/sum4/pallas_call | solution.py:566
  196.7 3.7 %all-to-all-start.2 = ((bf16[8,592,128]{2,1,0:T(8,128)(2,1)}), bf16[8,592,128]{2,1,0:T(8,128)(2,1)S(1)}, u32[]{:S(2)}, u32[]{:S(2)}) async-start(bf16[8,592,128]{2,1,0:T(8,128)(2,1)} %sum4.1), calls=%async_computation.2 | async-start | bytes 2424832 | tf_op jit(solution)/shard_map/all_to_all | solution.py:67
  200.5 0.7 fusion.16
  201.3 1.2 multiply_bitcast_fusion
  202.4 9.1 %all-to-all-done.2 = bf16[8,592,128]{2,1,0:T(8,128)(2,1)S(1)} async-done(((bf16[8,592,128]{2,1,0:T(8,128)(2,1)}), bf16[8,592,128]{2,1,0:T(8,128)(2,1)S(1)}, u32[]{:S(2)}, u32[]{:S(2)}) %all-to-all-start.2) | async-done | bytes 1212448 | tf_op jit(solution)/shard_map/all_to_all | solution.py:67
  211.5 0.2 convert_reduce_fusion
  211.9 0.8 fusion.6
  212.7 0.3 collective-permute-done.24
  213.0 0.6 add_divide_fusion
  (79 shorter events, 1.2 us)
Async XLA Ops:
  0.6 54.5 %copy-start = (s32[2048]{0:T(1024)S(1)}, s32[2048]{0:T(1024)}, u32[]{:S(2)}) copy-start(s32[2048]{0:T(1024)} %param.7) | copy-start | bytes 24580
  0.6 56.0 %collective-permute-start.9 = (bf16[512,4608]{1,0:T(8,128)(2,1)}, bf16[512,4608]{1,0:T(8,128)(2,1)}, u32[]{:S(2)}, u32[]{:S(2)}) collective-permute-start(bf16[512,4608]{1,0:T(8,128)(2,1)} %w.3), channel_id=1, source_target_pairs={{0,1},{1,0},{2,3},{3,2},{4,5},{5,4},{6,7},{7,6},{8,9},{9,8},{10,11... | collective-permute-start | bytes 14155784 | tf_op jit(solution)/shard_map/ppermute | solution.py:63
  19.8 9.5 %collective-permute-start.3 = (bf16[8,192,128]{2,1,0:T(8,128)(2,1)S(1)}, bf16[8,192,128]{2,1,0:T(8,128)(2,1)S(1)}, u32[]{:S(2)}, u32[]{:S(2)}) collective-permute-start(bf16[8,192,128]{2,1,0:T(8,128)(2,1)S(1)} %get-tuple-element.157), channel_id=1, source_target_pairs={{0,24},{1,17},{2,26},{3,19},{4,28},{5,21},{6,30},{7,23},{8,16},{9,... | collective-permute-start | bytes 1179656 | tf_op jit(solution)/shard_map/ppermute | solution.py:63
  22.1 10.1 %collective-permute-start = (bf16[8,208,128]{2,1,0:T(8,128)(2,1)S(1)}, bf16[8,208,128]{2,1,0:T(8,128)(2,1)S(1)}, u32[]{:S(2)}, u32[]{:S(2)}) collective-permute-start(bf16[8,208,128]{2,1,0:T(8,128)(2,1)S(1)} %slice.78), channel_id=1, source_target_pairs={{0,96},{1,33},{2,98},{3,35},{4,100},{5,37},{6,102},{7,39},{8,104},... | collective-permute-start | bytes 1277960 | tf_op jit(solution)/shard_map/ppermute | solution.py:63
  24.3 9.8 %collective-permute-start.6 = (bf16[8,192,128]{2,1,0:T(8,128)(2,1)S(1)}, bf16[8,192,128]{2,1,0:T(8,128)(2,1)S(1)}, u32[]{:S(2)}, u32[]{:S(2)}) collective-permute-start(bf16[8,192,128]{2,1,0:T(8,128)(2,1)S(1)} %get-tuple-element.156), channel_id=1, source_target_pairs={{0,6},{1,3},{2,4},{3,1},{4,2},{5,7},{6,0},{7,5},{8,14},{9,11},{10,... | collective-permute-start | bytes 1179656 | tf_op jit(solution)/shard_map/ppermute | solution.py:63
  29.4 13.3 %collective-permute-start.4 = (bf16[16,192,128]{2,1,0:T(8,128)(2,1)S(1)}, bf16[16,192,128]{2,1,0:T(8,128)(2,1)S(1)}, u32[]{:S(2)}, u32[]{:S(2)}) collective-permute-start(bf16[16,192,128]{2,1,0:T(8,128)(2,1)S(1)} %pad_maximum_fusion.4), channel_id=1, source_target_pairs={{0,6},{1,3},{2,4},{3,1},{4,2},{5,7},{6,0},{7,5},{8,14},{9,11},{10,... | collective-permute-start | bytes 2359304 | tf_op jit(solution)/shard_map/ppermute | solution.py:63
  32.2 14.0 %collective-permute-start.1 = (bf16[16,208,128]{2,1,0:T(8,128)(2,1)S(1)}, bf16[16,208,128]{2,1,0:T(8,128)(2,1)S(1)}, u32[]{:S(2)}, u32[]{:S(2)}) collective-permute-start(bf16[16,208,128]{2,1,0:T(8,128)(2,1)S(1)} %pad_maximum_fusion.3), channel_id=1, source_target_pairs={{0,24},{1,17},{2,26},{3,19},{4,28},{5,21},{6,30},{7,23},{8,16},{9,... | collective-permute-start | bytes 2555912 | tf_op jit(solution)/shard_map/ppermute | solution.py:63
  34.1 14.4 %collective-permute-start.7 = (bf16[16,192,128]{2,1,0:T(8,128)(2,1)S(1)}, bf16[16,192,128]{2,1,0:T(8,128)(2,1)S(1)}, u32[]{:S(2)}, u32[]{:S(2)}) collective-permute-start(bf16[16,192,128]{2,1,0:T(8,128)(2,1)S(1)} %pad_maximum_fusion.5), channel_id=1, source_target_pairs={{0,96},{1,33},{2,98},{3,35},{4,100},{5,37},{6,102},{7,39},{8,104},... | collective-permute-start | bytes 2359304 | tf_op jit(solution)/shard_map/ppermute | solution.py:63
  42.8 3.6 %copy-start.9 = (bf16[32,192,128]{2,1,0:T(8,128)(2,1)}, bf16[32,192,128]{2,1,0:T(8,128)(2,1)S(1)}, u32[]{:S(2)}) copy-start(bf16[32,192,128]{2,1,0:T(8,128)(2,1)S(1)} %pad_maximum_fusion.1.refs_2_) | copy-start | bytes 4718596
  42.8 22.5 %collective-permute-start.5 = (bf16[32,192,128]{2,1,0:T(8,128)(2,1)S(1)}, bf16[32,192,128]{2,1,0:T(8,128)(2,1)}, u32[]{:S(2)}, u32[]{:S(2)}) collective-permute-start(bf16[32,192,128]{2,1,0:T(8,128)(2,1)S(1)} %pad_maximum_fusion.1.refs_2_), channel_id=1, source_target_pairs={{0,96},{1,33},{2,98},{3,35},{4,100},{5,37},{6,102},{7,39},{8,104},... | collective-permute-start | bytes 4718600 | tf_op jit(solution)/shard_map/ppermute | solution.py:63
  46.4 5.0 %copy-start.8 = (bf16[32,208,128]{2,1,0:T(8,128)(2,1)}, bf16[32,208,128]{2,1,0:T(8,128)(2,1)S(1)}, u32[]{:S(2)}) copy-start(bf16[32,208,128]{2,1,0:T(8,128)(2,1)S(1)} %pad_maximum_fusion.refs_0_) | copy-start | bytes 5111812
  46.4 25.4 %collective-permute-start.2 = (bf16[32,208,128]{2,1,0:T(8,128)(2,1)S(1)}, bf16[32,208,128]{2,1,0:T(8,128)(2,1)}, u32[]{:S(2)}, u32[]{:S(2)}) collective-permute-start(bf16[32,208,128]{2,1,0:T(8,128)(2,1)S(1)} %pad_maximum_fusion.refs_0_), channel_id=1, source_target_pairs={{0,6},{1,3},{2,4},{3,1},{4,2},{5,7},{6,0},{7,5},{8,14},{9,11},{10,... | collective-permute-start | bytes 5111816 | tf_op jit(solution)/shard_map/ppermute | solution.py:63
  49.8 21.9 %collective-permute-start.8 = (bf16[32,192,128]{2,1,0:T(8,128)(2,1)}, bf16[32,192,128]{2,1,0:T(8,128)(2,1)}, u32[]{:S(2)}, u32[]{:S(2)}) collective-permute-start(bf16[32,192,128]{2,1,0:T(8,128)(2,1)} %pad_maximum_fusion.2.refs_4_), channel_id=1, source_target_pairs={{0,24},{1,17},{2,26},{3,19},{4,28},{5,21},{6,30},{7,23},{8,16},{9,... | collective-permute-start | bytes 4718600 | tf_op jit(solution)/shard_map/ppermute | solution.py:63
  113.3 25.2 %collective-permute-start.14 = (bf16[4,4608,256]{2,1,0:T(8,128)(2,1)}, bf16[4,4608,256]{2,1,0:T(8,128)(2,1)}, u32[]{:S(2)}, u32[]{:S(2)}) collective-permute-start(bf16[4,4608,256]{2,1,0:T(8,128)(2,1)} %get-tuple-element.115.own_xt), channel_id=1, source_target_pairs={{0,1},{1,0},{2,3},{3,2},{4,5},{5,4},{6,7},{7,6},{8,9},{9,8},{10,11... | collective-permute-start | bytes 28311560 | tf_op jit(solution)/shard_map/ppermute | solution.py:63
  125.2 25.0 %collective-permute-start.10 = (bf16[32,192,128]{2,1,0:T(8,128)(2,1)}, bf16[32,192,128]{2,1,0:T(8,128)(2,1)S(1)}, u32[]{:S(2)}, u32[]{:S(2)}) collective-permute-start(bf16[32,192,128]{2,1,0:T(8,128)(2,1)} %get-tuple-element.100), channel_id=1, source_target_pairs={{0,6},{1,3},{2,4},{3,1},{4,2},{5,7},{6,0},{7,5},{8,14},{9,11},{10,... | collective-permute-start | bytes 4718600 | tf_op jit(solution)/shard_map/ppermute | solution.py:63
  126.7 23.5 %collective-permute-start.11 = (bf16[32,192,128]{2,1,0:T(8,128)(2,1)}, bf16[32,192,128]{2,1,0:T(8,128)(2,1)S(1)}, u32[]{:S(2)}, u32[]{:S(2)}) collective-permute-start(bf16[32,192,128]{2,1,0:T(8,128)(2,1)} %get-tuple-element.101), channel_id=1, source_target_pairs={{0,96},{1,33},{2,98},{3,35},{4,100},{5,37},{6,102},{7,39},{8,104},... | collective-permute-start | bytes 4718600 | tf_op jit(solution)/shard_map/ppermute | solution.py:63
  127.5 22.7 %collective-permute-start.12 = (bf16[32,192,128]{2,1,0:T(8,128)(2,1)}, bf16[32,192,128]{2,1,0:T(8,128)(2,1)}, u32[]{:S(2)}, u32[]{:S(2)}) collective-permute-start(bf16[32,192,128]{2,1,0:T(8,128)(2,1)} %get-tuple-element.102), channel_id=1, source_target_pairs={{0,24},{1,17},{2,26},{3,19},{4,28},{5,21},{6,30},{7,23},{8,16},{9,... | collective-permute-start | bytes 4718600 | tf_op jit(solution)/shard_map/ppermute | solution.py:63
  128.5 10.0 %collective-permute-start.13 = (bf16[4,512,256]{2,1,0:T(8,128)(2,1)}, bf16[4,512,256]{2,1,0:T(8,128)(2,1)}, u32[]{:S(2)}, u32[]{:S(2)}) collective-permute-start(bf16[4,512,256]{2,1,0:T(8,128)(2,1)} %get-tuple-element.109), channel_id=1, source_target_pairs={{0,1},{1,0},{2,3},{3,2},{4,5},{5,4},{6,7},{7,6},{8,9},{9,8},{10,11... | collective-permute-start | bytes 3145736 | tf_op jit(solution)/shard_map/ppermute | solution.py:63
  150.2 1.2 copy-start.2
  150.2 1.7 copy-start.3
  155.5 13.9 %copy-start.14 = (f32[4,6,128]{2,1,0:T(8,128)S(1)}, f32[4,6,128]{2,1,0:T(8,128)}, u32[]{:S(2)}) copy-start(f32[4,6,128]{2,1,0:T(8,128)} %get-tuple-element.133) | copy-start | bytes 36868
  155.5 19.6 %collective-permute-start.15 = (bf16[16,192,128]{2,1,0:T(8,128)(2,1)}, bf16[16,192,128]{2,1,0:T(8,128)(2,1)S(1)}, u32[]{:S(2)}, u32[]{:S(2)}) collective-permute-start(bf16[16,192,128]{2,1,0:T(8,128)(2,1)} %get-tuple-element.130), channel_id=1, source_target_pairs={{0,24},{1,17},{2,26},{3,19},{4,28},{5,21},{6,30},{7,23},{8,16},{9,... | collective-permute-start | bytes 2359304 | tf_op jit(solution)/shard_map/ppermute | solution.py:63
  157.8 17.3 %collective-permute-start.16 = (bf16[16,192,128]{2,1,0:T(8,128)(2,1)}, bf16[16,192,128]{2,1,0:T(8,128)(2,1)S(1)}, u32[]{:S(2)}, u32[]{:S(2)}) collective-permute-start(bf16[16,192,128]{2,1,0:T(8,128)(2,1)} %get-tuple-element.131), channel_id=1, source_target_pairs={{0,6},{1,3},{2,4},{3,1},{4,2},{5,7},{6,0},{7,5},{8,14},{9,11},{10,... | collective-permute-start | bytes 2359304 | tf_op jit(solution)/shard_map/ppermute | solution.py:63
  159.9 15.3 %collective-permute-start.17 = (bf16[16,192,128]{2,1,0:T(8,128)(2,1)}, bf16[16,192,128]{2,1,0:T(8,128)(2,1)S(1)}, u32[]{:S(2)}, u32[]{:S(2)}) collective-permute-start(bf16[16,192,128]{2,1,0:T(8,128)(2,1)} %get-tuple-element.132), channel_id=1, source_target_pairs={{0,96},{1,33},{2,98},{3,35},{4,100},{5,37},{6,102},{7,39},{8,104},... | collective-permute-start | bytes 2359304 | tf_op jit(solution)/shard_map/ppermute | solution.py:63
  170.1 5.0 %collective-permute-start.18 = (f32[6,6,128]{2,1,0:T(8,128)S(1)}, f32[6,6,128]{2,1,0:T(8,128)S(1)}, u32[]{:S(2)}, u32[]{:S(2)}) collective-permute-start(f32[6,6,128]{2,1,0:T(8,128)S(1)} %constant_dynamic-update-slice_fusion), channel_id=1, source_target_pairs={{0,24},{1,17},{2,26},{3,19},{4,28},{5,21},{6,30},{7,23},{8,16},{9,... | collective-permute-start | bytes 55304 | tf_op jit(solution)/shard_map/ppermute | solution.py:63
  175.1 1.2 copy-start.4
  175.1 1.2 copy-start.5
  175.2 1.4 copy-start.6
  175.2 5.1 %collective-permute-start.19 = (f32[6,6,128]{2,1,0:T(8,128)S(1)}, f32[6,6,128]{2,1,0:T(8,128)S(1)}, u32[]{:S(2)}, u32[]{:S(2)}) collective-permute-start(f32[6,6,128]{2,1,0:T(8,128)S(1)} %add.109), channel_id=1, source_target_pairs={{0,96},{1,33},{2,98},{3,35},{4,100},{5,37},{6,102},{7,39},{8,104},... | collective-permute-start | bytes 55304 | tf_op jit(solution)/shard_map/ppermute | solution.py:63
  180.3 11.9 %collective-permute-start.20 = (bf16[8,192,128]{2,1,0:T(8,128)(2,1)}, bf16[8,192,128]{2,1,0:T(8,128)(2,1)S(1)}, u32[]{:S(2)}, u32[]{:S(2)}) collective-permute-start(bf16[8,192,128]{2,1,0:T(8,128)(2,1)} %get-tuple-element.145), channel_id=1, source_target_pairs={{0,96},{1,33},{2,98},{3,35},{4,100},{5,37},{6,102},{7,39},{8,104},... | collective-permute-start | bytes 1179656 | tf_op jit(solution)/shard_map/ppermute | solution.py:63
  181.7 10.5 %collective-permute-start.21 = (bf16[8,192,128]{2,1,0:T(8,128)(2,1)}, bf16[8,192,128]{2,1,0:T(8,128)(2,1)S(1)}, u32[]{:S(2)}, u32[]{:S(2)}) collective-permute-start(bf16[8,192,128]{2,1,0:T(8,128)(2,1)} %get-tuple-element.146), channel_id=1, source_target_pairs={{0,24},{1,17},{2,26},{3,19},{4,28},{5,21},{6,30},{7,23},{8,16},{9,... | collective-permute-start | bytes 1179656 | tf_op jit(solution)/shard_map/ppermute | solution.py:63
  182.7 9.5 %collective-permute-start.22 = (bf16[8,192,128]{2,1,0:T(8,128)(2,1)}, bf16[8,192,128]{2,1,0:T(8,128)(2,1)S(1)}, u32[]{:S(2)}, u32[]{:S(2)}) collective-permute-start(bf16[8,192,128]{2,1,0:T(8,128)(2,1)} %get-tuple-element.147), channel_id=1, source_target_pairs={{0,6},{1,3},{2,4},{3,1},{4,2},{5,7},{6,0},{7,5},{8,14},{9,11},{10,... | collective-permute-start | bytes 1179656 | tf_op jit(solution)/shard_map/ppermute | solution.py:63
  183.6 8.6 %collective-permute-start.23 = (f32[6,6,128]{2,1,0:T(8,128)S(1)}, f32[6,6,128]{2,1,0:T(8,128)S(1)}, u32[]{:S(2)}, u32[]{:S(2)}) collective-permute-start(f32[6,6,128]{2,1,0:T(8,128)S(1)} %add.110), channel_id=1, source_target_pairs={{0,6},{1,3},{2,4},{3,1},{4,2},{5,7},{6,0},{7,5},{8,14},{9,11},{10,... | collective-permute-start | bytes 55304 | tf_op jit(solution)/shard_map/ppermute | solution.py:63
  192.2 1.0 copy-start.11
  192.2 1.0 copy-start.12
  192.2 1.0 copy-start.13
  196.7 4.5 %copy-start.7 = (f32[64,16,128]{2,1,0:T(8,128)S(1)}, f32[64,16,128]{2,1,0:T(8,128)}, u32[]{:S(2)}) copy-start(f32[64,16,128]{2,1,0:T(8,128)} %all_to_all.16.totals_ref) | copy-start | bytes 1572868
  196.7 14.8 %all-to-all-start.2 = ((bf16[8,592,128]{2,1,0:T(8,128)(2,1)}), bf16[8,592,128]{2,1,0:T(8,128)(2,1)S(1)}, u32[]{:S(2)}, u32[]{:S(2)}) async-start(bf16[8,592,128]{2,1,0:T(8,128)(2,1)} %sum4.1), calls=%async_computation.2 | async-start | bytes 2424832 | tf_op jit(solution)/shard_map/all_to_all | solution.py:67
  200.4 11.4 %copy-start.10 = (bf16[128,576]{0,1:T(8,128)(2,1)S(1)}, bf16[128,576]{0,1:T(8,128)(2,1)}, u32[]{:S(2)}) copy-start(bf16[128,576]{0,1:T(8,128)(2,1)} %param.4) | copy-start | bytes 442372
  200.5 12.5 %copy-start.15 = (bf16[576]{0:T(1024)(128)(2,1)S(1)}, bf16[576]{0:T(1024)(128)(2,1)}, u32[]{:S(2)}) copy-start(bf16[576]{0:T(1024)(128)(2,1)} %param.5) | copy-start | bytes 3460
  200.5 13.1 %copy-start.1 = (s32[2048]{0:T(1024)S(1)}, s32[2048]{0:T(1024)}, u32[]{:S(2)}) copy-start(s32[2048]{0:T(1024)} %param.7) | copy-start | bytes 24580
  211.7 1.2 collective-permute-start.24

commit v5 on v4

--- a/solution.py
+++ b/solution.py
@@ -382,7 +382,7 @@
     outgoing = copies(list(zip(by_rows + (gz, gy) + away, out_refs)), out_sems)
     for copy in incoming:
         copy.start()
-    rows = 64
+    rows = 128
     inv = 1.0 / jnp.sum(totals_ref[...], axis=0)[0:8]
     line = lax.broadcasted_iota(jnp.int32, (8, TB), 0)
 

time: 215 us -> 215 us (level)
  no operation moved by 1% of the time
where the time goes in v5:
time: 215 us; the launch traced here: 214 us
  Pallas kernels  82.7 us (38%)
  starting transfers between devices  41.5 us (19%)
  waiting for transfers between devices  36.4 us (17%)
  blocking collectives  35.4 us (16%)
  local copies, waits for them, and re-layouts  7.18 us (3%)
  other arithmetic  6.75 us (3%)
  between operations  3.7 us (2%)
    ppermute x25, starting transfers between devices, send(): return lax.ppermute(a, AX, pairs)  37.8 us
    ppermute x25, waiting for transfers between devices, send(): return lax.ppermute(a, AX, pairs)  27.3 us
    pallas_call x1, Pallas kernels, act_call(): pl.pallas_call(act_kernel, grid_spec=pltpu.PrefetchScalarGridSpec(num_sca...  23 us
    pallas_call x2, Pallas kernels, head_call(): pl.pallas_call(head_kernel, grid=(count,), in_specs=[rows, rows, tokens,...  19 us
    all_to_all x1, blocking collectives, shards(): stats = lax.all_to_all(stats, AX[:4], 0, 0)  18.5 us
    all_to_all x1, blocking collectives, in_cube(): return lax.all_to_all(a, AX, 0, 0, axis_index_groups=CUBES)  16.9 us
    pallas_call x1, Pallas kernels, grad_call(): pl.pallas_call(grad_kernel, in_specs=[SMEM_SPEC, ANYWHERE] + [VMEM_SPEC]...  11.9 us
    pallas_call x3, Pallas kernels, sum_call(): pl.pallas_call(functools.partial(sum_kernel, terms), grid=(count // step,...  10.2 us
  transfers between devices with their start and end apart: 26, of which 9 were waited for; matrix products, arithmetic and copies ran while one was open for 5% of the time, Pallas kernels for 25%

profile of v5, /device:TPU:0, one launch (start us, length us, event | category | flops | bytes accessed | tf_op | source)
XLA Modules:
  0.0 213.6 jit_solution(9084347152792306202)
XLA Ops:
  0.7 0.7 convert_element_type.74
  1.4 1.1 fusion.1
  2.5 0.2 concatenate.33
  2.7 0.2 broadcast_in_dim.5
  2.9 16.9 %all_to_all.15 = bf16[8,592,128]{2,1,0:T(8,128)(2,1)S(1)} all-to-all(bf16[8,592,128]{2,1,0:T(8,128)(2,1)S(1)} %broadcast_in_dim.5), channel_id=1, replica_groups={{0,2,16,18,32,34,48,50},{6,4,22,20,38,36,54,52},{24,26,8,10,56,58,40,42..., dimensions={0} | all-to-all | bytes 2424832 | tf_op jit(solution)/shard_map/all_to_all | solution.py:67
  19.8 2.3 %collective-permute-start.3 = (bf16[8,192,128]{2,1,0:T(8,128)(2,1)S(1)}, bf16[8,192,128]{2,1,0:T(8,128)(2,1)S(1)}, u32[]{:S(2)}, u32[]{:S(2)}) collective-permute-start(bf16[8,192,128]{2,1,0:T(8,128)(2,1)S(1)} %get-tuple-element.157), channel_id=1, source_target_pairs={{0,24},{1,17},{2,26},{3,19},{4,28},{5,21},{6,30},{7,23},{8,16},{9,... | collective-permute-start | bytes 1179656 | tf_op jit(solution)/shard_map/ppermute | solution.py:63
  22.1 2.2 %collective-permute-start = (bf16[8,208,128]{2,1,0:T(8,128)(2,1)S(1)}, bf16[8,208,128]{2,1,0:T(8,128)(2,1)S(1)}, u32[]{:S(2)}, u32[]{:S(2)}) collective-permute-start(bf16[8,208,128]{2,1,0:T(8,128)(2,1)S(1)} %slice.78), channel_id=1, source_target_pairs={{0,96},{1,33},{2,98},{3,35},{4,100},{5,37},{6,102},{7,39},{8,104},... | collective-permute-start | bytes 1277960 | tf_op jit(solution)/shard_map/ppermute | solution.py:63
  24.3 3.0 %collective-permute-start.6 = (bf16[8,192,128]{2,1,0:T(8,128)(2,1)S(1)}, bf16[8,192,128]{2,1,0:T(8,128)(2,1)S(1)}, u32[]{:S(2)}, u32[]{:S(2)}) collective-permute-start(bf16[8,192,128]{2,1,0:T(8,128)(2,1)S(1)} %get-tuple-element.156), channel_id=1, source_target_pairs={{0,6},{1,3},{2,4},{3,1},{4,2},{5,7},{6,0},{7,5},{8,14},{9,11},{10,... | collective-permute-start | bytes 1179656 | tf_op jit(solution)/shard_map/ppermute | solution.py:63
  27.3 2.0 collective-permute-done.3
  29.4 2.8 %collective-permute-start.4 = (bf16[16,192,128]{2,1,0:T(8,128)(2,1)S(1)}, bf16[16,192,128]{2,1,0:T(8,128)(2,1)S(1)}, u32[]{:S(2)}, u32[]{:S(2)}) collective-permute-start(bf16[16,192,128]{2,1,0:T(8,128)(2,1)S(1)} %pad_maximum_fusion.4), channel_id=1, source_target_pairs={{0,6},{1,3},{2,4},{3,1},{4,2},{5,7},{6,0},{7,5},{8,14},{9,11},{10,... | collective-permute-start | bytes 2359304 | tf_op jit(solution)/shard_map/ppermute | solution.py:63
  32.2 1.8 collective-permute-start.1
  34.1 2.5 %collective-permute-start.7 = (bf16[16,192,128]{2,1,0:T(8,128)(2,1)S(1)}, bf16[16,192,128]{2,1,0:T(8,128)(2,1)S(1)}, u32[]{:S(2)}, u32[]{:S(2)}) collective-permute-start(bf16[16,192,128]{2,1,0:T(8,128)(2,1)S(1)} %pad_maximum_fusion.5), channel_id=1, source_target_pairs={{0,96},{1,33},{2,98},{3,35},{4,100},{5,37},{6,102},{7,39},{8,104},... | collective-permute-start | bytes 2359304 | tf_op jit(solution)/shard_map/ppermute | solution.py:63
  36.6 6.0 %collective-permute-done.4 = bf16[16,192,128]{2,1,0:T(8,128)(2,1)S(1)} collective-permute-done((bf16[16,192,128]{2,1,0:T(8,128)(2,1)S(1)}, bf16[16,192,128]{2,1,0:T(8,128)(2,1)S(1)}, u32[]{:S(2)}, u32[]{:S(2)}) %collective-permute-start.4) | collective-permute-done | bytes 786464 | tf_op jit(solution)/shard_map/ppermute | solution.py:63
  42.6 0.2 pad_maximum_fusion.1.refs_2_
  42.8 1.7 collective-permute-start.5
  44.6 1.6 collective-permute-done.1
  46.2 0.2 pad_maximum_fusion.refs_0_
  46.4 2.1 collective-permute-start.2
  48.5 1.3 pad_maximum_fusion.2.refs_4_
  49.8 1.5 collective-permute-start.8
  51.3 0.6 fusion.19
  53.2 0.6 fusion.18
  55.2 0.6 copy.14
  55.9 0.7 concatenate.40.tab
  56.6 8.7 %flip.1 = (bf16[2,4,192,1024]{3,2,1,0:T(8,128)(2,1)}, bf16[4,2,192,1024]{3,2,1,0:T(8,128)(2,1)}, bf16[2,4,192,1024]{3,2,1,0:T(8,128)(2,1)}) custom-call(bf16[512,4608]{1,0:T(8,128)(2,1)} %w.3, bf16[512,4608]{1,0:T(8,128)(2,1)} %collective-permute-done.9.other_ref.refs_7_), custom_call_target="tpu_custom_call" | custom-call | bytes 18874368 | tf_op jit(solution)/shard_map/flip/pallas_call | solution.py:133
  65.3 6.5 %collective-permute-done.8.refs_5_ = bf16[32,192,128]{2,1,0:T(8,128)(2,1)} collective-permute-done((bf16[32,192,128]{2,1,0:T(8,128)(2,1)}, bf16[32,192,128]{2,1,0:T(8,128)(2,1)}, u32[]{:S(2)}, u32[]{:S(2)}) %collective-permute-start.8) | collective-permute-done | bytes 1572896 | tf_op jit(solution)/shard_map/ppermute | solution.py:63
  71.8 23.0 %act.1 = (f32[4,1024,256]{2,1,0:T(8,128)}, f32[4,1,256]{2,1,0:T(1,128)}, f32[4,1,256]{2,1,0:T(1,128)}, f32[64,16,128]{2,1,0:T(8,128)}, bf16[4,4608,256]{2,1,0:T(8,128)(2,1)}) custom-call(s32[26]{0:T(128)} %concatenate.40.tab, bf16[32,208,128]{2,1,0:T(8,128)(2,1)} %copy-done.8, bf16[32,208,128]{2,1,0:T(8,128)(2,1)} %collective-permute-done.2.refs_1_, ...), custom_call_target="tpu_custom_call" | custom-call | flops 9663676416 | bytes 30000000 | tf_op jit(solution)/shard_map/act/pallas_call | solution.py:286
  94.8 18.5 %all_to_all.16.totals_ref = f32[64,16,128]{2,1,0:T(8,128)} all-to-all(f32[64,16,128]{2,1,0:T(8,128)} %get-tuple-element.91), channel_id=1, replica_groups=mesh['x'=4,'ylo'=2,'yhi'=2,'z'=4,'core'=2] {'x','ylo','yhi','z'}, dimensions={0} | all-to-all | bytes 1048576 | tf_op jit(solution)/shard_map/all_to_all | solution.py:604
  113.3 11.9 %grad.1 = (bf16[4,512,256]{2,1,0:T(8,128)(2,1)}, bf16[4,512,256]{2,1,0:T(8,128)(2,1)}, bf16[4,1024,256]{2,1,0:T(8,128)(2,1)}, bf16[2,2,1024,256]{3,2,1,0:T(8,128...) custom-call(s32[26]{0:T(128)} %concatenate.40.tab, ...), custom_call_target="tpu_custom_call" | custom-call | flops 4831838208 | bytes 24000000 | tf_op jit(solution)/shard_map/grad/pallas_call | solution.py:467
  125.2 1.5 collective-permute-start.10
  126.7 0.8 collective-permute-start.11
  127.5 1.0 collective-permute-start.12
  128.5 10.0 %keep.1 = (bf16[32,192,128]{2,1,0:T(8,128)(2,1)}, bf16[32,192,128]{2,1,0:T(8,128)(2,1)}, bf16[32,192,128]{2,1,0:T(8,128)(2,1)}) custom-call(s32[26]{0:T(128)} %concatenate.40.tab, bf16[4,1024,256]{2,1,0:T(8,128)(2,1)} %get-tuple-element.103.gz_ref, bf16[2,2,1024,256]{3,2,1,0:T(8,128)(2,1)} %get-tuple-element.104.gy_ref, ...), custom_call_target="tpu_custom_call" | custom-call | flops 4718592 | bytes 1000000 | tf_op jit(solution)/shard_map/keep/pallas_call | solution.py:484
  138.5 11.7 %head.2 = (bf16[512,4608]{1,0:T(8,128)(2,1)}, f32[4,6,128]{2,1,0:T(8,128)}) custom-call(bf16[4,512,256]{2,1,0:T(8,128)(2,1)} %get-tuple-element.134.own_gr, bf16[4,512,256]{2,1,0:T(8,128)(2,1)} %collective-permute-done.13.twin_gr, bf16[4,4608,256]{2,1,0:T(8,128)(2,1)} %get-tuple-element.115.own_xt, bf16[4,4608,256]{2,1,0:T(8,128)(2,1)} %collective-permute-done.14.twin_xt, ...), custom_call_target="tpu_custom_call" | custom-call | flops 4718592 | bytes 1000000 | tf_op jit(solution)/shard_map/head/pallas_call | solution.py:521
  150.2 1.1 copy-done.2
  151.4 0.5 copy-done.3
  151.9 3.6 %sum2.1 = (bf16[16,192,128]{2,1,0:T(8,128)(2,1)}, bf16[16,192,128]{2,1,0:T(8,128)(2,1)}, bf16[16,192,128]{2,1,0:T(8,128)(2,1)}) custom-call(bf16[32,192,128]{2,1,0:T(8,128)(2,1)} %get-tuple-element.118.refs_0_, bf16[32,192,128]{2,1,0:T(8,128)(2,1)} %copy-done.2, bf16[32,192,128]{2,1,0:T(8,128)(2,1)} %get-tuple-element.120.refs_2_.refs_3_.refs_4_, ...), custom_call_target="tpu_custom_call" | custom-call | flops 4194304 | bytes 6000000 | tf_op jit(solution)/shard_map/sum2/pallas_call | solution.py:566
  155.5 2.3 %collective-permute-start.15 = (bf16[16,192,128]{2,1,0:T(8,128)(2,1)}, bf16[16,192,128]{2,1,0:T(8,128)(2,1)S(1)}, u32[]{:S(2)}, u32[]{:S(2)}) collective-permute-start(bf16[16,192,128]{2,1,0:T(8,128)(2,1)} %get-tuple-element.130), channel_id=1, source_target_pairs={{0,24},{1,17},{2,26},{3,19},{4,28},{5,21},{6,30},{7,23},{8,16},{9,... | collective-permute-start | bytes 2359304 | tf_op jit(solution)/shard_map/ppermute | solution.py:63
  157.8 2.0 collective-permute-start.16
  159.9 2.2 %collective-permute-start.17 = (bf16[16,192,128]{2,1,0:T(8,128)(2,1)}, bf16[16,192,128]{2,1,0:T(8,128)(2,1)S(1)}, u32[]{:S(2)}, u32[]{:S(2)}) collective-permute-start(bf16[16,192,128]{2,1,0:T(8,128)(2,1)} %get-tuple-element.132), channel_id=1, source_target_pairs={{0,96},{1,33},{2,98},{3,35},{4,100},{5,37},{6,102},{7,39},{8,104},... | collective-permute-start | bytes 2359304 | tf_op jit(solution)/shard_map/ppermute | solution.py:63
  162.0 7.3 %head.3 = (bf16[512,4608]{1,0:T(8,128)(2,1)}, f32[2,6,128]{2,1,0:T(8,128)}) custom-call(bf16[4,512,256]{2,1,0:T(8,128)(2,1)} %get-tuple-element.134.own_gr, bf16[4,512,256]{2,1,0:T(8,128)(2,1)} %collective-permute-done.13.twin_gr, bf16[4,4608,256]{2,1,0:T(8,128)(2,1)} %get-tuple-element.115.own_xt, ...), custom_call_target="tpu_custom_call", output_to_operand_aliasing={{0}: (5, {})} | custom-call | flops 4718592 | bytes 1000000 | tf_op jit(solution)/shard_map/head/pallas_call | solution.py:521
  169.4 0.7 constant_dynamic-update-slice_fusion
  170.1 1.0 collective-permute-start.18
  171.1 4.0 %collective-permute-done.18 = f32[6,6,128]{2,1,0:T(8,128)S(1)} collective-permute-done((f32[6,6,128]{2,1,0:T(8,128)S(1)}, f32[6,6,128]{2,1,0:T(8,128)S(1)}, u32[]{:S(2)}, u32[]{:S(2)}) %collective-permute-start.18) | collective-permute-done | bytes 18464 | tf_op jit(solution)/shard_map/ppermute | solution.py:63
  175.2 1.1 collective-permute-start.19
  176.3 0.3 copy-done.6
  176.6 3.1 %sum3.1 = (bf16[8,192,128]{2,1,0:T(8,128)(2,1)}, bf16[8,192,128]{2,1,0:T(8,128)(2,1)}, bf16[8,192,128]{2,1,0:T(8,128)(2,1)}) custom-call(bf16[32,192,128]{2,1,0:T(8,128)(2,1)} %get-tuple-element.118.refs_0_, bf16[32,192,128]{2,1,0:T(8,128)(2,1)} %copy-done.2, bf16[16,192,128]{2,1,0:T(8,128)(2,1)} %copy-done.4, ...), custom_call_target="tpu_custom_call" | custom-call | flops 4194304 | bytes 6000000 | tf_op jit(solution)/shard_map/sum3/pallas_call | solution.py:566
  179.7 0.6 collective-permute-done.19
  180.3 1.4 collective-permute-start.20
  181.7 1.0 collective-permute-start.21
  182.7 0.9 collective-permute-start.22
  183.6 2.4 %collective-permute-start.23 = (f32[6,6,128]{2,1,0:T(8,128)S(1)}, f32[6,6,128]{2,1,0:T(8,128)S(1)}, u32[]{:S(2)}, u32[]{:S(2)}) collective-permute-start(f32[6,6,128]{2,1,0:T(8,128)S(1)} %add.110), channel_id=1, source_target_pairs={{0,6},{1,3},{2,4},{3,1},{4,2},{5,7},{6,0},{7,5},{8,14},{9,11},{10,... | collective-permute-start | bytes 55304 | tf_op jit(solution)/shard_map/ppermute | solution.py:63
  186.0 6.1 %collective-permute-done.23 = f32[6,6,128]{2,1,0:T(8,128)S(1)} collective-permute-done((f32[6,6,128]{2,1,0:T(8,128)S(1)}, f32[6,6,128]{2,1,0:T(8,128)S(1)}, u32[]{:S(2)}, u32[]{:S(2)}) %collective-permute-start.23) | collective-permute-done | bytes 18464 | tf_op jit(solution)/shard_map/ppermute | solution.py:63
  192.3 0.1 multiply_reduce_fusion
  192.6 0.6 slice.82.refs_12_
  193.2 3.5 %sum4.1 = bf16[8,592,128]{2,1,0:T(8,128)(2,1)} custom-call(bf16[32,192,128]{2,1,0:T(8,128)(2,1)} %get-tuple-element.118.refs_0_, bf16[32,192,128]{2,1,0:T(8,128)(2,1)} %copy-done.2, bf16[16,192,128]{2,1,0:T(8,128)(2,1)} %copy-done.4, bf16[8,192,128]{2,1,0:T(8,128)(2,1)} %copy-done.11, bf16[32,192,128]{2,1,0:T(8,128)(2,1)} %get-tuple-element.120.refs_2_.refs_3_.refs_4_, ...), custom_call_target="tpu_custom_call" | custom-call | flops 4194304 | bytes 6000000 | tf_op jit(solution)/shard_map/sum4/pallas_call | solution.py:566
  196.7 3.7 %all-to-all-start.2 = ((bf16[8,592,128]{2,1,0:T(8,128)(2,1)}), bf16[8,592,128]{2,1,0:T(8,128)(2,1)S(1)}, u32[]{:S(2)}, u32[]{:S(2)}) async-start(bf16[8,592,128]{2,1,0:T(8,128)(2,1)} %sum4.1), calls=%async_computation.2 | async-start | bytes 2424832 | tf_op jit(solution)/shard_map/all_to_all | solution.py:67
  200.5 0.7 fusion.16
  201.3 1.2 multiply_bitcast_fusion
  202.4 9.1 %all-to-all-done.2 = bf16[8,592,128]{2,1,0:T(8,128)(2,1)S(1)} async-done(((bf16[8,592,128]{2,1,0:T(8,128)(2,1)}), bf16[8,592,128]{2,1,0:T(8,128)(2,1)S(1)}, u32[]{:S(2)}, u32[]{:S(2)}) %all-to-all-start.2) | async-done | bytes 1212448 | tf_op jit(solution)/shard_map/all_to_all | solution.py:67
  211.5 0.2 convert_reduce_fusion
  211.9 0.8 fusion.6
  212.7 0.3 collective-permute-done.24
  213.0 0.6 add_divide_fusion
  (79 shorter events, 1.2 us)
Async XLA Ops:
  0.6 54.5 %copy-start = (s32[2048]{0:T(1024)S(1)}, s32[2048]{0:T(1024)}, u32[]{:S(2)}) copy-start(s32[2048]{0:T(1024)} %param.7) | copy-start | bytes 24580
  0.6 56.0 %collective-permute-start.9 = (bf16[512,4608]{1,0:T(8,128)(2,1)}, bf16[512,4608]{1,0:T(8,128)(2,1)}, u32[]{:S(2)}, u32[]{:S(2)}) collective-permute-start(bf16[512,4608]{1,0:T(8,128)(2,1)} %w.3), channel_id=1, source_target_pairs={{0,1},{1,0},{2,3},{3,2},{4,5},{5,4},{6,7},{7,6},{8,9},{9,8},{10,11... | collective-permute-start | bytes 14155784 | tf_op jit(solution)/shard_map/ppermute | solution.py:63
  19.8 9.5 %collective-permute-start.3 = (bf16[8,192,128]{2,1,0:T(8,128)(2,1)S(1)}, bf16[8,192,128]{2,1,0:T(8,128)(2,1)S(1)}, u32[]{:S(2)}, u32[]{:S(2)}) collective-permute-start(bf16[8,192,128]{2,1,0:T(8,128)(2,1)S(1)} %get-tuple-element.157), channel_id=1, source_target_pairs={{0,24},{1,17},{2,26},{3,19},{4,28},{5,21},{6,30},{7,23},{8,16},{9,... | collective-permute-start | bytes 1179656 | tf_op jit(solution)/shard_map/ppermute | solution.py:63
  22.1 10.1 %collective-permute-start = (bf16[8,208,128]{2,1,0:T(8,128)(2,1)S(1)}, bf16[8,208,128]{2,1,0:T(8,128)(2,1)S(1)}, u32[]{:S(2)}, u32[]{:S(2)}) collective-permute-start(bf16[8,208,128]{2,1,0:T(8,128)(2,1)S(1)} %slice.78), channel_id=1, source_target_pairs={{0,96},{1,33},{2,98},{3,35},{4,100},{5,37},{6,102},{7,39},{8,104},... | collective-permute-start | bytes 1277960 | tf_op jit(solution)/shard_map/ppermute | solution.py:63
  24.3 9.8 %collective-permute-start.6 = (bf16[8,192,128]{2,1,0:T(8,128)(2,1)S(1)}, bf16[8,192,128]{2,1,0:T(8,128)(2,1)S(1)}, u32[]{:S(2)}, u32[]{:S(2)}) collective-permute-start(bf16[8,192,128]{2,1,0:T(8,128)(2,1)S(1)} %get-tuple-element.156), channel_id=1, source_target_pairs={{0,6},{1,3},{2,4},{3,1},{4,2},{5,7},{6,0},{7,5},{8,14},{9,11},{10,... | collective-permute-start | bytes 1179656 | tf_op jit(solution)/shard_map/ppermute | solution.py:63
  29.4 13.3 %collective-permute-start.4 = (bf16[16,192,128]{2,1,0:T(8,128)(2,1)S(1)}, bf16[16,192,128]{2,1,0:T(8,128)(2,1)S(1)}, u32[]{:S(2)}, u32[]{:S(2)}) collective-permute-start(bf16[16,192,128]{2,1,0:T(8,128)(2,1)S(1)} %pad_maximum_fusion.4), channel_id=1, source_target_pairs={{0,6},{1,3},{2,4},{3,1},{4,2},{5,7},{6,0},{7,5},{8,14},{9,11},{10,... | collective-permute-start | bytes 2359304 | tf_op jit(solution)/shard_map/ppermute | solution.py:63
  32.2 14.0 %collective-permute-start.1 = (bf16[16,208,128]{2,1,0:T(8,128)(2,1)S(1)}, bf16[16,208,128]{2,1,0:T(8,128)(2,1)S(1)}, u32[]{:S(2)}, u32[]{:S(2)}) collective-permute-start(bf16[16,208,128]{2,1,0:T(8,128)(2,1)S(1)} %pad_maximum_fusion.3), channel_id=1, source_target_pairs={{0,24},{1,17},{2,26},{3,19},{4,28},{5,21},{6,30},{7,23},{8,16},{9,... | collective-permute-start | bytes 2555912 | tf_op jit(solution)/shard_map/ppermute | solution.py:63
  34.1 14.4 %collective-permute-start.7 = (bf16[16,192,128]{2,1,0:T(8,128)(2,1)S(1)}, bf16[16,192,128]{2,1,0:T(8,128)(2,1)S(1)}, u32[]{:S(2)}, u32[]{:S(2)}) collective-permute-start(bf16[16,192,128]{2,1,0:T(8,128)(2,1)S(1)} %pad_maximum_fusion.5), channel_id=1, source_target_pairs={{0,96},{1,33},{2,98},{3,35},{4,100},{5,37},{6,102},{7,39},{8,104},... | collective-permute-start | bytes 2359304 | tf_op jit(solution)/shard_map/ppermute | solution.py:63
  42.8 3.6 %copy-start.9 = (bf16[32,192,128]{2,1,0:T(8,128)(2,1)}, bf16[32,192,128]{2,1,0:T(8,128)(2,1)S(1)}, u32[]{:S(2)}) copy-start(bf16[32,192,128]{2,1,0:T(8,128)(2,1)S(1)} %pad_maximum_fusion.1.refs_2_) | copy-start | bytes 4718596
  42.8 22.5 %collective-permute-start.5 = (bf16[32,192,128]{2,1,0:T(8,128)(2,1)S(1)}, bf16[32,192,128]{2,1,0:T(8,128)(2,1)}, u32[]{:S(2)}, u32[]{:S(2)}) collective-permute-start(bf16[32,192,128]{2,1,0:T(8,128)(2,1)S(1)} %pad_maximum_fusion.1.refs_2_), channel_id=1, source_target_pairs={{0,96},{1,33},{2,98},{3,35},{4,100},{5,37},{6,102},{7,39},{8,104},... | collective-permute-start | bytes 4718600 | tf_op jit(solution)/shard_map/ppermute | solution.py:63
  46.4 5.0 %copy-start.8 = (bf16[32,208,128]{2,1,0:T(8,128)(2,1)}, bf16[32,208,128]{2,1,0:T(8,128)(2,1)S(1)}, u32[]{:S(2)}) copy-start(bf16[32,208,128]{2,1,0:T(8,128)(2,1)S(1)} %pad_maximum_fusion.refs_0_) | copy-start | bytes 5111812
  46.4 25.4 %collective-permute-start.2 = (bf16[32,208,128]{2,1,0:T(8,128)(2,1)S(1)}, bf16[32,208,128]{2,1,0:T(8,128)(2,1)}, u32[]{:S(2)}, u32[]{:S(2)}) collective-permute-start(bf16[32,208,128]{2,1,0:T(8,128)(2,1)S(1)} %pad_maximum_fusion.refs_0_), channel_id=1, source_target_pairs={{0,6},{1,3},{2,4},{3,1},{4,2},{5,7},{6,0},{7,5},{8,14},{9,11},{10,... | collective-permute-start | bytes 5111816 | tf_op jit(solution)/shard_map/ppermute | solution.py:63
  49.8 21.9 %collective-permute-start.8 = (bf16[32,192,128]{2,1,0:T(8,128)(2,1)}, bf16[32,192,128]{2,1,0:T(8,128)(2,1)}, u32[]{:S(2)}, u32[]{:S(2)}) collective-permute-start(bf16[32,192,128]{2,1,0:T(8,128)(2,1)} %pad_maximum_fusion.2.refs_4_), channel_id=1, source_target_pairs={{0,24},{1,17},{2,26},{3,19},{4,28},{5,21},{6,30},{7,23},{8,16},{9,... | collective-permute-start | bytes 4718600 | tf_op jit(solution)/shard_map/ppermute | solution.py:63
  113.3 25.2 %collective-permute-start.14 = (bf16[4,4608,256]{2,1,0:T(8,128)(2,1)}, bf16[4,4608,256]{2,1,0:T(8,128)(2,1)}, u32[]{:S(2)}, u32[]{:S(2)}) collective-permute-start(bf16[4,4608,256]{2,1,0:T(8,128)(2,1)} %get-tuple-element.115.own_xt), channel_id=1, source_target_pairs={{0,1},{1,0},{2,3},{3,2},{4,5},{5,4},{6,7},{7,6},{8,9},{9,8},{10,11... | collective-permute-start | bytes 28311560 | tf_op jit(solution)/shard_map/ppermute | solution.py:63
  125.2 25.0 %collective-permute-start.10 = (bf16[32,192,128]{2,1,0:T(8,128)(2,1)}, bf16[32,192,128]{2,1,0:T(8,128)(2,1)S(1)}, u32[]{:S(2)}, u32[]{:S(2)}) collective-permute-start(bf16[32,192,128]{2,1,0:T(8,128)(2,1)} %get-tuple-element.100), channel_id=1, source_target_pairs={{0,6},{1,3},{2,4},{3,1},{4,2},{5,7},{6,0},{7,5},{8,14},{9,11},{10,... | collective-permute-start | bytes 4718600 | tf_op jit(solution)/shard_map/ppermute | solution.py:63
  126.7 23.5 %collective-permute-start.11 = (bf16[32,192,128]{2,1,0:T(8,128)(2,1)}, bf16[32,192,128]{2,1,0:T(8,128)(2,1)S(1)}, u32[]{:S(2)}, u32[]{:S(2)}) collective-permute-start(bf16[32,192,128]{2,1,0:T(8,128)(2,1)} %get-tuple-element.101), channel_id=1, source_target_pairs={{0,96},{1,33},{2,98},{3,35},{4,100},{5,37},{6,102},{7,39},{8,104},... | collective-permute-start | bytes 4718600 | tf_op jit(solution)/shard_map/ppermute | solution.py:63
  127.5 22.7 %collective-permute-start.12 = (bf16[32,192,128]{2,1,0:T(8,128)(2,1)}, bf16[32,192,128]{2,1,0:T(8,128)(2,1)}, u32[]{:S(2)}, u32[]{:S(2)}) collective-permute-start(bf16[32,192,128]{2,1,0:T(8,128)(2,1)} %get-tuple-element.102), channel_id=1, source_target_pairs={{0,24},{1,17},{2,26},{3,19},{4,28},{5,21},{6,30},{7,23},{8,16},{9,... | collective-permute-start | bytes 4718600 | tf_op jit(solution)/shard_map/ppermute | solution.py:63
  128.5 10.0 %collective-permute-start.13 = (bf16[4,512,256]{2,1,0:T(8,128)(2,1)}, bf16[4,512,256]{2,1,0:T(8,128)(2,1)}, u32[]{:S(2)}, u32[]{:S(2)}) collective-permute-start(bf16[4,512,256]{2,1,0:T(8,128)(2,1)} %get-tuple-element.109), channel_id=1, source_target_pairs={{0,1},{1,0},{2,3},{3,2},{4,5},{5,4},{6,7},{7,6},{8,9},{9,8},{10,11... | collective-permute-start | bytes 3145736 | tf_op jit(solution)/shard_map/ppermute | solution.py:63
  150.2 1.2 copy-start.2
  150.2 1.7 copy-start.3
  155.5 13.9 %copy-start.14 = (f32[4,6,128]{2,1,0:T(8,128)S(1)}, f32[4,6,128]{2,1,0:T(8,128)}, u32[]{:S(2)}) copy-start(f32[4,6,128]{2,1,0:T(8,128)} %get-tuple-element.133) | copy-start | bytes 36868
  155.5 19.6 %collective-permute-start.15 = (bf16[16,192,128]{2,1,0:T(8,128)(2,1)}, bf16[16,192,128]{2,1,0:T(8,128)(2,1)S(1)}, u32[]{:S(2)}, u32[]{:S(2)}) collective-permute-start(bf16[16,192,128]{2,1,0:T(8,128)(2,1)} %get-tuple-element.130), channel_id=1, source_target_pairs={{0,24},{1,17},{2,26},{3,19},{4,28},{5,21},{6,30},{7,23},{8,16},{9,... | collective-permute-start | bytes 2359304 | tf_op jit(solution)/shard_map/ppermute | solution.py:63
  157.8 17.3 %collective-permute-start.16 = (bf16[16,192,128]{2,1,0:T(8,128)(2,1)}, bf16[16,192,128]{2,1,0:T(8,128)(2,1)S(1)}, u32[]{:S(2)}, u32[]{:S(2)}) collective-permute-start(bf16[16,192,128]{2,1,0:T(8,128)(2,1)} %get-tuple-element.131), channel_id=1, source_target_pairs={{0,6},{1,3},{2,4},{3,1},{4,2},{5,7},{6,0},{7,5},{8,14},{9,11},{10,... | collective-permute-start | bytes 2359304 | tf_op jit(solution)/shard_map/ppermute | solution.py:63
  159.9 15.3 %collective-permute-start.17 = (bf16[16,192,128]{2,1,0:T(8,128)(2,1)}, bf16[16,192,128]{2,1,0:T(8,128)(2,1)S(1)}, u32[]{:S(2)}, u32[]{:S(2)}) collective-permute-start(bf16[16,192,128]{2,1,0:T(8,128)(2,1)} %get-tuple-element.132), channel_id=1, source_target_pairs={{0,96},{1,33},{2,98},{3,35},{4,100},{5,37},{6,102},{7,39},{8,104},... | collective-permute-start | bytes 2359304 | tf_op jit(solution)/shard_map/ppermute | solution.py:63
  170.1 5.0 %collective-permute-start.18 = (f32[6,6,128]{2,1,0:T(8,128)S(1)}, f32[6,6,128]{2,1,0:T(8,128)S(1)}, u32[]{:S(2)}, u32[]{:S(2)}) collective-permute-start(f32[6,6,128]{2,1,0:T(8,128)S(1)} %constant_dynamic-update-slice_fusion), channel_id=1, source_target_pairs={{0,24},{1,17},{2,26},{3,19},{4,28},{5,21},{6,30},{7,23},{8,16},{9,... | collective-permute-start | bytes 55304 | tf_op jit(solution)/shard_map/ppermute | solution.py:63
  175.1 1.2 copy-start.4
  175.1 1.2 copy-start.5
  175.2 1.4 copy-start.6
  175.2 5.1 %collective-permute-start.19 = (f32[6,6,128]{2,1,0:T(8,128)S(1)}, f32[6,6,128]{2,1,0:T(8,128)S(1)}, u32[]{:S(2)}, u32[]{:S(2)}) collective-permute-start(f32[6,6,128]{2,1,0:T(8,128)S(1)} %add.109), channel_id=1, source_target_pairs={{0,96},{1,33},{2,98},{3,35},{4,100},{5,37},{6,102},{7,39},{8,104},... | collective-permute-start | bytes 55304 | tf_op jit(solution)/shard_map/ppermute | solution.py:63
  180.3 11.9 %collective-permute-start.20 = (bf16[8,192,128]{2,1,0:T(8,128)(2,1)}, bf16[8,192,128]{2,1,0:T(8,128)(2,1)S(1)}, u32[]{:S(2)}, u32[]{:S(2)}) collective-permute-start(bf16[8,192,128]{2,1,0:T(8,128)(2,1)} %get-tuple-element.145), channel_id=1, source_target_pairs={{0,96},{1,33},{2,98},{3,35},{4,100},{5,37},{6,102},{7,39},{8,104},... | collective-permute-start | bytes 1179656 | tf_op jit(solution)/shard_map/ppermute | solution.py:63
  181.7 10.5 %collective-permute-start.21 = (bf16[8,192,128]{2,1,0:T(8,128)(2,1)}, bf16[8,192,128]{2,1,0:T(8,128)(2,1)S(1)}, u32[]{:S(2)}, u32[]{:S(2)}) collective-permute-start(bf16[8,192,128]{2,1,0:T(8,128)(2,1)} %get-tuple-element.146), channel_id=1, source_target_pairs={{0,24},{1,17},{2,26},{3,19},{4,28},{5,21},{6,30},{7,23},{8,16},{9,... | collective-permute-start | bytes 1179656 | tf_op jit(solution)/shard_map/ppermute | solution.py:63
  182.7 9.5 %collective-permute-start.22 = (bf16[8,192,128]{2,1,0:T(8,128)(2,1)}, bf16[8,192,128]{2,1,0:T(8,128)(2,1)S(1)}, u32[]{:S(2)}, u32[]{:S(2)}) collective-permute-start(bf16[8,192,128]{2,1,0:T(8,128)(2,1)} %get-tuple-element.147), channel_id=1, source_target_pairs={{0,6},{1,3},{2,4},{3,1},{4,2},{5,7},{6,0},{7,5},{8,14},{9,11},{10,... | collective-permute-start | bytes 1179656 | tf_op jit(solution)/shard_map/ppermute | solution.py:63
  183.6 8.6 %collective-permute-start.23 = (f32[6,6,128]{2,1,0:T(8,128)S(1)}, f32[6,6,128]{2,1,0:T(8,128)S(1)}, u32[]{:S(2)}, u32[]{:S(2)}) collective-permute-start(f32[6,6,128]{2,1,0:T(8,128)S(1)} %add.110), channel_id=1, source_target_pairs={{0,6},{1,3},{2,4},{3,1},{4,2},{5,7},{6,0},{7,5},{8,14},{9,11},{10,... | collective-permute-start | bytes 55304 | tf_op jit(solution)/shard_map/ppermute | solution.py:63
  192.2 1.0 copy-start.11
  192.2 1.0 copy-start.12
  192.2 1.0 copy-start.13
  196.7 4.5 %copy-start.7 = (f32[64,16,128]{2,1,0:T(8,128)S(1)}, f32[64,16,128]{2,1,0:T(8,128)}, u32[]{:S(2)}) copy-start(f32[64,16,128]{2,1,0:T(8,128)} %all_to_all.16.totals_ref) | copy-start | bytes 1572868
  196.7 14.8 %all-to-all-start.2 = ((bf16[8,592,128]{2,1,0:T(8,128)(2,1)}), bf16[8,592,128]{2,1,0:T(8,128)(2,1)S(1)}, u32[]{:S(2)}, u32[]{:S(2)}) async-start(bf16[8,592,128]{2,1,0:T(8,128)(2,1)} %sum4.1), calls=%async_computation.2 | async-start | bytes 2424832 | tf_op jit(solution)/shard_map/all_to_all | solution.py:67
  200.4 11.4 %copy-start.10 = (bf16[128,576]{0,1:T(8,128)(2,1)S(1)}, bf16[128,576]{0,1:T(8,128)(2,1)}, u32[]{:S(2)}) copy-start(bf16[128,576]{0,1:T(8,128)(2,1)} %param.4) | copy-start | bytes 442372
  200.5 12.5 %copy-start.15 = (bf16[576]{0:T(1024)(128)(2,1)S(1)}, bf16[576]{0:T(1024)(128)(2,1)}, u32[]{:S(2)}) copy-start(bf16[576]{0:T(1024)(128)(2,1)} %param.5) | copy-start | bytes 3460
  200.5 13.1 %copy-start.1 = (s32[2048]{0:T(1024)S(1)}, s32[2048]{0:T(1024)}, u32[]{:S(2)}) copy-start(s32[2048]{0:T(1024)} %param.7) | copy-start | bytes 24580
  211.7 1.2 collective-permute-start.24
